TPU v7x, 128 devices: a whole 4x4x4 slice. The times are simulated.
128 devices in a mesh: gx: 16 (over y, x), gy: 8 (over z, core).
Axes of the slice: x: 4, y: 4, z: 4, core: 2. Of those that a mesh axis runs over, the one named last changes fastest.
Arguments:
- points_in: bfloat16 [1048576, 64], P(('gx', 'gy')), may hold values from -6 to 6
- tree_perm: int32 [1048576], P(('gx', 'gy')), may hold values from 0 to 8191, as said below
- basis: bfloat16 [4096, 256, 64], P(('gx', 'gy')), may hold values from -0.75 to 0.75
- transfer: bfloat16 [4096, 64, 64], P(('gx', 'gy')), may hold values from -0.75 to 0.75
- couple_fine: bfloat16 [65536, 64, 64], P(('gx', 'gy')), may hold values from -0.1875 to 0.1875
- couple_coarse: bfloat16 [32768, 64, 64], P(('gx', 'gy')), may hold values from -0.1875 to 0.1875
- list_fine: int32 [4096, 16], P(('gx', 'gy')), may hold values from 0 to 4095, as said below
- list_coarse: int32 [2048, 16], P(('gx', 'gy')), may hold values from 0 to 2047, as said below
- near_blocks: bfloat16 [16384, 256, 256], P(('gx', 'gy')), may hold values from -0.375 to 0.375
- near_target: int32 [16384], P(('gx', 'gy')), may hold values from 0 to 31
- near_source: int32 [16384], P(('gx', 'gy')), may hold values from 0 to 35
- task_count: int32 [128], P(('gx', 'gy')), may hold values from 32 to 128, as said below
Outputs:
- product: float32 [1048576, 64], P(('gx', 'gy'))
Inputs may be any that keep to these rules, and one draw needn't show every extreme that they name: `tree_perm`: each device's slice of 8192 entries is a permutation of 0 to 8191. `list_fine`: devices are numbered in tree order, gx index times the size of gy plus gy index, each holding 32 consecutive leaves. Every entry of a device names a leaf of one of the nine devices at most one step away along gx and along gy, wrapping round, itself included; each of those nine is named by some entry of every device. `list_coarse`: likewise for parents, each device holding 16 consecutive parents: every entry names a parent of one of the nine devices at most one step away along gx and along gy, wrapping round, itself included; each of those nine is named by some entry of every device. `task_count`: some device is full in every draw.
All inputs are finite; a program needn't handle non-finite values.
Results may differ from a plain program's by a relative error of at most 0.0048.
Values may be sent and summed in bfloat16 or wider, within the bound.
No kernel may reach another device: no remote copies, remote signals or barrier semaphores. Data moves between devices by JAX's collectives and lax.ppermute only.
A program may use at most 192 MiB of HBM per device.

v0:
```python
import jax
import jax.numpy as jnp
from jax import lax
from jax.sharding import PartitionSpec as P

W = 2


tile_tasks = 8


def extended(x, sides, width, wrap):
    for axis, dim in sides:
        count, length = (lax.axis_size(axis), x.shape[dim])
        up = [(i, (i + 1) % count) for i in range(count if wrap else count - 1)]
        down = [(j, i) for i, j in up]
        last = lax.slice_in_dim(x, length - width, length, axis=dim)
        initial = lax.slice_in_dim(x, 0, width, axis=dim)
        before = lax.ppermute(last, axis, up)
        after = lax.ppermute(initial, axis, down)
        x = jnp.concatenate([before, x, after], axis=dim)
    return x


def couple_level(skeleton, matrices, lists):
    clusters, entries_each = lists.shape
    rank_k, columns = (skeleton.shape[1], skeleton.shape[2])
    outer_size = lax.axis_size("gx")
    inner_size = lax.axis_size("gy")
    outer_here = lax.axis_index("gx")
    inner_here = lax.axis_index("gy")
    flat = lists.reshape(-1)
    owner = flat // clusters
    within = flat % clusters
    step_x = (owner // inner_size - outer_here + 1 + outer_size) % outer_size
    step_y = (owner % inner_size - inner_here + 1 + inner_size) % inner_size
    slots = (step_x * 3 + step_y) * clusters + within
    own = skeleton.reshape(1, 1, clusters, rank_k * columns)
    arrived = extended(own, (("gx", 0), ("gy", 1)), 1, True)
    picked = arrived.reshape(9 * clusters, rank_k * columns)[slots]
    picked = picked.reshape(clusters, entries_each, rank_k, columns)
    blocks = matrices.reshape(clusters, entries_each, rank_k, rank_k)
    return jnp.einsum("cjkl,cjlr->ckr", blocks, picked, preferred_element_type=jnp.float32)


def add_to_leaves(total, targets, products, live):
    leaf_ids = jnp.arange(total.shape[0], dtype=jnp.int32)
    selector = ((targets[:, None] == leaf_ids[None, :]) & live[:, None]).astype(jnp.float32)
    return total + jnp.einsum("tc,tpr->cpr", selector, products, precision=lax.Precision.HIGHEST)


def home_tasks(near_blocks, near_target, near_source, window, upper, leaf_clusters):
    points, columns = (window.shape[1], window.shape[2])
    steps = (upper + tile_tasks - 1) // tile_tasks

    def one_step(number, total):
        offset = number * tile_tasks
        blocks = lax.dynamic_slice_in_dim(near_blocks, offset, tile_tasks, 0)
        sources = lax.dynamic_slice_in_dim(near_source, offset, tile_tasks, 0)
        targets = lax.dynamic_slice_in_dim(near_target, offset, tile_tasks, 0)
        products = jnp.einsum(
            "tpq,tqr->tpr", blocks, window[sources], preferred_element_type=jnp.float32
        )
        live = offset + jnp.arange(tile_tasks, dtype=jnp.int32) < upper
        return add_to_leaves(total, targets, products, live)

    return lax.fori_loop(
        0, steps, one_step, jnp.zeros((leaf_clusters, points, columns), jnp.float32)
    )


def on_device(
    points_in,
    tree_perm,
    basis,
    transfer,
    couple_fine,
    couple_coarse,
    list_fine,
    list_coarse,
    near_blocks,
    near_target,
    near_source,
    task_count,
):
    leaf_clusters, points, rank_k = basis.shape
    columns = points_in.shape[1]
    ordered = points_in[tree_perm]
    leaf_points = ordered.reshape(leaf_clusters, points, columns)
    fine_skeleton = jnp.einsum(
        "cpk,cpr->ckr", basis, leaf_points, preferred_element_type=jnp.float32
    ).astype(jnp.bfloat16)
    parent_clusters = leaf_clusters // 2
    cluster_pairs = transfer.reshape(parent_clusters, 2, rank_k, rank_k)
    coarse_skeleton = jnp.einsum(
        "mzgh,mzgp->mhp",
        cluster_pairs,
        fine_skeleton.reshape(parent_clusters, 2, rank_k, columns),
        preferred_element_type=jnp.float32,
    ).astype(jnp.bfloat16)
    window = extended(ordered, ((("gx", "gy"), 0),), W * points, False)
    window = window.reshape(leaf_clusters + 2 * W, points, columns)
    local_fine = couple_level(fine_skeleton, couple_fine, list_fine)
    coarse_local_rows = couple_level(coarse_skeleton, couple_coarse, list_coarse).astype(
        jnp.bfloat16
    )
    forwarded_skeletons = jnp.einsum(
        "ednx,exw->ednw", cluster_pairs, coarse_local_rows, preferred_element_type=jnp.float32
    ).reshape(leaf_clusters, rank_k, columns)
    local_leaf = (local_fine + forwarded_skeletons).astype(jnp.bfloat16)
    far_field = jnp.einsum("cpk,ckr->cpr", basis, local_leaf, preferred_element_type=jnp.float32)
    mine = task_count[0]
    near_field = home_tasks(near_blocks, near_target, near_source, window, mine, leaf_clusters)
    tree_result = (far_field + near_field).reshape(leaf_clusters * points, columns)
    return jnp.zeros_like(tree_result).at[tree_perm].set(tree_result)


def solution(mesh):
    return jax.shard_map(
        on_device,
        mesh=mesh,
        in_specs=(
            P(("gx", "gy"), None),
            P(("gx", "gy")),
            P(("gx", "gy"), None, None),
            P(("gx", "gy"), None, None),
            P(("gx", "gy"), None, None),
            P(("gx", "gy"), None, None),
            P(("gx", "gy"), None),
            P(("gx", "gy"), None),
            P(("gx", "gy"), None, None),
            P(("gx", "gy")),
            P(("gx", "gy")),
            P(("gx", "gy")),
        ),
        out_specs=P(("gx", "gy"), None),
        check_vma=False,
    )
```

profile of v0, /device:TPU:1, one launch (start us, length us, event | category | flops | bytes accessed | tf_op | source)
XLA Modules:
  0.0 307.7 jit_solution(13569985429340038459)
XLA Ops:
  1.5 2.0 copy.16
  3.5 29.5 %gather_fusion.1 = bf16[8192,64]{1,0:T(8,128)(2,1)} fusion(bf16[8192,64]{1,0:T(8,128)(2,1)S(1)} %copy.16, s32[8192]{0:T(1024)S(1)} %get-tuple-element.67), kind=kCustom, calls=%fused_computation.1 | custom fusion | bytes 2129920 | tf_op jit(solution)/shard_map/gather | solution.py:88
  33.0 2.6 convolution_convert_fusion
  38.8 5.8 %collective-permute-start.5 = (bf16[1,1,16,4096]{3,2,1,0:T(8,128)(2,1)S(1)}, bf16[1,1,16,4096]{3,2,1,0:T(8,128)(2,1)}, u32[]{:S(2)}, u32[]{:S(2)}) collective-permute-start(bf16[1,1,16,4096]{3,2,1,0:T(8,128)(2,1)S(1)} %reshape.578), channel_id=1, source_target_pairs={{8,0},{16,8},{24,16},{32,24},{40,32},{48,40},{56,48},{64,56},{72,6... | collective-permute-start | bytes 393224 | tf_op jit(solution)/shard_map/ppermute | solution.py:20
  45.4 4.4 %collective-permute-start.8 = (bf16[512,64]{1,0:T(8,128)(2,1)}, bf16[512,64]{1,0:T(8,128)(2,1)}, u32[]{:S(2)}, u32[]{:S(2)}) collective-permute-start(bf16[512,64]{1,0:T(8,128)(2,1)} %get-tuple-element.65), channel_id=1, source_target_pairs={{0,1},{1,2},{2,3},{3,4},{4,5},{5,6},{6,7},{7,8},{8,9},{9,10},{10,1... | collective-permute-start | bytes 196616 | tf_op jit(solution)/shard_map/ppermute | solution.py:19
  49.7 1.9 collective-permute-start.9
  51.7 2.0 copy.18
  55.2 5.1 %collective-permute-start.1 = (bf16[1,1,32,4096]{3,2,1,0:T(8,128)(2,1)S(1)}, bf16[1,1,32,4096]{3,2,1,0:T(8,128)(2,1)}, u32[]{:S(2)}, u32[]{:S(2)}) collective-permute-start(bf16[1,1,32,4096]{3,2,1,0:T(8,128)(2,1)S(1)} %reshape.571), channel_id=1, source_target_pairs={{8,0},{16,8},{24,16},{32,24},{40,32},{48,40},{56,48},{64,56},{72,6... | collective-permute-start | bytes 786440 | tf_op jit(solution)/shard_map/ppermute | solution.py:20
  63.9 7.4 %copy.22 = bf16[256,64,64]{2,1,0:T(8,128)(2,1)} copy(bf16[256,64,64]{0,2,1:T(8,128)(2,1)} %param.19) | data formatting | bytes 4194304 | tf_op args[5]
  71.3 13.0 %copy.20 = bf16[512,64,64]{2,1,0:T(8,128)(2,1)} copy(bf16[512,64,64]{0,2,1:T(8,128)(2,1)} %param.18) | data formatting | bytes 8388608 | tf_op args[4]
  84.5 4.1 %pad_maximum_fusion.1 = bf16[9216,64]{1,0:T(8,128)(2,1)} fusion(bf16[512,64]{1,0:T(8,128)(2,1)} %collective-permute-done.9, bf16[8192,64]{1,0:T(8,128)(2,1)S(1)} %copy-done.3, bf16[512,64]{1,0:T(8,128)(2,1)} %collective-permute-done.8), kind=kLoop, calls=%fused_computation.19 | loop fusion | flops 3538944 | bytes 2359296 | tf_op jit(solution)/shard_map/concatenate | solution.py:21
  88.9 49.2 %while.10 = (s32[]{:T(128)}, f32[32,256,64]{1,0,2:T(8,128)S(1)}, s32[]{:T(128)}, s32[128]{0:T(128)S(1)}, s32[]{:T(128)}, /*index=5*/bf16[128,256,256]{2,1,0:T(8,...) while((s32[]{:T(128)}, f32[32,256,64]{1,0,2:T(8,128)S(1)}, ...), condition=%wide.region_1.2_spmd, body=%wide.region_0.1_spmd.sunk | while | flops 117966384 | bytes 7346635 | solution.py:67
  90.4 3.1 gather_fusion
  98.6 3.1 gather_fusion
  106.7 3.1 gather_fusion
  114.9 3.1 gather_fusion
  119.8 1.8 convolution_add_fusion.2
  123.1 3.1 gather_fusion
  128.0 1.8 convolution_add_fusion.2
  131.3 3.1 gather_fusion
  136.2 1.8 convolution_add_fusion.2
  140.1 84.7 %collective-permute-start.7 = (bf16[3,1,16,4096]{3,2,1,0:T(8,128)(2,1)S(1)}, bf16[3,1,16,4096]{3,2,1,0:T(8,128)(2,1)S(1)}, u32[]{:S(2)}, u32[]{:S(2)}) collective-permute-start(bf16[3,1,16,4096]{3,2,1,0:T(8,128)(2,1)S(1)} %constant_dynamic-update-slice_fusion.3), channel_id=1, source_target_pairs={{1,0},{2,1},{3,2},{4,3},{5,4},{6,5},{7,6},{0,7},{9,8},{10,9},{11,1... | collective-permute-start | bytes 1179656 | tf_op jit(solution)/shard_map/ppermute | solution.py:20
  230.7 3.3 %gather_fusion.3 = bf16[256,4096]{1,0:T(8,128)(2,1)} fusion(bf16[144,4096]{1,0:T(8,128)(2,1)S(1)} %bitcast.75, s32[1024]{0:T(1024)} %pad_clamp_fusion.1), kind=kCustom, calls=%fused_computation.3 | custom fusion | bytes 4195328 | tf_op jit(solution)/shard_map/gather | solution.py:40
  234.1 6.9 %reshape.581 = bf16[16,16,64,64]{3,2,1,0:T(8,128)(2,1)} reshape(bf16[256,4096]{1,0:T(8,128)(2,1)} %gather_fusion.3) | data formatting | bytes 4194304 | tf_op jit(solution)/shard_map/reshape | solution.py:41
  241.0 6.2 %fusion.17 = f32[16,64,2,64]{3,1,2,0:T(8,128)} fusion(bf16[16,2,64,64]{3,2,1,0:T(8,128)(2,1)S(1)} %bitcast.85, bf16[16,16,64,64]{3,2,1,0:T(8,128)(2,1)} %reshape.581, bf16[16,16,64,64]{3,2,1,0:T(8,128)(2,1)} %bitcast.78), kind=kOutput, calls=%fused_computation.34 | convolution fusion | flops 151060480 | bytes 4980736 | tf_op jit(solution)/shard_map/ednx,exw->ednw/dot_general | solution.py:107
  247.2 1.9 pad_maximum_fusion
  249.1 4.4 %gather_fusion.2 = bf16[512,4096]{1,0:T(8,128)(2,1)} fusion(bf16[288,4096]{1,0:T(8,128)(2,1)S(1)} %bitcast.74, s32[1024]{0:T(1024)S(1)} %pad_clamp_fusion.2), kind=kCustom, calls=%fused_computation.2 | custom fusion | bytes 8390656 | tf_op jit(solution)/shard_map/gather | solution.py:40
  253.4 12.7 %reshape.574 = bf16[32,16,64,64]{3,2,1,0:T(8,128)(2,1)} reshape(bf16[512,4096]{1,0:T(8,128)(2,1)} %gather_fusion.2) | data formatting | bytes 8388608 | tf_op jit(solution)/shard_map/reshape | solution.py:41
  266.1 11.0 %bitcast_add_fusion = f32[32,256,64]{1,2,0:T(8,128)} fusion(f32[32,256,64]{1,0,2:T(8,128)S(1)} %copy-done.2, bf16[32,256,64]{1,2,0:T(8,128)(2,1)S(1)} %copy-done, f32[32,64,64]{1,2,0:T(8,128)} %bitcast.82, bf16[32,16,64,64]{3,2,1,0:T(8,128)(2,1)} %reshape.574, bf16[32,16,64,64]{3,2,1,0:T(8,128)(2,1)} %bitcast.76), kind=kOutput, calls=%fused_computation.20 | convolution fusion | flops 336330752 | bytes 14155776 | tf_op jit(solution)/shard_map/cpk,ckr->cpr/dot_general | solution.py:111
  277.1 3.8 %copy.33 = f32[32,256,64]{2,1,0:T(8,128)} copy(f32[32,256,64]{1,2,0:T(8,128)} %bitcast_add_fusion) | data formatting | bytes 4194304 | tf_op jit(solution)/shard_map/reshape | solution.py:114
  280.9 23.0 %scatter_custom_fusion = f32[8192,64]{1,0:T(8,128)} fusion(s32[8192]{0:T(1024)} %get-tuple-element.68, f32[8192,64]{1,0:T(8,128)} %bitcast.83, f32[]{:T(128)} %constant.144.clone.1), kind=kCustom, calls=%fused_computation.21 | custom fusion | bytes 2097664 | tf_op jit(solution)/shard_map/scatter | solution.py:115
  303.9 3.8 %copy.26 = f32[8192,64]{0,1:T(8,128)} copy(f32[8192,64]{1,0:T(8,128)} %scatter_custom_fusion) | data formatting | bytes 4194304 | tf_op jit(solution)/shard_map/scatter | solution.py:115
  (99 shorter events, 43.1 us)
Async XLA Ops:
  0.0 33.0 %copy-start = (bf16[32,256,64]{1,2,0:T(8,128)(2,1)S(1)}, bf16[32,256,64]{1,2,0:T(8,128)(2,1)}, u32[]{:S(2)}) copy-start(bf16[32,256,64]{1,2,0:T(8,128)(2,1)} %param.16) | copy-start | bytes 3145732
  33.0 3.4 %copy-start.5 = (bf16[32,64,64]{2,1,0:T(8,128)(2,1)S(1)}, bf16[32,64,64]{2,1,0:T(8,128)(2,1)}, u32[]{:S(2)}) copy-start(bf16[32,64,64]{2,1,0:T(8,128)(2,1)} %param.17) | copy-start | bytes 786436
  33.0 11.6 %copy-start.3 = (bf16[8192,64]{1,0:T(8,128)(2,1)S(1)}, bf16[8192,64]{1,0:T(8,128)(2,1)}, u32[]{:S(2)}) copy-start(bf16[8192,64]{1,0:T(8,128)(2,1)} %gather_fusion.1) | copy-start | bytes 3145732
  35.6 0.8 copy-start.4
  35.6 25.4 %copy-start.7 = (s32[16,16]{1,0:T(8,128)S(1)}, s32[16,16]{1,0:T(8,128)}, u32[]{:S(2)}) copy-start(s32[16,16]{1,0:T(8,128)} %param.21) | copy-start | bytes 3076
  38.8 100.4 %collective-permute-start.5 = (bf16[1,1,16,4096]{3,2,1,0:T(8,128)(2,1)S(1)}, bf16[1,1,16,4096]{3,2,1,0:T(8,128)(2,1)}, u32[]{:S(2)}, u32[]{:S(2)}) collective-permute-start(bf16[1,1,16,4096]{3,2,1,0:T(8,128)(2,1)S(1)} %reshape.578), channel_id=1, source_target_pairs={{8,0},{16,8},{24,16},{32,24},{40,32},{48,40},{56,48},{64,56},{72,6... | collective-permute-start | bytes 393224 | tf_op jit(solution)/shard_map/ppermute | solution.py:20
  44.6 93.5 %collective-permute-start.4 = (bf16[1,1,16,4096]{3,2,1,0:T(8,128)(2,1)S(1)}, bf16[1,1,16,4096]{3,2,1,0:T(8,128)(2,1)}, u32[]{:S(2)}, u32[]{:S(2)}) collective-permute-start(bf16[1,1,16,4096]{3,2,1,0:T(8,128)(2,1)S(1)} %reshape.578), channel_id=1, source_target_pairs={{0,8},{8,16},{16,24},{24,32},{32,40},{40,48},{48,56},{56,64},{64,7... | collective-permute-start | bytes 393224 | tf_op jit(solution)/shard_map/ppermute | solution.py:19
  45.4 39.0 %collective-permute-start.8 = (bf16[512,64]{1,0:T(8,128)(2,1)}, bf16[512,64]{1,0:T(8,128)(2,1)}, u32[]{:S(2)}, u32[]{:S(2)}) collective-permute-start(bf16[512,64]{1,0:T(8,128)(2,1)} %get-tuple-element.65), channel_id=1, source_target_pairs={{0,1},{1,2},{2,3},{3,4},{4,5},{5,6},{6,7},{7,8},{8,9},{9,10},{10,1... | collective-permute-start | bytes 196616 | tf_op jit(solution)/shard_map/ppermute | solution.py:19
  49.7 34.7 %collective-permute-start.9 = (bf16[512,64]{1,0:T(8,128)(2,1)}, bf16[512,64]{1,0:T(8,128)(2,1)}, u32[]{:S(2)}, u32[]{:S(2)}) collective-permute-start(bf16[512,64]{1,0:T(8,128)(2,1)} %get-tuple-element.66), channel_id=1, source_target_pairs={{1,0},{2,1},{3,2},{4,3},{5,4},{6,5},{7,6},{8,7},{9,8},{10,9},{11,1... | collective-permute-start | bytes 196616 | tf_op jit(solution)/shard_map/ppermute | solution.py:20
  55.2 172.0 %collective-permute-start.1 = (bf16[1,1,32,4096]{3,2,1,0:T(8,128)(2,1)S(1)}, bf16[1,1,32,4096]{3,2,1,0:T(8,128)(2,1)}, u32[]{:S(2)}, u32[]{:S(2)}) collective-permute-start(bf16[1,1,32,4096]{3,2,1,0:T(8,128)(2,1)S(1)} %reshape.571), channel_id=1, source_target_pairs={{8,0},{16,8},{24,16},{32,24},{40,32},{48,40},{56,48},{64,56},{72,6... | collective-permute-start | bytes 786440 | tf_op jit(solution)/shard_map/ppermute | solution.py:20
  84.3 4.5 %copy-start.8 = (s32[128]{0:T(128)S(1)}, s32[128]{0:T(128)}, u32[]{:S(2)}) copy-start(s32[128]{0:T(128)} %param.23) | copy-start | bytes 1540
  84.4 140.4 %collective-permute-start = (bf16[1,1,32,4096]{3,2,1,0:T(8,128)(2,1)S(1)}, bf16[1,1,32,4096]{3,2,1,0:T(8,128)(2,1)}, u32[]{:S(2)}, u32[]{:S(2)}) collective-permute-start(bf16[1,1,32,4096]{3,2,1,0:T(8,128)(2,1)S(1)} %reshape.571), channel_id=1, source_target_pairs={{0,8},{8,16},{16,24},{24,32},{32,40},{40,48},{48,56},{56,64},{64,7... | collective-permute-start | bytes 786440 | tf_op jit(solution)/shard_map/ppermute | solution.py:19
  95.2 1.8 copy-start.9
  103.4 1.8 copy-start.9
  111.6 1.8 copy-start.9
  119.8 1.8 copy-start.9
  128.0 1.8 copy-start.9
  136.2 1.8 copy-start.9
  138.1 92.5 %copy-start.1 = (f32[32,256,64]{1,0,2:T(8,128)}, f32[32,256,64]{1,0,2:T(8,128)S(1)}, u32[]{:S(2)}) copy-start(f32[32,256,64]{1,0,2:T(8,128)S(1)} %get-tuple-element.164) | copy-start | bytes 6291460
  140.1 90.5 %collective-permute-start.7 = (bf16[3,1,16,4096]{3,2,1,0:T(8,128)(2,1)S(1)}, bf16[3,1,16,4096]{3,2,1,0:T(8,128)(2,1)S(1)}, u32[]{:S(2)}, u32[]{:S(2)}) collective-permute-start(bf16[3,1,16,4096]{3,2,1,0:T(8,128)(2,1)S(1)} %constant_dynamic-update-slice_fusion.3), channel_id=1, source_target_pairs={{1,0},{2,1},{3,2},{4,3},{5,4},{6,5},{7,6},{0,7},{9,8},{10,9},{11,1... | collective-permute-start | bytes 1179656 | tf_op jit(solution)/shard_map/ppermute | solution.py:20
  224.8 5.8 %collective-permute-start.6 = (bf16[3,1,16,4096]{3,2,1,0:T(8,128)(2,1)S(1)}, bf16[3,1,16,4096]{3,2,1,0:T(8,128)(2,1)S(1)}, u32[]{:S(2)}, u32[]{:S(2)}) collective-permute-start(bf16[3,1,16,4096]{3,2,1,0:T(8,128)(2,1)S(1)} %constant_dynamic-update-slice_fusion.3), channel_id=1, source_target_pairs={{0,1},{1,2},{2,3},{3,4},{4,5},{5,6},{6,7},{7,0},{8,9},{9,10},{10,1... | collective-permute-start | bytes 1179656 | tf_op jit(solution)/shard_map/ppermute | solution.py:19
  228.8 18.4 %collective-permute-start.3 = (bf16[3,1,32,4096]{3,2,1,0:T(8,128)(2,1)}, bf16[3,1,32,4096]{3,2,1,0:T(8,128)(2,1)}, u32[]{:S(2)}, u32[]{:S(2)}) collective-permute-start(bf16[3,1,32,4096]{3,2,1,0:T(8,128)(2,1)} %constant_dynamic-update-slice_fusion), channel_id=1, source_target_pairs={{1,0},{2,1},{3,2},{4,3},{5,4},{6,5},{7,6},{0,7},{9,8},{10,9},{11,1... | collective-permute-start | bytes 2359304 | tf_op jit(solution)/shard_map/ppermute | solution.py:20
  229.3 17.9 %collective-permute-start.2 = (bf16[3,1,32,4096]{3,2,1,0:T(8,128)(2,1)}, bf16[3,1,32,4096]{3,2,1,0:T(8,128)(2,1)}, u32[]{:S(2)}, u32[]{:S(2)}) collective-permute-start(bf16[3,1,32,4096]{3,2,1,0:T(8,128)(2,1)} %constant_dynamic-update-slice_fusion), channel_id=1, source_target_pairs={{0,1},{1,2},{2,3},{3,4},{4,5},{5,6},{6,7},{7,0},{8,9},{9,10},{10,1... | collective-permute-start | bytes 2359304 | tf_op jit(solution)/shard_map/ppermute | solution.py:19
  234.1 6.9 %copy-start.6 = (bf16[32,64,64]{2,1,0:T(8,128)(2,1)S(1)}, bf16[32,64,64]{2,1,0:T(8,128)(2,1)}, u32[]{:S(2)}) copy-start(bf16[32,64,64]{2,1,0:T(8,128)(2,1)} %param.17) | copy-start | bytes 786436
  253.4 12.7 %copy-start.2 = (f32[32,256,64]{1,0,2:T(8,128)S(1)}, f32[32,256,64]{1,0,2:T(8,128)}, u32[]{:S(2)}) copy-start(f32[32,256,64]{1,0,2:T(8,128)} %copy-done.1) | copy-start | bytes 6291460
where the time goes:
time: 311 us; the launch traced here: 308 us
  local copies, waits for them, and re-layouts  144 us (46%)
  starting transfers between devices  104 us (33%)
  matrix products  41.7 us (13%)
  other arithmetic  17.3 us (6%)
    ppermute x5, starting transfers between devices, extended(): after = lax.ppermute(initial, axis, down)  98 us
    gather x1, local copies, waits for them, and re-layouts, on_device(): ordered = points_in[tree_perm]  29.5 us
    unnamed x26, local copies, waits for them, and re-layouts  27.5 us
    scatter x2, local copies, waits for them, and re-layouts, on_device(): return jnp.zeros_like(tree_result).at[tree_perm].set(tree_result)  26.8 us
    reshape x2, local copies, waits for them, and re-layouts, couple_level(): picked = picked.reshape(clusters, entries_each, rank_k, columns)  19.6 us
    gather x6, local copies, waits for them, and re-layouts, one_step(): window[sources]  18.4 us
    dot_general x1, matrix products, on_device(): jnp.einsum('cpk,ckr->cpr', basis, local_leaf, preferred_element_type=jnp....  11 us
    dot_general x6, matrix products, add_to_leaves(): jnp.einsum('tc,tpr->cpr', selector, products, precision=lax.Precision.HIG...  10.8 us
  transfers between devices with their start and end apart: 10, of which 0 were waited for; matrix products, arithmetic and copies ran while one was open for 34% of the time, Pallas kernels for 0%

commit v1 on v0

v1 whole, which is shorter than its diff:
```python
import jax
import jax.numpy as jnp
from jax import lax
from jax.experimental import pallas as pl
from jax.experimental.pallas import tpu as pltpu
from jax.sharding import PartitionSpec as P

LEAVES = 32
PARENTS = LEAVES // 2
POINTS = 256
RANK = 64
COLS = 64
ENTRIES = 16
HALO = 2
TASKS = 128
ROWS = LEAVES * POINTS
PAIRS = LEAVES // 2 + PARENTS // 2
TASK_STEP = 8
LEAF_STEP = 4

SMEM = pltpu.SMEM
VMEM = pltpu.VMEM
F32 = jnp.float32
BF16 = jnp.bfloat16


def params(mib):
    return pltpu.CompilerParams(vmem_limit_bytes=mib << 20)


def low_half(rows):
    return lax.broadcasted_iota(jnp.int32, (rows, 128), 1) < 64


def swap_halves(x):
    return jnp.concatenate([x[:, 64:], x[:, :64]], axis=1)


def order_kernel(perm, points, basis, transfer, ordered, skeleton, edges, table, even, odd, fine):
    for c in range(ROWS // 128):
        block = points[:, c * 128 : (c + 1) * 128].astype(F32)
        table[c * 128 : (c + 1) * 128, :] = jnp.concatenate([block, block], axis=0).T

    def gather(leaf, into):
        rows = perm.at[pl.ds(leaf * POINTS, POINTS)]
        for i in range(POINTS):
            into[i : i + 1, :] = table[pl.ds(rows[i], 1), :]

    def finish(leaf, source):
        block = source[...].astype(BF16)
        ordered[leaf] = block
        fine[leaf] = jnp.dot(basis[leaf], block, preferred_element_type=F32).astype(BF16)

    gather(0, even)

    def two_leaves(step, _):
        gather(2 * step + 1, odd)
        finish(2 * step, even)
        gather(jnp.minimum(2 * step + 2, LEAVES - 1), even)
        finish(2 * step + 1, odd)
        return 0

    lax.fori_loop(0, LEAVES // 2, two_leaves, 0)

    low = low_half(RANK)
    low_points = low_half(POINTS)
    for p in range(PARENTS):
        skeleton[p] = jnp.where(low, fine[2 * p], fine[2 * p + 1])
    for q in range(PARENTS // 2):
        coarse = []
        for p in (2 * q, 2 * q + 1):
            pair = transfer[2 * p : 2 * p + 2].reshape(2 * RANK, RANK)
            stacked = fine[2 * p : 2 * p + 2].reshape(2 * RANK, 128)
            coarse.append(
                lax.dot_general(
                    pair, stacked, (((0,), (0,)), ((), ())), preferred_element_type=F32
                ).astype(BF16)
            )
        skeleton[PARENTS + q] = jnp.where(low, coarse[0], coarse[1])
    edges[0] = jnp.where(low_points, ordered[0], ordered[1])
    edges[1] = jnp.where(low_points, ordered[LEAVES - 2], ordered[LEAVES - 1])


def order_points(points, perm, basis, transfer):
    return pl.pallas_call(
        order_kernel,
        out_shape=(
            jax.ShapeDtypeStruct((LEAVES, POINTS, 128), BF16),
            jax.ShapeDtypeStruct((PAIRS, RANK, 128), BF16),
            jax.ShapeDtypeStruct((2, POINTS, 128), BF16),
        ),
        in_specs=[
            pl.BlockSpec(memory_space=SMEM),
            pl.BlockSpec(memory_space=VMEM),
            pl.BlockSpec(memory_space=VMEM),
            pl.BlockSpec(memory_space=VMEM),
        ],
        out_specs=(pl.BlockSpec(memory_space=VMEM),) * 3,
        scratch_shapes=[
            pltpu.VMEM((ROWS, 128), F32),
            pltpu.VMEM((POINTS, 128), F32),
            pltpu.VMEM((POINTS, 128), F32),
            pltpu.VMEM((LEAVES, RANK, 128), BF16),
        ],
        compiler_params=params(24),
        name="order_points",
    )(perm, points, basis, transfer)


def turn_kernel(blocks, turned, table):
    half = RANK // 2
    for k in range(half):
        block = jnp.concatenate([blocks[k], blocks[k + half]], axis=0).astype(F32)
        table[pl.ds(k, 128, stride=half), :] = block.T
    low = low_half(half)
    for t in range(128 // ENTRIES):
        for j in range(0, ENTRIES, 2):
            first = table[pl.ds((t * ENTRIES + j) * half, half), :]
            second = table[pl.ds((t * ENTRIES + j + 1) * half, half), :]
            turned[t, :half, j * 64 : (j + 2) * 64] = jnp.where(
                low, first, pltpu.roll(second, 64, 1)
            ).astype(BF16)
            turned[t, half:, j * 64 : (j + 2) * 64] = jnp.where(
                low, pltpu.roll(first, 64, 1), second
            ).astype(BF16)


def turn_blocks(blocks):
    entries = blocks.shape[2]
    targets = 128 // ENTRIES
    return pl.pallas_call(
        turn_kernel,
        grid=(entries // 128,),
        out_shape=jax.ShapeDtypeStruct((entries // ENTRIES, RANK, ENTRIES * RANK), BF16),
        in_specs=[pl.BlockSpec((RANK, RANK, 128), lambda i: (0, 0, i))],
        out_specs=pl.BlockSpec((targets, RANK, ENTRIES * RANK), lambda i: (i, 0, 0)),
        scratch_shapes=[pltpu.VMEM((128 * RANK // 2, 128), F32)],
        compiler_params=params(24),
        cost_estimate=pl.CostEstimate(
            flops=0, bytes_accessed=12 * blocks.size, transcendentals=0
        ),
        name="turn_blocks",
    )(blocks)


def near_kernel(targets, sources, count, before, after, ordered, blocks, total, window, sem):
    step = pl.program_id(0)

    @pl.when(step == 0)
    def _():
        copy = pltpu.make_async_copy(ordered, window.at[pl.ds(HALO, LEAVES)], sem)
        copy.start()
        window[0] = before[...]
        window[1] = swap_halves(before[...])
        window[LEAVES + 2] = after[...]
        window[LEAVES + 3] = swap_halves(after[...])
        total[...] = jnp.zeros_like(total)
        copy.wait()

    for i in range(TASK_STEP):
        task = step * TASK_STEP + i
        target = jnp.where(task < count[0], targets[task], LEAVES)
        total[target] += jnp.dot(blocks[i], window[sources[task]], preferred_element_type=F32)


def near_field(targets, sources, count, before, after, ordered, blocks):
    return pl.pallas_call(
        near_kernel,
        grid=(TASKS // TASK_STEP,),
        out_shape=jax.ShapeDtypeStruct((LEAVES + 1, POINTS, 128), F32),
        in_specs=[
            pl.BlockSpec(memory_space=SMEM),
            pl.BlockSpec(memory_space=SMEM),
            pl.BlockSpec(memory_space=SMEM),
            pl.BlockSpec(memory_space=VMEM),
            pl.BlockSpec(memory_space=VMEM),
            pl.BlockSpec(memory_space=pl.ANY),
            pl.BlockSpec((TASK_STEP, POINTS, POINTS), lambda i: (i, 0, 0)),
        ],
        out_specs=pl.BlockSpec((LEAVES + 1, POINTS, 128), lambda i: (0, 0, 0)),
        scratch_shapes=[
            pltpu.VMEM((LEAVES + 2 * HALO, POINTS, 128), BF16),
            pltpu.SemaphoreType.DMA,
        ],
        compiler_params=params(24),
        cost_estimate=pl.CostEstimate(
            flops=2 * TASKS * POINTS * POINTS * 128,
            bytes_accessed=2 * TASKS * POINTS * POINTS,
            transcendentals=0,
        ),
        name="near_field",
    )(targets, sources, count, before, after, ordered, blocks)


def result_kernel(*refs):
    perm, slots = refs[:2]
    skeletons = refs[2:11]
    fine, coarse, transfer, basis, near, out, spread, rows, table = refs[11:]
    step = pl.program_id(0)

    @pl.when(step == 0)
    def _():
        low = low_half(RANK)
        for a in range(9):

            def unpack(p, _):
                pair = skeletons[a][p]
                swapped = swap_halves(pair)
                spread[a * 2 * PAIRS + 2 * p] = jnp.where(low, pair, swapped)
                spread[a * 2 * PAIRS + 2 * p + 1] = jnp.where(low, swapped, pair)
                return 0

            lax.fori_loop(0, PAIRS, unpack, 0, unroll=4)

    def coupled(matrix, first):
        picked = [spread[slots[first + j]] for j in range(ENTRIES)]
        return jnp.dot(matrix, jnp.concatenate(picked, axis=0), preferred_element_type=F32)

    for p in range(LEAF_STEP // 2):
        parent = step * (LEAF_STEP // 2) + p
        from_parent = coupled(coarse[p], (LEAVES + parent) * ENTRIES).astype(BF16)
        for z in range(2):
            c = 2 * p + z
            leaf = step * LEAF_STEP + c
            local = coupled(fine[c], leaf * ENTRIES)
            local += jnp.dot(transfer[c], from_parent, preferred_element_type=F32)
            far = lax.dot_general(
                basis[c],
                local.astype(BF16),
                (((0,), (0,)), ((), ())),
                preferred_element_type=F32,
            )
            rows[c] = far + near[c]
    for c in range(LEAF_STEP):
        places = perm.at[pl.ds((step * LEAF_STEP + c) * POINTS, POINTS)]
        for i in range(POINTS):
            table[pl.ds(places[i], 1), :] = rows[c, i : i + 1, :]

    @pl.when(step == pl.num_programs(0) - 1)
    def _():
        for c in range(ROWS // 128):
            out[:, c * 128 : (c + 1) * 128] = table[c * 128 : (c + 1) * 128, :COLS].T


def result(perm, slots, skeletons, fine, coarse, transfer, basis, near):
    whole = pl.BlockSpec((PAIRS, RANK, 128), lambda i: (0, 0, 0))
    parents = LEAF_STEP // 2
    return pl.pallas_call(
        result_kernel,
        grid=(LEAVES // LEAF_STEP,),
        out_shape=jax.ShapeDtypeStruct((COLS, ROWS), F32),
        in_specs=[
            pl.BlockSpec(memory_space=SMEM),
            pl.BlockSpec(memory_space=SMEM),
            *[whole] * 9,
            pl.BlockSpec((LEAF_STEP, RANK, ENTRIES * RANK), lambda i: (i, 0, 0)),
            pl.BlockSpec((parents, RANK, ENTRIES * RANK), lambda i: (i, 0, 0)),
            pl.BlockSpec((LEAF_STEP, RANK, RANK), lambda i: (i, 0, 0)),
            pl.BlockSpec((LEAF_STEP, RANK, POINTS), lambda i: (i, 0, 0)),
            pl.BlockSpec((LEAF_STEP, POINTS, 128), lambda i: (i, 0, 0)),
        ],
        out_specs=pl.BlockSpec((COLS, ROWS), lambda i: (0, 0)),
        scratch_shapes=[
            pltpu.VMEM((9 * 2 * PAIRS, RANK, 128), BF16),
            pltpu.VMEM((LEAF_STEP, POINTS, 128), F32),
            pltpu.VMEM((ROWS, 128), F32),
        ],
        compiler_params=params(40),
        name="result",
    )(perm, slots, *skeletons, fine, coarse, transfer, basis, near)


def swaps(count, odd):
    pairs = [((i + odd) % count, (i + odd + 1) % count) for i in range(0, count, 2)]
    return [(a, b) for a, b in pairs] + [(b, a) for a, b in pairs]


def swap(x, axis, odd):
    return lax.ppermute(x, axis, swaps(lax.axis_size(axis), odd))


def places(lists, clusters, first):
    outer, inner = lax.axis_size("gx"), lax.axis_size("gy")
    gx, gy = lax.axis_index("gx"), lax.axis_index("gy")
    owner = lists // clusters
    step_x = (owner // inner - gx + outer) % outer
    step_y = (owner % inner - gy + inner) % inner
    array_x = jnp.where(step_x == 0, 0, jnp.where((step_x == 1) == (gx % 2 == 0), 1, 2))
    array_y = jnp.where(step_y == 0, 0, jnp.where((step_y == 1) == (gy % 2 == 0), 1, 2))
    return (array_x * 3 + array_y) * (2 * PAIRS) + first + lists % clusters


def on_device(
    points_in,
    tree_perm,
    basis,
    transfer,
    couple_fine,
    couple_coarse,
    list_fine,
    list_coarse,
    near_blocks,
    near_target,
    near_source,
    task_count,
):
    basis_rows = basis.transpose(0, 2, 1)
    slots = jnp.concatenate(
        [
            places(list_fine, LEAVES, 0).reshape(-1),
            places(list_coarse, PARENTS, LEAVES).reshape(-1),
        ]
    )
    ordered, own, edges = order_points(points_in.T, tree_perm, basis_rows, transfer)
    x_even = swap(own, "gx", 0)
    x_odd = swap(own, "gx", 1)
    y_even = swap(own, "gy", 0)
    y_odd = swap(own, "gy", 1)
    both = ("gx", "gy")
    last = lax.axis_size(both) - 1
    before = lax.ppermute(edges[1], both, [(i, i + 1) for i in range(last)])
    after = lax.ppermute(edges[0], both, [(i + 1, i) for i in range(last)])
    fine = turn_blocks(couple_fine.transpose(1, 2, 0))
    coarse = turn_blocks(couple_coarse.transpose(1, 2, 0))
    near = near_field(near_target, near_source, task_count, before, after, ordered, near_blocks)
    skeletons = [own, y_even, y_odd]
    for x in (x_even, x_odd):
        skeletons += [x, swap(x, "gy", 0), swap(x, "gy", 1)]
    out = result(tree_perm, slots, skeletons, fine, coarse, transfer, basis_rows, near)
    return out.T


def solution(mesh):
    flat = P(("gx", "gy"))
    return jax.shard_map(
        on_device,
        mesh=mesh,
        in_specs=(flat,) * 12,
        out_specs=flat,
        check_vma=False,
    )
```

time: 311 us -> 90.3 us (0.29)
  local copies, waits for them, and re-layouts: 144 us -> 14 us
  starting transfers between devices: 104 us -> 19.8 us
  Pallas kernels: 0 us -> 53.5 us
  matrix products: 41.7 us -> 0 us
  other arithmetic: 17.3 us -> 1.48 us
    ppermute x10, starting transfers between devices: 104 us -> 19.8 us  [the longest x8 14.2 us: swap(): return lax.ppermute(x, axis, swaps(lax.axis_size(axis), odd))]
    gather x9 -> x0, local copies, waits for them, and re-layouts: 55.6 us -> none  [the longest x1 29.5 us: on_device(): ordered = points_in[tree_perm]]
    pallas_call x0 -> x5, Pallas kernels: none -> 53.5 us  [the longest x1 23.4 us: result(): pl.pallas_call(result_kernel, grid=(LEAVES // LEAF_STEP,), out_shape=jax....]
    dot_general x16 -> x0, matrix products: 41.7 us -> none  [the longest x1 11 us: on_device(): jnp.einsum('cpk,ckr->cpr', basis, local_leaf, preferred_element_type=jnp....]
    scatter x2 -> x0, local copies, waits for them, and re-layouts: 26.8 us -> none  [on_device(): return jnp.zeros_like(tree_result).at[tree_perm].set(tree_result)]
    reshape x7 -> x2, local copies, waits for them, and re-layouts: 26.9 us -> 0.16 us  [the longest x1 0.08 us: on_device(): places(list_fine, LEAVES, 0).reshape(-1)]
    unnamed x26, local copies, waits for them, and re-layouts: 27.5 us -> 13.8 us
    concatenate x3 -> x1, other arithmetic: 6.14 us -> 0.01 us  [on_device(): jnp.concatenate([places(list_fine, LEAVES, 0).reshape(-1), places(list_co...]
  transfers between devices with their start and end apart: 10 -> 10, of which waited for: 0 -> 1; matrix products, arithmetic and copies ran while one was open for 34% -> 2% of each run, Pallas kernels for 0% -> 22%
where the time goes in v1:
time: 90.3 us; the launch traced here: 89.8 us
  Pallas kernels  53.5 us (59%)
  starting transfers between devices  19.8 us (22%)
  local copies, waits for them, and re-layouts  14 us (16%)
  other arithmetic  1.48 us (2%)
    pallas_call x1, Pallas kernels, result(): pl.pallas_call(result_kernel, grid=(LEAVES // LEAF_STEP,), out_shape=jax....  23.4 us
    ppermute x8, starting transfers between devices, swap(): return lax.ppermute(x, axis, swaps(lax.axis_size(axis), odd))  14.2 us
    unnamed x26, local copies, waits for them, and re-layouts  13.8 us
    pallas_call x2, Pallas kernels, turn_blocks(): pl.pallas_call(turn_kernel, grid=(entries // 128,), out_shape=jax.ShapeDt...  11 us
    pallas_call x1, Pallas kernels, order_points(): pl.pallas_call(order_kernel, out_shape=(jax.ShapeDtypeStruct((LEAVES, POI...  10.6 us
    pallas_call x1, Pallas kernels, near_field(): pl.pallas_call(near_kernel, grid=(TASKS // TASK_STEP,), out_shape=jax.Sha...  8.49 us
    ppermute x1, starting transfers between devices, on_device(): after = lax.ppermute(edges[0], both, [(i + 1, i) for i in range(last)])  3.57 us
    ppermute x1, starting transfers between devices, on_device(): before = lax.ppermute(edges[1], both, [(i, i + 1) for i in range(last)])  1.99 us
  transfers between devices with their start and end apart: 10, of which 1 were waited for; matrix products, arithmetic and copies ran while one was open for 2% of the time, Pallas kernels for 22%

profile of v1, /device:TPU:1, one launch (start us, length us, event | category | flops | bytes accessed | tf_op | source)
XLA Modules:
  0.0 89.8 jit_solution(5583470514961517303)
XLA Ops:
  0.0 1.2 %copy-done.3 = bf16[32,256,64]{1,2,0:T(8,128)(2,1)S(1)} copy-done((bf16[32,256,64]{1,2,0:T(8,128)(2,1)S(1)}, bf16[32,256,64]{1,2,0:T(8,128)(2,1)}, u32[]{:S(2)}) %copy-start.3) | copy-done | bytes 1048600
  1.2 1.0 %copy-done.6 = bf16[32,64,64]{2,1,0:T(8,128)(2,1)S(1)} copy-done((bf16[32,64,64]{2,1,0:T(8,128)(2,1)S(1)}, bf16[32,64,64]{2,1,0:T(8,128)(2,1)}, u32[]{:S(2)}) %copy-start.6) | copy-done | bytes 262168
  2.3 1.2 %copy-done.8 = bf16[8192,64]{0,1:T(8,128)(2,1)S(1)} copy-done((bf16[8192,64]{0,1:T(8,128)(2,1)S(1)}, bf16[8192,64]{0,1:T(8,128)(2,1)}, u32[]{:S(2)}) %copy-start.8) | copy-done | bytes 1048600
  3.5 0.8 copy-done.9
  4.3 10.6 %order_points.1 = (bf16[32,256,128]{2,1,0:T(8,128)(2,1)S(1)}, bf16[24,64,128]{2,1,0:T(8,128)(2,1)S(1)}, bf16[2,256,128]{2,1,0:T(8,128)(2,1)S(1)}) custom-call(s32[8192]{0:T(1024)S(1)} %copy-done.9, bf16[64,8192]{1,0:T(8,128)(2,1)S(1)} %bitcast.13, bf16[32,64,256]{2,1,0:T(8,128)(2,1)S(1)} %bitcast.10, bf16[32,64,64]{2,1,0:T(8,128)(2,1)S(1)} %copy-done.6), custom_call_target="tpu_custom_call" | custom-call | tf_op jit(solution)/shard_map/order_points/pallas_call | solution.py:85
  14.8 5.8 %collective-permute-start.5 = (bf16[24,64,128]{2,1,0:T(8,128)(2,1)S(1)}, bf16[24,64,128]{2,1,0:T(8,128)(2,1)S(1)}, u32[]{:S(2)}, u32[]{:S(2)}) collective-permute-start(bf16[24,64,128]{2,1,0:T(8,128)(2,1)S(1)} %get-tuple-element.8.refs_2_), channel_id=1, source_target_pairs={{8,16},{24,32},{40,48},{56,64},{72,80},{88,96},{104,112},{120,0},{... | collective-permute-start | bytes 1179656 | tf_op jit(solution)/shard_map/ppermute | solution.py:279
  20.7 0.0 collective-permute-start.2
  20.7 2.5 %collective-permute-start.1 = (bf16[24,64,128]{2,1,0:T(8,128)(2,1)S(1)}, bf16[24,64,128]{2,1,0:T(8,128)(2,1)}, u32[]{:S(2)}, u32[]{:S(2)}) collective-permute-start(bf16[24,64,128]{2,1,0:T(8,128)(2,1)S(1)} %get-tuple-element.8.refs_2_), channel_id=1, source_target_pairs={{1,2},{3,4},{5,6},{7,0},{2,1},{4,3},{6,5},{0,7},{9,10},{11,12},{13... | collective-permute-start | bytes 1179656 | tf_op jit(solution)/shard_map/ppermute | solution.py:279
  23.2 3.6 %collective-permute-start.9 = (bf16[256,128]{1,0:T(8,128)(2,1)S(1)}, bf16[256,128]{1,0:T(8,128)(2,1)S(1)}, u32[]{:S(2)}, u32[]{:S(2)}) collective-permute-start(bf16[256,128]{1,0:T(8,128)(2,1)S(1)} %get-tuple-element.11), channel_id=1, source_target_pairs={{1,0},{2,1},{3,2},{4,3},{5,4},{6,5},{7,6},{8,7},{9,8},{10,9},{11,1... | collective-permute-start | bytes 196616 | tf_op jit(solution)/shard_map/ppermute | solution.py:322
  26.7 2.0 %collective-permute-start.8 = (bf16[256,128]{1,0:T(8,128)(2,1)S(1)}, bf16[256,128]{1,0:T(8,128)(2,1)S(1)}, u32[]{:S(2)}, u32[]{:S(2)}) collective-permute-start(bf16[256,128]{1,0:T(8,128)(2,1)S(1)} %get-tuple-element.12), channel_id=1, source_target_pairs={{0,1},{1,2},{2,3},{3,4},{4,5},{5,6},{6,7},{7,8},{8,9},{9,10},{10,1... | collective-permute-start | bytes 196616 | tf_op jit(solution)/shard_map/ppermute | solution.py:321
  28.8 0.7 fusion.6
  29.5 0.2 collective-permute-done.9.after
  29.7 0.3 collective-permute-start
  30.0 0.0 collective-permute-done.5.refs_8_
  30.0 2.2 %collective-permute-start.7 = (bf16[24,64,128]{2,1,0:T(8,128)(2,1)S(1)}, bf16[24,64,128]{2,1,0:T(8,128)(2,1)}, u32[]{:S(2)}, u32[]{:S(2)}) collective-permute-start(bf16[24,64,128]{2,1,0:T(8,128)(2,1)S(1)} %collective-permute-done.5.refs_8_), channel_id=1, source_target_pairs={{1,2},{3,4},{5,6},{7,0},{2,1},{4,3},{6,5},{0,7},{9,10},{11,12},{13... | collective-permute-start | bytes 1179656 | tf_op jit(solution)/shard_map/ppermute | solution.py:279
  32.3 2.7 %collective-permute-start.6 = (bf16[24,64,128]{2,1,0:T(8,128)(2,1)S(1)}, bf16[24,64,128]{2,1,0:T(8,128)(2,1)}, u32[]{:S(2)}, u32[]{:S(2)}) collective-permute-start(bf16[24,64,128]{2,1,0:T(8,128)(2,1)S(1)} %collective-permute-done.5.refs_8_), channel_id=1, source_target_pairs={{0,1},{2,3},{4,5},{6,7},{1,0},{3,2},{5,4},{7,6},{8,9},{10,11},{12,... | collective-permute-start | bytes 1179656 | tf_op jit(solution)/shard_map/ppermute | solution.py:279
  35.0 0.0 collective-permute-done.2.refs_5_
  35.0 0.6 collective-permute-start.3
  35.6 0.7 fusion.13
  37.0 0.1 reshape.7
  37.1 0.1 copy.13
  37.2 0.1 reshape.6
  37.2 1.7 %copy-done.5 = bf16[256,64,64]{0,2,1:T(8,128)(2,1)S(1)} copy-done((bf16[256,64,64]{0,2,1:T(8,128)(2,1)S(1)}, bf16[256,64,64]{0,2,1:T(8,128)(2,1)}, u32[]{:S(2)}) %copy-start.5) | copy-done | bytes 2097176
  39.0 3.7 %turn_blocks.3.refs_12_ = bf16[16,64,1024]{2,1,0:T(8,128)(2,1)S(1)} custom-call(bf16[64,64,256]{2,1,0:T(8,128)(2,1)S(1)} %bitcast.12), custom_call_target="tpu_custom_call" | custom-call | bytes 12582912 | tf_op jit(solution)/shard_map/turn_blocks/pallas_call | solution.py:131
  42.7 0.0 copy-start.11
  42.7 0.0 copy-start.12
  42.7 7.3 %turn_blocks.2.refs_11_ = bf16[32,64,1024]{2,1,0:T(8,128)(2,1)S(1)} custom-call(bf16[64,64,512]{2,1,0:T(8,128)(2,1)S(1)} %bitcast.9), custom_call_target="tpu_custom_call" | custom-call | bytes 25165824 | tf_op jit(solution)/shard_map/turn_blocks/pallas_call | solution.py:131
  50.1 0.0 copy-start.1
  50.1 5.8 %copy-done.1 = bf16[128,256,256]{2,1,0:T(8,128)(2,1)S(1)} copy-done((bf16[128,256,256]{2,1,0:T(8,128)(2,1)S(1)}, bf16[128,256,256]{2,1,0:T(8,128)(2,1)}, u32[]{:S(2)}) %copy-start.1) | copy-done | bytes 16777240
  55.9 8.5 %near_field.1.refs_15_ = f32[33,256,128]{2,1,0:T(8,128)S(1)} custom-call(s32[128]{0:T(128)S(1)} %copy-done.11, s32[128]{0:T(128)S(1)} %copy-done.12, s32[1]{0:T(128)S(6)} %copy.14.count, bf16[256,128]{1,0:T(8,128)(2,1)S(1)} %collective-permute-done.8.before, bf16[256,128]{1,0:T(8,128)(2,1)S(1)} %collective-permute-done.9.after, ...), custom_call_target="tpu_custom_call" | custom-call | flops 2147483648 | bytes 16777216 | tf_op jit(solution)/shard_map/near_field/pallas_call | solution.py:167
  64.4 2.0 %copy-done = f32[33,256,128]{2,1,0:T(8,128)} copy-done((f32[33,256,128]{2,1,0:T(8,128)}, f32[33,256,128]{2,1,0:T(8,128)S(1)}, u32[]{:S(2)}) %copy-start) | copy-done | bytes 4325400
  66.4 23.4 %result.1 = f32[64,8192]{1,0:T(8,128)} custom-call(s32[8192]{0:T(1024)S(1)} %copy-done.10, s32[768]{0:T(1024)S(1)} %pad_add_fusion.refs_1_, bf16[24,64,128]{2,1,0:T(8,128)(2,1)S(1)} %get-tuple-element.8.refs_2_, bf16[24,64,128]{2,1,0:T(8,128)(2,1)} %collective-permute-done.refs_3_, bf16[24,64,128]{2,1,0:T(8,128)(2,1)} %collective-permute-done.1.refs_4_, ...), custom_call_target="tpu_custom_call" | custom-call | tf_op jit(solution)/shard_map/result/pallas_call | solution.py:248
  (26 shorter events, 0.1 us)
Async XLA Ops:
  0.0 1.2 %copy-start.3 = (bf16[32,256,64]{1,2,0:T(8,128)(2,1)S(1)}, bf16[32,256,64]{1,2,0:T(8,128)(2,1)}, u32[]{:S(2)}) copy-start(bf16[32,256,64]{1,2,0:T(8,128)(2,1)} %param.14) | copy-start | bytes 3145732
  1.2 1.0 %copy-start.6 = (bf16[32,64,64]{2,1,0:T(8,128)(2,1)S(1)}, bf16[32,64,64]{2,1,0:T(8,128)(2,1)}, u32[]{:S(2)}) copy-start(bf16[32,64,64]{2,1,0:T(8,128)(2,1)} %refs_13_.1) | copy-start | bytes 786436
  2.3 1.2 %copy-start.8 = (bf16[8192,64]{0,1:T(8,128)(2,1)S(1)}, bf16[8192,64]{0,1:T(8,128)(2,1)}, u32[]{:S(2)}) copy-start(bf16[8192,64]{0,1:T(8,128)(2,1)} %param.12) | copy-start | bytes 3145732
  3.5 0.8 copy-start.9
  14.8 15.2 %collective-permute-start.5 = (bf16[24,64,128]{2,1,0:T(8,128)(2,1)S(1)}, bf16[24,64,128]{2,1,0:T(8,128)(2,1)S(1)}, u32[]{:S(2)}, u32[]{:S(2)}) collective-permute-start(bf16[24,64,128]{2,1,0:T(8,128)(2,1)S(1)} %get-tuple-element.8.refs_2_), channel_id=1, source_target_pairs={{8,16},{24,32},{40,48},{56,64},{72,80},{88,96},{104,112},{120,0},{... | collective-permute-start | bytes 1179656 | tf_op jit(solution)/shard_map/ppermute | solution.py:279
  20.7 14.3 %collective-permute-start.2 = (bf16[24,64,128]{2,1,0:T(8,128)(2,1)S(1)}, bf16[24,64,128]{2,1,0:T(8,128)(2,1)S(1)}, u32[]{:S(2)}, u32[]{:S(2)}) collective-permute-start(bf16[24,64,128]{2,1,0:T(8,128)(2,1)S(1)} %get-tuple-element.8.refs_2_), channel_id=1, source_target_pairs={{0,8},{16,24},{32,40},{48,56},{64,72},{80,88},{96,104},{112,120},{... | collective-permute-start | bytes 1179656 | tf_op jit(solution)/shard_map/ppermute | solution.py:279
  20.7 14.3 %collective-permute-start.1 = (bf16[24,64,128]{2,1,0:T(8,128)(2,1)S(1)}, bf16[24,64,128]{2,1,0:T(8,128)(2,1)}, u32[]{:S(2)}, u32[]{:S(2)}) collective-permute-start(bf16[24,64,128]{2,1,0:T(8,128)(2,1)S(1)} %get-tuple-element.8.refs_2_), channel_id=1, source_target_pairs={{1,2},{3,4},{5,6},{7,0},{2,1},{4,3},{6,5},{0,7},{9,10},{11,12},{13... | collective-permute-start | bytes 1179656 | tf_op jit(solution)/shard_map/ppermute | solution.py:279
  23.2 6.5 %collective-permute-start.9 = (bf16[256,128]{1,0:T(8,128)(2,1)S(1)}, bf16[256,128]{1,0:T(8,128)(2,1)S(1)}, u32[]{:S(2)}, u32[]{:S(2)}) collective-permute-start(bf16[256,128]{1,0:T(8,128)(2,1)S(1)} %get-tuple-element.11), channel_id=1, source_target_pairs={{1,0},{2,1},{3,2},{4,3},{5,4},{6,5},{7,6},{8,7},{9,8},{10,9},{11,1... | collective-permute-start | bytes 196616 | tf_op jit(solution)/shard_map/ppermute | solution.py:322
  26.7 5.5 %collective-permute-start.8 = (bf16[256,128]{1,0:T(8,128)(2,1)S(1)}, bf16[256,128]{1,0:T(8,128)(2,1)S(1)}, u32[]{:S(2)}, u32[]{:S(2)}) collective-permute-start(bf16[256,128]{1,0:T(8,128)(2,1)S(1)} %get-tuple-element.12), channel_id=1, source_target_pairs={{0,1},{1,2},{2,3},{3,4},{4,5},{5,6},{6,7},{7,8},{8,9},{9,10},{10,1... | collective-permute-start | bytes 196616 | tf_op jit(solution)/shard_map/ppermute | solution.py:321
  29.7 36.6 %collective-permute-start = (bf16[24,64,128]{2,1,0:T(8,128)(2,1)S(1)}, bf16[24,64,128]{2,1,0:T(8,128)(2,1)}, u32[]{:S(2)}, u32[]{:S(2)}) collective-permute-start(bf16[24,64,128]{2,1,0:T(8,128)(2,1)S(1)} %get-tuple-element.8.refs_2_), channel_id=1, source_target_pairs={{0,1},{2,3},{4,5},{6,7},{1,0},{3,2},{5,4},{7,6},{8,9},{10,11},{12,... | collective-permute-start | bytes 1179656 | tf_op jit(solution)/shard_map/ppermute | solution.py:279
  30.0 36.3 %collective-permute-start.7 = (bf16[24,64,128]{2,1,0:T(8,128)(2,1)S(1)}, bf16[24,64,128]{2,1,0:T(8,128)(2,1)}, u32[]{:S(2)}, u32[]{:S(2)}) collective-permute-start(bf16[24,64,128]{2,1,0:T(8,128)(2,1)S(1)} %collective-permute-done.5.refs_8_), channel_id=1, source_target_pairs={{1,2},{3,4},{5,6},{7,0},{2,1},{4,3},{6,5},{0,7},{9,10},{11,12},{13... | collective-permute-start | bytes 1179656 | tf_op jit(solution)/shard_map/ppermute | solution.py:279
  32.3 34.1 %collective-permute-start.6 = (bf16[24,64,128]{2,1,0:T(8,128)(2,1)S(1)}, bf16[24,64,128]{2,1,0:T(8,128)(2,1)}, u32[]{:S(2)}, u32[]{:S(2)}) collective-permute-start(bf16[24,64,128]{2,1,0:T(8,128)(2,1)S(1)} %collective-permute-done.5.refs_8_), channel_id=1, source_target_pairs={{0,1},{2,3},{4,5},{6,7},{1,0},{3,2},{5,4},{7,6},{8,9},{10,11},{12,... | collective-permute-start | bytes 1179656 | tf_op jit(solution)/shard_map/ppermute | solution.py:279
  35.0 31.4 %collective-permute-start.4 = (bf16[24,64,128]{2,1,0:T(8,128)(2,1)S(1)}, bf16[24,64,128]{2,1,0:T(8,128)(2,1)}, u32[]{:S(2)}, u32[]{:S(2)}) collective-permute-start(bf16[24,64,128]{2,1,0:T(8,128)(2,1)S(1)} %collective-permute-done.2.refs_5_), channel_id=1, source_target_pairs={{1,2},{3,4},{5,6},{7,0},{2,1},{4,3},{6,5},{0,7},{9,10},{11,12},{13... | collective-permute-start | bytes 1179656 | tf_op jit(solution)/shard_map/ppermute | solution.py:279
  35.0 31.4 %collective-permute-start.3 = (bf16[24,64,128]{2,1,0:T(8,128)(2,1)S(1)}, bf16[24,64,128]{2,1,0:T(8,128)(2,1)}, u32[]{:S(2)}, u32[]{:S(2)}) collective-permute-start(bf16[24,64,128]{2,1,0:T(8,128)(2,1)S(1)} %collective-permute-done.2.refs_5_), channel_id=1, source_target_pairs={{0,1},{2,3},{4,5},{6,7},{1,0},{3,2},{5,4},{7,6},{8,9},{10,11},{12,... | collective-permute-start | bytes 1179656 | tf_op jit(solution)/shard_map/ppermute | solution.py:279
  37.2 5.4 %copy-start.2 = (bf16[512,64,64]{0,2,1:T(8,128)(2,1)S(1)}, bf16[512,64,64]{0,2,1:T(8,128)(2,1)}, u32[]{:S(2)}) copy-start(bf16[512,64,64]{0,2,1:T(8,128)(2,1)} %param.16) | copy-start | bytes 12582916
  37.2 1.7 %copy-start.5 = (bf16[256,64,64]{0,2,1:T(8,128)(2,1)S(1)}, bf16[256,64,64]{0,2,1:T(8,128)(2,1)}, u32[]{:S(2)}) copy-start(bf16[256,64,64]{0,2,1:T(8,128)(2,1)} %param.17) | copy-start | bytes 6291460
  42.7 7.4 %copy-start.11 = (s32[128]{0:T(128)S(1)}, s32[128]{0:T(128)}, u32[]{:S(2)}) copy-start(s32[128]{0:T(128)} %targets.1) | copy-start | bytes 1540
  42.7 7.4 %copy-start.12 = (s32[128]{0:T(128)S(1)}, s32[128]{0:T(128)}, u32[]{:S(2)}) copy-start(s32[128]{0:T(128)} %sources.1) | copy-start | bytes 1540
  50.1 5.8 %copy-start.1 = (bf16[128,256,256]{2,1,0:T(8,128)(2,1)S(1)}, bf16[128,256,256]{2,1,0:T(8,128)(2,1)}, u32[]{:S(2)}) copy-start(bf16[128,256,256]{2,1,0:T(8,128)(2,1)} %blocks.1) | copy-start | bytes 50331652
  55.9 10.5 %copy-start.4 = (bf16[32,256,64]{1,2,0:T(8,128)(2,1)S(1)}, bf16[32,256,64]{1,2,0:T(8,128)(2,1)}, u32[]{:S(2)}) copy-start(bf16[32,256,64]{1,2,0:T(8,128)(2,1)} %param.14) | copy-start | bytes 3145732
  55.9 10.5 %copy-start.7 = (bf16[32,64,64]{2,1,0:T(8,128)(2,1)S(1)}, bf16[32,64,64]{2,1,0:T(8,128)(2,1)}, u32[]{:S(2)}) copy-start(bf16[32,64,64]{2,1,0:T(8,128)(2,1)} %refs_13_.1) | copy-start | bytes 786436
  55.9 10.6 %copy-start.10 = (s32[8192]{0:T(1024)S(1)}, s32[8192]{0:T(1024)}, u32[]{:S(2)}) copy-start(s32[8192]{0:T(1024)} %refs_0_.1) | copy-start | bytes 98308
  64.4 2.0 %copy-start = (f32[33,256,128]{2,1,0:T(8,128)}, f32[33,256,128]{2,1,0:T(8,128)S(1)}, u32[]{:S(2)}) copy-start(f32[33,256,128]{2,1,0:T(8,128)S(1)} %near_field.1.refs_15_) | copy-start | bytes 12976132

commit v2 on v1

v2 whole, which is shorter than its diff:
```python
import jax
import jax.numpy as jnp
from jax import lax
from jax.experimental import pallas as pl
from jax.experimental.pallas import tpu as pltpu
from jax.sharding import PartitionSpec as P

LEAVES = 32
PARENTS = LEAVES // 2
POINTS = 256
RANK = 64
COLS = 64
ENTRIES = 16
HALO = 2
TASKS = 128
ROWS = LEAVES * POINTS
PAIRS = LEAVES // 2 + PARENTS // 2
TASK_STEP = 16
LEAF_STEP = 4
CHUNK = 1024
POINT_PARTS = 4
OUT_PARTS = 8
ORDER_MIB = 60
NEAR_MIB = 48
HELD = 4
PITCH = RANK // 2 + 1

SMEM = pltpu.SMEM
VMEM = pltpu.VMEM
F32 = jnp.float32
BF16 = jnp.bfloat16


def params(mib):
    return pltpu.CompilerParams(vmem_limit_bytes=mib << 20)


def low_half(rows):
    return lax.broadcasted_iota(jnp.int32, (rows, 128), 1) < 64


def swap_halves(x):
    return jnp.concatenate([x[:, 64:], x[:, :64]], axis=1)


def order_kernel(
    perm,
    points,
    basis,
    transfer,
    ordered,
    skeleton,
    edges,
    table,
    even,
    odd,
    fine,
    first_rows,
    second_rows,
    points_here,
    basis_here,
    transfer_here,
    ordered_here,
    sems,
    out_sems,
):
    width = ROWS // POINT_PARTS

    def part(n):
        span = pl.ds(n * width, width)
        return pltpu.make_async_copy(points.at[:, span], points_here.at[:, span], sems.at[n])

    def load_rows(chunk, into, sem):
        return pltpu.make_async_copy(
            perm.at[pl.ds(chunk * CHUNK, CHUNK)], into, sems.at[POINT_PARTS + sem]
        )

    for n in range(POINT_PARTS):
        part(n).start()
    load_rows(0, first_rows, 0).start()
    load_rows(1, second_rows, 1).start()
    bases = pltpu.make_async_copy(basis, basis_here, sems.at[POINT_PARTS + 2])
    transfers = pltpu.make_async_copy(transfer, transfer_here, sems.at[POINT_PARTS + 3])
    bases.start()
    transfers.start()
    for n in range(POINT_PARTS):
        part(n).wait()
        for c in range(n * width // 128, (n + 1) * width // 128):
            block = points_here[:, c * 128 : (c + 1) * 128].astype(F32)
            table[c * 128 : (c + 1) * 128, :] = jnp.concatenate([block, block], axis=0).T
    bases.wait()

    leaves = CHUNK // POINTS

    def gather(places, into):
        for i in range(CHUNK):
            into[i : i + 1, :] = table[pl.ds(places[i], 1), :]

    def finish(chunk, source):
        for n in range(leaves):
            leaf = chunk * leaves + n
            block = source[n * POINTS : (n + 1) * POINTS, :].astype(BF16)
            ordered_here[leaf] = block
            fine[leaf] = jnp.dot(basis_here[leaf], block, preferred_element_type=F32).astype(BF16)

    def send(chunk):
        span = pl.ds(chunk * leaves, leaves)
        return pltpu.make_async_copy(ordered_here.at[span], ordered.at[span], out_sems.at[chunk])

    chunks = ROWS // CHUNK
    load_rows(0, first_rows, 0).wait()
    gather(first_rows, even)

    def two_chunks(step, _):
        load_rows(2 * step + 1, second_rows, 1).wait()
        load_rows(2 * step + 2, first_rows, 0).start()
        finish(2 * step, even)
        gather(second_rows, odd)
        send(2 * step).start()

        load_rows(2 * step + 3, second_rows, 1).start()
        load_rows(2 * step + 2, first_rows, 0).wait()
        finish(2 * step + 1, odd)
        gather(first_rows, even)
        send(2 * step + 1).start()
        return 0

    lax.fori_loop(0, chunks // 2 - 1, two_chunks, 0)
    load_rows(chunks - 1, second_rows, 1).wait()
    finish(chunks - 2, even)
    gather(second_rows, odd)
    send(chunks - 2).start()
    finish(chunks - 1, odd)
    send(chunks - 1).start()

    transfers.wait()
    low = low_half(RANK)
    low_points = low_half(POINTS)
    for p in range(PARENTS):
        skeleton[p] = jnp.where(low, fine[2 * p], fine[2 * p + 1])
    for q in range(PARENTS // 2):
        coarse = []
        for p in (2 * q, 2 * q + 1):
            pair = transfer_here[2 * p : 2 * p + 2].reshape(2 * RANK, RANK)
            stacked = fine[2 * p : 2 * p + 2].reshape(2 * RANK, 128)
            coarse.append(
                lax.dot_general(
                    pair, stacked, (((0,), (0,)), ((), ())), preferred_element_type=F32
                ).astype(BF16)
            )
        skeleton[PARENTS + q] = jnp.where(low, coarse[0], coarse[1])
    edges[0] = jnp.where(low_points, ordered_here[0], ordered_here[1])
    edges[1] = jnp.where(low_points, ordered_here[LEAVES - 2], ordered_here[LEAVES - 1])
    for chunk in range(ROWS // CHUNK):
        send(chunk).wait()


def order_points(points, perm, basis, transfer):
    anywhere = pl.BlockSpec(memory_space=pl.ANY)
    return pl.pallas_call(
        order_kernel,
        out_shape=(
            jax.ShapeDtypeStruct((LEAVES, POINTS, 128), BF16),
            jax.ShapeDtypeStruct((PAIRS, RANK, 128), BF16),
            jax.ShapeDtypeStruct((2, POINTS, 128), BF16),
        ),
        in_specs=[anywhere] * 4,
        out_specs=(
            pl.BlockSpec(memory_space=pl.ANY),
            pl.BlockSpec(memory_space=VMEM),
            pl.BlockSpec(memory_space=VMEM),
        ),
        scratch_shapes=[
            pltpu.VMEM((ROWS, 128), F32),
            pltpu.VMEM((CHUNK, 128), F32),
            pltpu.VMEM((CHUNK, 128), F32),
            pltpu.VMEM((LEAVES, RANK, 128), BF16),
            pltpu.SMEM((CHUNK,), jnp.int32),
            pltpu.SMEM((CHUNK,), jnp.int32),
            pltpu.VMEM((COLS, ROWS), BF16),
            pltpu.VMEM((LEAVES, RANK, POINTS), BF16),
            pltpu.VMEM((LEAVES, RANK, RANK), BF16),
            pltpu.VMEM((LEAVES, POINTS, 128), BF16),
            pltpu.SemaphoreType.DMA((POINT_PARTS + 4,)),
            pltpu.SemaphoreType.DMA((ROWS // CHUNK,)),
        ],
        compiler_params=params(ORDER_MIB),
        name="order_points",
    )(perm, points, basis, transfer)


def turn_kernel(blocks, turned, table):
    half = RANK // 2
    targets = 128 // ENTRIES
    low = low_half(half)

    def tile(n, _):
        entries = pl.ds(pl.multiple_of(n * 128, 128), 128)
        for k in range(half):
            block = jnp.concatenate([blocks[k, :, entries], blocks[k + half, :, entries]], axis=0)
            table[pl.ds(k, 128, stride=PITCH), :] = block.astype(F32).T
        for t in range(targets):
            into = turned.at[n * targets + t]
            for j in range(0, ENTRIES, 2):
                first = table[pl.ds((t * ENTRIES + j) * PITCH, half), :]
                second = table[pl.ds((t * ENTRIES + j + 1) * PITCH, half), :]
                into[:half, j * 64 : (j + 2) * 64] = jnp.where(
                    low, first, pltpu.roll(second, 64, 1)
                ).astype(BF16)
                into[half:, j * 64 : (j + 2) * 64] = jnp.where(
                    low, pltpu.roll(first, 64, 1), second
                ).astype(BF16)
        return 0

    lax.fori_loop(0, blocks.shape[2] // 128, tile, 0)


def turn_blocks(blocks):
    return pl.pallas_call(
        turn_kernel,
        out_shape=jax.ShapeDtypeStruct((blocks.shape[2] // ENTRIES, RANK, ENTRIES * RANK), BF16),
        in_specs=[pl.BlockSpec(memory_space=VMEM)],
        out_specs=pl.BlockSpec(memory_space=VMEM),
        scratch_shapes=[pltpu.VMEM((128 * PITCH, 128), F32)],
        compiler_params=params(24),
        cost_estimate=pl.CostEstimate(
            flops=0, bytes_accessed=6 * blocks.size, transcendentals=0
        ),
        name="turn_blocks",
    )(blocks)


def near_kernel(
    targets, sources, count, before, after, ordered, blocks, total, window, held, sem, sems
):
    steps = TASKS // TASK_STEP

    def fetch(step):
        slot = lax.rem(step, HELD)
        tasks = pl.ds(step * TASK_STEP, TASK_STEP)
        return pltpu.make_async_copy(blocks.at[tasks], held.at[slot], sems.at[slot])

    copy = pltpu.make_async_copy(ordered, window.at[pl.ds(HALO, LEAVES)], sem)
    copy.start()
    for step in range(HELD - 1):
        fetch(step).start()
    low = low_half(POINTS)
    for pair, place in ((before[...], 0), (after[...], LEAVES + HALO)):
        swapped = swap_halves(pair)
        window[place] = jnp.where(low, pair, swapped)
        window[place + 1] = jnp.where(low, swapped, pair)
    total[...] = jnp.zeros_like(total)
    copy.wait()

    def one_step(step, _):
        slot = lax.rem(step, HELD)
        fetch(step).wait()

        @pl.when(step < steps - (HELD - 1))
        def _():
            fetch(step + HELD - 1).start()

        for i in range(TASK_STEP):
            task = step * TASK_STEP + i
            target = jnp.where(task < count[0], targets[task], LEAVES)
            total[target] += jnp.dot(
                held[slot, i], window[sources[task]], preferred_element_type=F32
            )
        return 0

    lax.fori_loop(0, steps, one_step, 0)


def near_field(targets, sources, count, before, after, ordered, blocks):
    return pl.pallas_call(
        near_kernel,
        out_shape=jax.ShapeDtypeStruct((LEAVES + 1, POINTS, 128), F32),
        in_specs=[
            pl.BlockSpec(memory_space=SMEM),
            pl.BlockSpec(memory_space=SMEM),
            pl.BlockSpec(memory_space=SMEM),
            pl.BlockSpec(memory_space=VMEM),
            pl.BlockSpec(memory_space=VMEM),
            pl.BlockSpec(memory_space=pl.ANY),
            pl.BlockSpec(memory_space=pl.ANY),
        ],
        out_specs=pl.BlockSpec(memory_space=VMEM),
        scratch_shapes=[
            pltpu.VMEM((LEAVES + 2 * HALO, POINTS, 128), BF16),
            pltpu.VMEM((HELD, TASK_STEP, POINTS, POINTS), BF16),
            pltpu.SemaphoreType.DMA,
            pltpu.SemaphoreType.DMA((HELD,)),
        ],
        compiler_params=params(NEAR_MIB),
        cost_estimate=pl.CostEstimate(
            flops=2 * TASKS * POINTS * POINTS * 128,
            bytes_accessed=2 * TASKS * POINTS * POINTS,
            transcendentals=0,
        ),
        name="near_field",
    )(targets, sources, count, before, after, ordered, blocks)


def result_kernel(*refs):
    perm, slots = refs[:2]
    skeletons = refs[2:11]
    fine, coarse, transfer, basis, near, out = refs[11:17]
    spread, below, above, first_rows, second_rows, table, wide = refs[17:24]
    first_places, second_places, sems, out_sems = refs[24:]
    steps = LEAVES // LEAF_STEP

    def load_places(step, into, sem):
        return pltpu.make_async_copy(perm.at[pl.ds(step * CHUNK, CHUNK)], into, sems.at[sem])

    load_places(0, first_places, 0).start()
    load_places(1, second_places, 1).start()
    low = low_half(RANK)
    keep = (low.astype(F32).astype(BF16), (~low).astype(F32).astype(BF16))
    for a in range(9):

        def part(p, _):
            for z in range(2):
                spread[a * 2 * PAIRS + 2 * p + z] = skeletons[a][p] * keep[z]
            return 0

        lax.fori_loop(0, PAIRS, part, 0, unroll=8)

    def coupled(matrix, first):
        picked = [spread[slots[first + j]] for j in range(ENTRIES)]
        return jnp.dot(matrix, jnp.concatenate(picked, axis=0), preferred_element_type=F32)

    def couple(step, _):
        for p in range(2):
            parent = step * 2 + p
            above[parent] = coupled(coarse[parent], (LEAVES + parent) * ENTRIES)
        for c in range(4):
            leaf = step * 4 + c
            below[leaf] = coupled(fine[leaf], leaf * ENTRIES)
        return 0

    lax.fori_loop(0, LEAVES // 4, couple, 0)

    def fold(halves):
        return halves + pltpu.roll(halves, 64, 1)

    def compute(step, rows):
        for p in range(LEAF_STEP // 2):
            parent = step * (LEAF_STEP // 2) + p
            from_parent = fold(above[parent]).astype(BF16)
            for z in range(2):
                c = 2 * p + z
                leaf = step * LEAF_STEP + c
                local = fold(below[leaf])
                local += jnp.dot(transfer[leaf], from_parent, preferred_element_type=F32)
                far = lax.dot_general(
                    basis[leaf],
                    local.astype(BF16),
                    (((0,), (0,)), ((), ())),
                    preferred_element_type=F32,
                )
                rows[c * POINTS : (c + 1) * POINTS, :] = far + near[leaf]

    def scatter(places, rows):
        for i in range(CHUNK):
            table[pl.ds(places[i], 1), :] = rows[i : i + 1, :]

    compute(0, first_rows)

    def two_steps(pair, _):
        load_places(2 * pair, first_places, 0).wait()
        compute(2 * pair + 1, second_rows)
        scatter(first_places, first_rows)
        more = pair < steps // 2 - 1

        @pl.when(more)
        def _():
            load_places(2 * pair + 2, first_places, 0).start()

        load_places(2 * pair + 1, second_places, 1).wait()
        compute(jnp.minimum(2 * pair + 2, steps - 1), first_rows)
        scatter(second_places, second_rows)

        @pl.when(more)
        def _():
            load_places(2 * pair + 3, second_places, 1).start()

        return 0

    lax.fori_loop(0, steps // 2, two_steps, 0)

    low = low_half(128)
    sends = []
    for n in range(OUT_PARTS):
        width = ROWS // OUT_PARTS
        for c in range(n * width // 128, (n + 1) * width // 128):
            block = table[c * 128 : (c + 1) * 128, :]
            high = block.astype(BF16)
            rest = (block - high.astype(F32)).astype(BF16)
            both = jnp.where(low, high, rest).T.astype(F32)
            wide[:, c * 128 : (c + 1) * 128] = both[:COLS] + both[COLS:]
        span = pl.ds(n * width, width)
        sends.append(pltpu.make_async_copy(wide.at[:, span], out.at[:, span], out_sems.at[n]))
        sends[-1].start()
    for send in sends:
        send.wait()


def result(perm, slots, skeletons, fine, coarse, transfer, basis, near):
    return pl.pallas_call(
        result_kernel,
        out_shape=jax.ShapeDtypeStruct((COLS, ROWS), F32),
        in_specs=[
            pl.BlockSpec(memory_space=pl.ANY),
            pl.BlockSpec(memory_space=SMEM),
            *[pl.BlockSpec(memory_space=VMEM)] * 14,
        ],
        out_specs=pl.BlockSpec(memory_space=pl.ANY),
        scratch_shapes=[
            pltpu.VMEM((9 * 2 * PAIRS, RANK, 128), BF16),
            pltpu.VMEM((LEAVES, RANK, 128), F32),
            pltpu.VMEM((PARENTS, RANK, 128), F32),
            pltpu.VMEM((CHUNK, 128), F32),
            pltpu.VMEM((CHUNK, 128), F32),
            pltpu.VMEM((ROWS, 128), F32),
            pltpu.VMEM((COLS, ROWS), F32),
            pltpu.SMEM((CHUNK,), jnp.int32),
            pltpu.SMEM((CHUNK,), jnp.int32),
            pltpu.SemaphoreType.DMA((2,)),
            pltpu.SemaphoreType.DMA((OUT_PARTS,)),
        ],
        compiler_params=params(36),
        name="result",
    )(perm, slots, *skeletons, fine, coarse, transfer, basis, near)


def swaps(count, odd):
    pairs = [((i + odd) % count, (i + odd + 1) % count) for i in range(0, count, 2)]
    return [(a, b) for a, b in pairs] + [(b, a) for a, b in pairs]


def swap(x, axis, odd):
    return lax.ppermute(x, axis, swaps(lax.axis_size(axis), odd))


def places(lists, clusters, first):
    outer, inner = lax.axis_size("gx"), lax.axis_size("gy")
    gx, gy = lax.axis_index("gx"), lax.axis_index("gy")
    owner = lists // clusters
    step_x = (owner // inner - gx + outer) % outer
    step_y = (owner % inner - gy + inner) % inner
    array_x = jnp.where(step_x == 0, 0, jnp.where((step_x == 1) == (gx % 2 == 0), 1, 2))
    array_y = jnp.where(step_y == 0, 0, jnp.where((step_y == 1) == (gy % 2 == 0), 1, 2))
    return (array_x * 3 + array_y) * (2 * PAIRS) + first + lists % clusters


def on_device(
    points_in,
    tree_perm,
    basis,
    transfer,
    couple_fine,
    couple_coarse,
    list_fine,
    list_coarse,
    near_blocks,
    near_target,
    near_source,
    task_count,
):
    basis_rows = basis.transpose(0, 2, 1)
    slots = jnp.concatenate(
        [
            places(list_fine, LEAVES, 0).reshape(-1),
            places(list_coarse, PARENTS, LEAVES).reshape(-1),
        ]
    )
    ordered, own, edges = order_points(points_in.T, tree_perm, basis_rows, transfer)
    x_even = swap(own, "gx", 0)
    x_odd = swap(own, "gx", 1)
    y_even = swap(own, "gy", 0)
    y_odd = swap(own, "gy", 1)
    both = ("gx", "gy")
    last = lax.axis_size(both) - 1
    before = lax.ppermute(edges[1], both, [(i, i + 1) for i in range(last)])
    after = lax.ppermute(edges[0], both, [(i + 1, i) for i in range(last)])
    fine = turn_blocks(couple_fine.transpose(1, 2, 0))
    coarse = turn_blocks(couple_coarse.transpose(1, 2, 0))
    near = near_field(near_target, near_source, task_count, before, after, ordered, near_blocks)
    skeletons = [own, y_even, y_odd]
    for x in (x_even, x_odd):
        skeletons += [x, swap(x, "gy", 0), swap(x, "gy", 1)]
    out = result(tree_perm, slots, skeletons, fine, coarse, transfer, basis_rows, near)
    return out.T


def solution(mesh):
    flat = P(("gx", "gy"))
    return jax.shard_map(
        on_device,
        mesh=mesh,
        in_specs=(flat,) * 12,
        out_specs=flat,
        check_vma=False,
    )
```

time: 90.3 us -> 62.4 us (0.69)
  Pallas kernels: 53.5 us -> 35.8 us
  local copies, waits for them, and re-layouts: 14 us -> 4.24 us
    pallas_call x4, Pallas kernels: 42.9 us -> 26.7 us  [the longest x1 12.6 us: result(): pl.pallas_call(result_kernel, out_shape=jax.ShapeDtypeStruct((COLS, ROWS)...]
    unnamed x26 -> x20, local copies, waits for them, and re-layouts: 13.8 us -> 3.12 us
    pallas_call x1, Pallas kernels: 10.6 us -> 9.11 us  [order_points(): pl.pallas_call(order_kernel, out_shape=(jax.ShapeDtypeStruct((LEAVES, POI...]
  transfers between devices with their start and end apart: 10 -> 10, of which waited for: 1 -> 0; matrix products, arithmetic and copies ran while one was open for 2% -> 4% of each run, Pallas kernels for 22% -> 23%
where the time goes in v2:
time: 62.4 us; the launch traced here: 61.8 us
  Pallas kernels  35.8 us (57%)
  starting transfers between devices  19.4 us (31%)
  local copies, waits for them, and re-layouts  4.24 us (7%)
  other arithmetic  1.48 us (2%)
  between operations  0.9 us (1%)
    ppermute x8, starting transfers between devices, swap(): return lax.ppermute(x, axis, swaps(lax.axis_size(axis), odd))  13.8 us
    pallas_call x1, Pallas kernels, result(): pl.pallas_call(result_kernel, out_shape=jax.ShapeDtypeStruct((COLS, ROWS)...  12.6 us
    pallas_call x1, Pallas kernels, near_field(): pl.pallas_call(near_kernel, out_shape=jax.ShapeDtypeStruct((LEAVES + 1, P...  10.1 us
    pallas_call x1, Pallas kernels, order_points(): pl.pallas_call(order_kernel, out_shape=(jax.ShapeDtypeStruct((LEAVES, POI...  9.11 us
    pallas_call x2, Pallas kernels, turn_blocks(): pl.pallas_call(turn_kernel, out_shape=jax.ShapeDtypeStruct((blocks.shape[...  3.94 us
    ppermute x1, starting transfers between devices, on_device(): after = lax.ppermute(edges[0], both, [(i + 1, i) for i in range(last)])  3.58 us
    unnamed x20, local copies, waits for them, and re-layouts  3.12 us
    ppermute x1, starting transfers between devices, on_device(): before = lax.ppermute(edges[1], both, [(i, i + 1) for i in range(last)])  1.98 us
  transfers between devices with their start and end apart: 10, of which 0 were waited for; matrix products, arithmetic and copies ran while one was open for 4% of the time, Pallas kernels for 23%

profile of v2, /device:TPU:1, one launch (start us, length us, event | category | flops | bytes accessed | tf_op | source)
XLA Modules:
  0.0 61.8 jit_solution(4838727967141249603)
XLA Ops:
  0.0 9.1 %order_points.1 = (bf16[32,256,128]{2,1,0:T(8,128)(2,1)}, bf16[24,64,128]{2,1,0:T(8,128)(2,1)}, bf16[2,256,128]{2,1,0:T(8,128)(2,1)}) custom-call(s32[8192]{0:T(1024)} %refs_0_.1, bf16[64,8192]{1,0:T(8,128)(2,1)} %bitcast.13, bf16[32,64,256]{2,1,0:T(8,128)(2,1)} %bitcast.10, bf16[32,64,64]{2,1,0:T(8,128)(2,1)} %refs_13_.1), custom_call_target="tpu_custom_call" | custom-call | tf_op jit(solution)/shard_map/order_points/pallas_call | solution.py:160
  9.1 5.8 %collective-permute-start.5 = (bf16[24,64,128]{2,1,0:T(8,128)(2,1)}, bf16[24,64,128]{2,1,0:T(8,128)(2,1)S(1)}, u32[]{:S(2)}, u32[]{:S(2)}) collective-permute-start(bf16[24,64,128]{2,1,0:T(8,128)(2,1)} %get-tuple-element.8.refs_2_), channel_id=1, source_target_pairs={{8,16},{24,32},{40,48},{56,64},{72,80},{88,96},{104,112},{120,0},{... | collective-permute-start | bytes 1179656 | tf_op jit(solution)/shard_map/ppermute | solution.py:442
  15.0 0.0 collective-permute-start.2
  15.0 2.5 %collective-permute-start.1 = (bf16[24,64,128]{2,1,0:T(8,128)(2,1)}, bf16[24,64,128]{2,1,0:T(8,128)(2,1)S(1)}, u32[]{:S(2)}, u32[]{:S(2)}) collective-permute-start(bf16[24,64,128]{2,1,0:T(8,128)(2,1)} %get-tuple-element.8.refs_2_), channel_id=1, source_target_pairs={{1,2},{3,4},{5,6},{7,0},{2,1},{4,3},{6,5},{0,7},{9,10},{11,12},{13... | collective-permute-start | bytes 1179656 | tf_op jit(solution)/shard_map/ppermute | solution.py:442
  17.4 0.9 %slice_bitcast_fusion = (bf16[256,128]{1,0:T(8,128)(2,1)S(1)}, bf16[256,128]{1,0:T(8,128)(2,1)S(1)}) fusion(bf16[2,256,128]{2,1,0:T(8,128)(2,1)} %get-tuple-element.9), kind=kLoop, calls=%fused_computation | loop fusion | bytes 262144 | tf_op jit(solution)/shard_map/squeeze | solution.py:485
  18.3 3.6 %collective-permute-start.9 = (bf16[256,128]{1,0:T(8,128)(2,1)S(1)}, bf16[256,128]{1,0:T(8,128)(2,1)S(1)}, u32[]{:S(2)}, u32[]{:S(2)}) collective-permute-start(bf16[256,128]{1,0:T(8,128)(2,1)S(1)} %get-tuple-element.11), channel_id=1, source_target_pairs={{1,0},{2,1},{3,2},{4,3},{5,4},{6,5},{7,6},{8,7},{9,8},{10,9},{11,1... | collective-permute-start | bytes 196616 | tf_op jit(solution)/shard_map/ppermute | solution.py:485
  21.9 2.0 %collective-permute-start.8 = (bf16[256,128]{1,0:T(8,128)(2,1)S(1)}, bf16[256,128]{1,0:T(8,128)(2,1)S(1)}, u32[]{:S(2)}, u32[]{:S(2)}) collective-permute-start(bf16[256,128]{1,0:T(8,128)(2,1)S(1)} %get-tuple-element.12), channel_id=1, source_target_pairs={{0,1},{1,2},{2,3},{3,4},{4,5},{5,6},{6,7},{7,8},{8,9},{9,10},{10,1... | collective-permute-start | bytes 196616 | tf_op jit(solution)/shard_map/ppermute | solution.py:484
  23.9 0.7 %fusion.6 = s32[32,16]{0,1:T(8,128)S(1)} fusion(s32[32,16]{0,1:T(8,128)} %param.18, s32[]{:T(128)S(6)} %axis_index.33, s32[]{:T(128)S(6)} %axis_index.15, pred[]{:T(512)S(6)} %eq.78, pred[]{:T(512)S(6)} %eq.73), kind=kLoop, calls=%fused_computation.40 | loop fusion | flops 39936 | bytes 4106 | tf_op jit(solution)/shard_map/add | solution.py:453
  24.7 0.0 collective-permute-done.9.after
  24.7 0.5 collective-permute-start
  25.2 0.0 collective-permute-done.5.refs_8_
  25.2 1.6 %collective-permute-start.7 = (bf16[24,64,128]{2,1,0:T(8,128)(2,1)S(1)}, bf16[24,64,128]{2,1,0:T(8,128)(2,1)}, u32[]{:S(2)}, u32[]{:S(2)}) collective-permute-start(bf16[24,64,128]{2,1,0:T(8,128)(2,1)S(1)} %collective-permute-done.5.refs_8_), channel_id=1, source_target_pairs={{1,2},{3,4},{5,6},{7,0},{2,1},{4,3},{6,5},{0,7},{9,10},{11,12},{13... | collective-permute-start | bytes 1179656 | tf_op jit(solution)/shard_map/ppermute | solution.py:442
  26.8 0.0 collective-permute-done.8.before
  26.8 2.7 %collective-permute-start.6 = (bf16[24,64,128]{2,1,0:T(8,128)(2,1)S(1)}, bf16[24,64,128]{2,1,0:T(8,128)(2,1)}, u32[]{:S(2)}, u32[]{:S(2)}) collective-permute-start(bf16[24,64,128]{2,1,0:T(8,128)(2,1)S(1)} %collective-permute-done.5.refs_8_), channel_id=1, source_target_pairs={{0,1},{2,3},{4,5},{6,7},{1,0},{3,2},{5,4},{7,6},{8,9},{10,11},{12,... | collective-permute-start | bytes 1179656 | tf_op jit(solution)/shard_map/ppermute | solution.py:442
  29.5 0.0 collective-permute-done.2.refs_5_
  29.5 0.0 collective-permute-start.4
  29.5 0.7 %collective-permute-start.3 = (bf16[24,64,128]{2,1,0:T(8,128)(2,1)S(1)}, bf16[24,64,128]{2,1,0:T(8,128)(2,1)}, u32[]{:S(2)}, u32[]{:S(2)}) collective-permute-start(bf16[24,64,128]{2,1,0:T(8,128)(2,1)S(1)} %collective-permute-done.2.refs_5_), channel_id=1, source_target_pairs={{0,1},{2,3},{4,5},{6,7},{1,0},{3,2},{5,4},{7,6},{8,9},{10,11},{12,... | collective-permute-start | bytes 1179656 | tf_op jit(solution)/shard_map/ppermute | solution.py:442
  30.2 0.7 %fusion.13 = s32[16,16]{1,0:T(8,128)S(1)} fusion(s32[16,16]{1,0:T(8,128)} %param.19, s32[]{:T(128)S(6)} %axis_index.33, s32[]{:T(128)S(6)} %axis_index.15, pred[]{:T(512)S(6)} %eq.78, pred[]{:T(512)S(6)} %eq.73), kind=kLoop, calls=%fused_computation.47 | loop fusion | flops 20224 | bytes 2058 | tf_op jit(solution)/shard_map/add | solution.py:453
  31.6 0.1 reshape.7
  31.7 0.1 copy.13
  31.7 0.1 reshape.6
  31.8 1.3 %turn_blocks.3.refs_12_ = bf16[16,64,1024]{2,1,0:T(8,128)(2,1)S(1)} custom-call(bf16[64,64,256]{2,1,0:T(8,128)(2,1)S(1)} %bitcast.12), custom_call_target="tpu_custom_call" | custom-call | bytes 6291456 | tf_op jit(solution)/shard_map/turn_blocks/pallas_call | solution.py:219
  33.2 0.9 %copy-done.1 = bf16[512,64,64]{0,2,1:T(8,128)(2,1)S(1)} copy-done((bf16[512,64,64]{0,2,1:T(8,128)(2,1)S(1)}, bf16[512,64,64]{0,2,1:T(8,128)(2,1)}, u32[]{:S(2)}) %copy-start.1) | copy-done | bytes 4194328
  34.0 2.6 %turn_blocks.2.refs_11_ = bf16[32,64,1024]{2,1,0:T(8,128)(2,1)S(1)} custom-call(bf16[64,64,512]{2,1,0:T(8,128)(2,1)S(1)} %bitcast.9), custom_call_target="tpu_custom_call" | custom-call | bytes 12582912 | tf_op jit(solution)/shard_map/turn_blocks/pallas_call | solution.py:219
  36.7 0.0 copy-start.2
  36.7 0.0 copy-start.5
  36.7 0.0 copy-start.7
  36.8 10.1 %near_field.1.refs_15_ = f32[33,256,128]{2,1,0:T(8,128)} custom-call(s32[128]{0:T(128)S(1)} %copy-done.8, s32[128]{0:T(128)S(1)} %copy-done.9, s32[1]{0:T(128)S(6)} %copy.14.count, bf16[256,128]{1,0:T(8,128)(2,1)S(1)} %collective-permute-done.8.before, bf16[256,128]{1,0:T(8,128)(2,1)S(1)} %collective-permute-done.9.after, ...), custom_call_target="tpu_custom_call" | custom-call | flops 2147483648 | bytes 16777216 | tf_op jit(solution)/shard_map/near_field/pallas_call | solution.py:275
  46.9 0.0 collective-permute-done.6.refs_9_
  46.9 0.0 collective-permute-done.4.refs_7_
  46.9 2.2 %copy-done = f32[33,256,128]{2,1,0:T(8,128)S(1)} copy-done((f32[33,256,128]{2,1,0:T(8,128)S(1)}, f32[33,256,128]{2,1,0:T(8,128)}, u32[]{:S(2)}) %copy-start) | copy-done | bytes 4325400
  49.1 12.6 %result.1 = f32[64,8192]{1,0:T(8,128)} custom-call(s32[8192]{0:T(1024)S(1)} %copy-done.7, s32[768]{0:T(1024)S(1)} %pad_add_fusion.refs_1_, bf16[24,64,128]{2,1,0:T(8,128)(2,1)S(1)} %copy-done.6, bf16[24,64,128]{2,1,0:T(8,128)(2,1)} %collective-permute-done.refs_3_, bf16[24,64,128]{2,1,0:T(8,128)(2,1)S(1)} %collective-permute-done.1.refs_4_, ...), custom_call_target="tpu_custom_call" | custom-call | tf_op jit(solution)/shard_map/result/pallas_call | solution.py:409
  (20 shorter events, 0.0 us)
Async XLA Ops:
  0.0 31.8 %copy-start.4 = (bf16[256,64,64]{0,2,1:T(8,128)(2,1)S(1)}, bf16[256,64,64]{0,2,1:T(8,128)(2,1)}, u32[]{:S(2)}) copy-start(bf16[256,64,64]{0,2,1:T(8,128)(2,1)} %param.17) | copy-start | bytes 6291460
  9.1 16.1 %collective-permute-start.5 = (bf16[24,64,128]{2,1,0:T(8,128)(2,1)}, bf16[24,64,128]{2,1,0:T(8,128)(2,1)S(1)}, u32[]{:S(2)}, u32[]{:S(2)}) collective-permute-start(bf16[24,64,128]{2,1,0:T(8,128)(2,1)} %get-tuple-element.8.refs_2_), channel_id=1, source_target_pairs={{8,16},{24,32},{40,48},{56,64},{72,80},{88,96},{104,112},{120,0},{... | collective-permute-start | bytes 1179656 | tf_op jit(solution)/shard_map/ppermute | solution.py:442
  15.0 14.6 %collective-permute-start.2 = (bf16[24,64,128]{2,1,0:T(8,128)(2,1)}, bf16[24,64,128]{2,1,0:T(8,128)(2,1)S(1)}, u32[]{:S(2)}, u32[]{:S(2)}) collective-permute-start(bf16[24,64,128]{2,1,0:T(8,128)(2,1)} %get-tuple-element.8.refs_2_), channel_id=1, source_target_pairs={{0,8},{16,24},{32,40},{48,56},{64,72},{80,88},{96,104},{112,120},{... | collective-permute-start | bytes 1179656 | tf_op jit(solution)/shard_map/ppermute | solution.py:442
  15.0 14.6 %collective-permute-start.1 = (bf16[24,64,128]{2,1,0:T(8,128)(2,1)}, bf16[24,64,128]{2,1,0:T(8,128)(2,1)S(1)}, u32[]{:S(2)}, u32[]{:S(2)}) collective-permute-start(bf16[24,64,128]{2,1,0:T(8,128)(2,1)} %get-tuple-element.8.refs_2_), channel_id=1, source_target_pairs={{1,2},{3,4},{5,6},{7,0},{2,1},{4,3},{6,5},{0,7},{9,10},{11,12},{13... | collective-permute-start | bytes 1179656 | tf_op jit(solution)/shard_map/ppermute | solution.py:442
  18.3 6.3 %collective-permute-start.9 = (bf16[256,128]{1,0:T(8,128)(2,1)S(1)}, bf16[256,128]{1,0:T(8,128)(2,1)S(1)}, u32[]{:S(2)}, u32[]{:S(2)}) collective-permute-start(bf16[256,128]{1,0:T(8,128)(2,1)S(1)} %get-tuple-element.11), channel_id=1, source_target_pairs={{1,0},{2,1},{3,2},{4,3},{5,4},{6,5},{7,6},{8,7},{9,8},{10,9},{11,1... | collective-permute-start | bytes 196616 | tf_op jit(solution)/shard_map/ppermute | solution.py:485
  21.9 4.9 %collective-permute-start.8 = (bf16[256,128]{1,0:T(8,128)(2,1)S(1)}, bf16[256,128]{1,0:T(8,128)(2,1)S(1)}, u32[]{:S(2)}, u32[]{:S(2)}) collective-permute-start(bf16[256,128]{1,0:T(8,128)(2,1)S(1)} %get-tuple-element.12), channel_id=1, source_target_pairs={{0,1},{1,2},{2,3},{3,4},{4,5},{5,6},{6,7},{7,8},{8,9},{9,10},{10,1... | collective-permute-start | bytes 196616 | tf_op jit(solution)/shard_map/ppermute | solution.py:484
  24.7 22.2 %collective-permute-start = (bf16[24,64,128]{2,1,0:T(8,128)(2,1)}, bf16[24,64,128]{2,1,0:T(8,128)(2,1)}, u32[]{:S(2)}, u32[]{:S(2)}) collective-permute-start(bf16[24,64,128]{2,1,0:T(8,128)(2,1)} %get-tuple-element.8.refs_2_), channel_id=1, source_target_pairs={{0,1},{2,3},{4,5},{6,7},{1,0},{3,2},{5,4},{7,6},{8,9},{10,11},{12,... | collective-permute-start | bytes 1179656 | tf_op jit(solution)/shard_map/ppermute | solution.py:442
  25.2 21.7 %collective-permute-start.7 = (bf16[24,64,128]{2,1,0:T(8,128)(2,1)S(1)}, bf16[24,64,128]{2,1,0:T(8,128)(2,1)}, u32[]{:S(2)}, u32[]{:S(2)}) collective-permute-start(bf16[24,64,128]{2,1,0:T(8,128)(2,1)S(1)} %collective-permute-done.5.refs_8_), channel_id=1, source_target_pairs={{1,2},{3,4},{5,6},{7,0},{2,1},{4,3},{6,5},{0,7},{9,10},{11,12},{13... | collective-permute-start | bytes 1179656 | tf_op jit(solution)/shard_map/ppermute | solution.py:442
  26.8 20.1 %collective-permute-start.6 = (bf16[24,64,128]{2,1,0:T(8,128)(2,1)S(1)}, bf16[24,64,128]{2,1,0:T(8,128)(2,1)}, u32[]{:S(2)}, u32[]{:S(2)}) collective-permute-start(bf16[24,64,128]{2,1,0:T(8,128)(2,1)S(1)} %collective-permute-done.5.refs_8_), channel_id=1, source_target_pairs={{0,1},{2,3},{4,5},{6,7},{1,0},{3,2},{5,4},{7,6},{8,9},{10,11},{12,... | collective-permute-start | bytes 1179656 | tf_op jit(solution)/shard_map/ppermute | solution.py:442
  29.5 17.3 %collective-permute-start.4 = (bf16[24,64,128]{2,1,0:T(8,128)(2,1)S(1)}, bf16[24,64,128]{2,1,0:T(8,128)(2,1)}, u32[]{:S(2)}, u32[]{:S(2)}) collective-permute-start(bf16[24,64,128]{2,1,0:T(8,128)(2,1)S(1)} %collective-permute-done.2.refs_5_), channel_id=1, source_target_pairs={{1,2},{3,4},{5,6},{7,0},{2,1},{4,3},{6,5},{0,7},{9,10},{11,12},{13... | collective-permute-start | bytes 1179656 | tf_op jit(solution)/shard_map/ppermute | solution.py:442
  29.5 17.4 %collective-permute-start.3 = (bf16[24,64,128]{2,1,0:T(8,128)(2,1)S(1)}, bf16[24,64,128]{2,1,0:T(8,128)(2,1)}, u32[]{:S(2)}, u32[]{:S(2)}) collective-permute-start(bf16[24,64,128]{2,1,0:T(8,128)(2,1)S(1)} %collective-permute-done.2.refs_5_), channel_id=1, source_target_pairs={{0,1},{2,3},{4,5},{6,7},{1,0},{3,2},{5,4},{7,6},{8,9},{10,11},{12,... | collective-permute-start | bytes 1179656 | tf_op jit(solution)/shard_map/ppermute | solution.py:442
  31.8 2.2 %copy-start.1 = (bf16[512,64,64]{0,2,1:T(8,128)(2,1)S(1)}, bf16[512,64,64]{0,2,1:T(8,128)(2,1)}, u32[]{:S(2)}) copy-start(bf16[512,64,64]{0,2,1:T(8,128)(2,1)} %param.16) | copy-start | bytes 12582916
  34.0 2.7 %copy-start.3 = (bf16[32,256,128]{2,1,0:T(8,128)(2,1)S(1)}, bf16[32,256,128]{2,1,0:T(8,128)(2,1)}, u32[]{:S(2)}) copy-start(bf16[32,256,128]{2,1,0:T(8,128)(2,1)} %get-tuple-element.10.ordered) | copy-start | bytes 6291460
  34.0 2.7 %copy-start.8 = (s32[128]{0:T(128)S(1)}, s32[128]{0:T(128)}, u32[]{:S(2)}) copy-start(s32[128]{0:T(128)} %targets.1) | copy-start | bytes 1540
  34.0 2.7 %copy-start.9 = (s32[128]{0:T(128)S(1)}, s32[128]{0:T(128)}, u32[]{:S(2)}) copy-start(s32[128]{0:T(128)} %sources.1) | copy-start | bytes 1540
  36.7 10.2 %copy-start.2 = (bf16[32,256,64]{1,2,0:T(8,128)(2,1)S(1)}, bf16[32,256,64]{1,2,0:T(8,128)(2,1)}, u32[]{:S(2)}) copy-start(bf16[32,256,64]{1,2,0:T(8,128)(2,1)} %param.14) | copy-start | bytes 3145732
  36.7 10.2 %copy-start.5 = (bf16[32,64,64]{2,1,0:T(8,128)(2,1)S(1)}, bf16[32,64,64]{2,1,0:T(8,128)(2,1)}, u32[]{:S(2)}) copy-start(bf16[32,64,64]{2,1,0:T(8,128)(2,1)} %refs_13_.1) | copy-start | bytes 786436
  36.7 10.2 %copy-start.6 = (bf16[24,64,128]{2,1,0:T(8,128)(2,1)S(1)}, bf16[24,64,128]{2,1,0:T(8,128)(2,1)}, u32[]{:S(2)}) copy-start(bf16[24,64,128]{2,1,0:T(8,128)(2,1)} %get-tuple-element.8.refs_2_) | copy-start | bytes 1179652
  36.7 10.2 %copy-start.7 = (s32[8192]{0:T(1024)S(1)}, s32[8192]{0:T(1024)}, u32[]{:S(2)}) copy-start(s32[8192]{0:T(1024)} %refs_0_.1) | copy-start | bytes 98308
  46.9 2.2 %copy-start = (f32[33,256,128]{2,1,0:T(8,128)S(1)}, f32[33,256,128]{2,1,0:T(8,128)}, u32[]{:S(2)}) copy-start(f32[33,256,128]{2,1,0:T(8,128)} %near_field.1.refs_15_) | copy-start | bytes 12976132

commit v3 on v2

--- a/solution.py
+++ b/solution.py
@@ -15,13 +15,14 @@
 TASKS = 128
 ROWS = LEAVES * POINTS
 PAIRS = LEAVES // 2 + PARENTS // 2
+EDGE = POINTS // RANK
 TASK_STEP = 16
 LEAF_STEP = 4
 CHUNK = 1024
 POINT_PARTS = 4
 OUT_PARTS = 8
 ORDER_MIB = 60
-NEAR_MIB = 48
+NEAR_MIB = 36
 HELD = 4
 PITCH = RANK // 2 + 1
 
@@ -41,6 +42,18 @@
 
 def swap_halves(x):
     return jnp.concatenate([x[:, 64:], x[:, :64]], axis=1)
+
+
+def places(lists, clusters, first):
+    outer, inner = lax.axis_size("gx"), lax.axis_size("gy")
+    gx, gy = lax.axis_index("gx"), lax.axis_index("gy")
+    owner = lax.div(lists, clusters)
+    step_x = lax.rem(lax.div(owner, inner) - gx + outer, outer)
+    step_y = lax.rem(lax.rem(owner, inner) - gy + inner, inner)
+    swap_x = jnp.where(step_x == 1, 1 + lax.rem(gx, 2), 2 - lax.rem(gx, 2))
+    swap_y = jnp.where(step_y == 1, 1 + lax.rem(gy, 2), 2 - lax.rem(gy, 2))
+    array = jnp.where(step_x == 0, 0, swap_x) * 3 + jnp.where(step_y == 0, 0, swap_y)
+    return array * (2 * PAIRS) + first + lax.rem(lists, clusters)
 
 
 def order_kernel(
@@ -48,9 +61,14 @@
     points,
     basis,
     transfer,
+    fine_lists,
+    coarse_lists,
     ordered,
     skeleton,
-    edges,
+    even_sent,
+    odd_edge,
+    fine_slots,
+    coarse_slots,
     table,
     even,
     odd,
@@ -133,11 +151,18 @@
     finish(chunks - 1, odd)
     send(chunks - 1).start()
 
+    fine_slots[...] = places(fine_lists[...], LEAVES, 0)
+    coarse_slots[...] = places(coarse_lists[...], PARENTS, LEAVES)
     transfers.wait()
     low = low_half(RANK)
     low_points = low_half(POINTS)
+
+    def put(n, block):
+        skeleton[n] = block
+        even_sent[n] = block
+
     for p in range(PARENTS):
-        skeleton[p] = jnp.where(low, fine[2 * p], fine[2 * p + 1])
+        put(p, jnp.where(low, fine[2 * p], fine[2 * p + 1]))
     for q in range(PARENTS // 2):
         coarse = []
         for p in (2 * q, 2 * q + 1):
@@ -148,28 +173,32 @@
                     pair, stacked, (((0,), (0,)), ((), ())), preferred_element_type=F32
                 ).astype(BF16)
             )
-        skeleton[PARENTS + q] = jnp.where(low, coarse[0], coarse[1])
-    edges[0] = jnp.where(low_points, ordered_here[0], ordered_here[1])
-    edges[1] = jnp.where(low_points, ordered_here[LEAVES - 2], ordered_here[LEAVES - 1])
+        put(PARENTS + q, jnp.where(low, coarse[0], coarse[1]))
+    odd_here = lax.rem(lax.axis_index("gy"), 2)
+    last = (1 - odd_here) * (LEAVES - 2)
+    edge = jnp.where(low_points, ordered_here[last], ordered_here[last + 1])
+    even_sent[PAIRS:] = edge.reshape(EDGE, RANK, 128)
+    last = odd_here * (LEAVES - 2)
+    odd_edge[...] = jnp.where(low_points, ordered_here[last], ordered_here[last + 1])
     for chunk in range(ROWS // CHUNK):
         send(chunk).wait()
 
 
-def order_points(points, perm, basis, transfer):
+def order_points(points, perm, basis, transfer, fine_lists, coarse_lists):
     anywhere = pl.BlockSpec(memory_space=pl.ANY)
+    vmem = pl.BlockSpec(memory_space=VMEM)
     return pl.pallas_call(
         order_kernel,
         out_shape=(
             jax.ShapeDtypeStruct((LEAVES, POINTS, 128), BF16),
             jax.ShapeDtypeStruct((PAIRS, RANK, 128), BF16),
-            jax.ShapeDtypeStruct((2, POINTS, 128), BF16),
+            jax.ShapeDtypeStruct((PAIRS + EDGE, RANK, 128), BF16),
+            jax.ShapeDtypeStruct((POINTS, 128), BF16),
+            jax.ShapeDtypeStruct(fine_lists.shape, jnp.int32),
+            jax.ShapeDtypeStruct(coarse_lists.shape, jnp.int32),
         ),
-        in_specs=[anywhere] * 4,
-        out_specs=(
-            pl.BlockSpec(memory_space=pl.ANY),
-            pl.BlockSpec(memory_space=VMEM),
-            pl.BlockSpec(memory_space=VMEM),
-        ),
+        in_specs=[anywhere] * 4 + [vmem] * 2,
+        out_specs=(anywhere,) + (vmem,) * 5,
         scratch_shapes=[
             pltpu.VMEM((ROWS, 128), F32),
             pltpu.VMEM((CHUNK, 128), F32),
@@ -186,7 +215,7 @@
         ],
         compiler_params=params(ORDER_MIB),
         name="order_points",
-    )(perm, points, basis, transfer)
+    )(perm, points, basis, transfer, fine_lists, coarse_lists)
 
 
 def turn_kernel(blocks, turned, table):
@@ -231,7 +260,7 @@
 
 
 def near_kernel(
-    targets, sources, count, before, after, ordered, blocks, total, window, held, sem, sems
+    targets, sources, count, even, odd, ordered, blocks, total, window, held, sem, sems
 ):
     steps = TASKS // TASK_STEP
 
@@ -245,7 +274,10 @@
     for step in range(HELD - 1):
         fetch(step).start()
     low = low_half(POINTS)
-    for pair, place in ((before[...], 0), (after[...], LEAVES + HALO)):
+    odd_here = lax.rem(lax.axis_index("gy"), 2)
+    from_even = even[PAIRS:].reshape(POINTS, 128)
+    after = LEAVES + HALO
+    for pair, place in ((from_even, (1 - odd_here) * after), (odd[...], odd_here * after)):
         swapped = swap_halves(pair)
         window[place] = jnp.where(low, pair, swapped)
         window[place + 1] = jnp.where(low, swapped, pair)
@@ -271,7 +303,7 @@
     lax.fori_loop(0, steps, one_step, 0)
 
 
-def near_field(targets, sources, count, before, after, ordered, blocks):
+def near_field(targets, sources, count, even, odd, ordered, blocks):
     return pl.pallas_call(
         near_kernel,
         out_shape=jax.ShapeDtypeStruct((LEAVES + 1, POINTS, 128), F32),
@@ -298,15 +330,17 @@
             transcendentals=0,
         ),
         name="near_field",
-    )(targets, sources, count, before, after, ordered, blocks)
+    )(targets, sources, count, even, odd, ordered, blocks)
 
 
 def result_kernel(*refs):
-    perm, slots = refs[:2]
-    skeletons = refs[2:11]
-    fine, coarse, transfer, basis, near, out = refs[11:17]
-    spread, below, above, first_rows, second_rows, table, wide = refs[17:24]
-    first_places, second_places, sems, out_sems = refs[24:]
+    perm, fine_slots, coarse_slots = refs[:3]
+    own, y_even, y_odd, x_even, x_odd, xy_even, xy_odd = refs[3:10]
+    fine, coarse, transfer, basis, near, out = refs[10:16]
+    spread, below, above, first_rows, second_rows, table, wide = refs[16:23]
+    first_places, second_places, sems, out_sems = refs[23:]
+    skeletons = [(own, 0), (y_even, 0), (y_odd, 0), (x_even, 0), (xy_even, 0), (xy_odd, 0)]
+    skeletons += [(x_odd, 0), (xy_even, PAIRS), (xy_odd, PAIRS)]
     steps = LEAVES // LEAF_STEP
 
     def load_places(step, into, sem):
@@ -316,26 +350,28 @@
     load_places(1, second_places, 1).start()
     low = low_half(RANK)
     keep = (low.astype(F32).astype(BF16), (~low).astype(F32).astype(BF16))
-    for a in range(9):
+    for a, (source, start) in enumerate(skeletons):
 
         def part(p, _):
             for z in range(2):
-                spread[a * 2 * PAIRS + 2 * p + z] = skeletons[a][p] * keep[z]
+                spread[a * 2 * PAIRS + 2 * p + z] = source[start + p] * keep[z]
             return 0
 
         lax.fori_loop(0, PAIRS, part, 0, unroll=8)
 
-    def coupled(matrix, first):
-        picked = [spread[slots[first + j]] for j in range(ENTRIES)]
+    def coupled(matrix, slots):
+        picked = [spread[slot] for slot in slots]
         return jnp.dot(matrix, jnp.concatenate(picked, axis=0), preferred_element_type=F32)
 
     def couple(step, _):
         for p in range(2):
             parent = step * 2 + p
-            above[parent] = coupled(coarse[parent], (LEAVES + parent) * ENTRIES)
+            above[parent] = coupled(
+                coarse[parent], [coarse_slots[parent, j] for j in range(ENTRIES)]
+            )
         for c in range(4):
             leaf = step * 4 + c
-            below[leaf] = coupled(fine[leaf], leaf * ENTRIES)
+            below[leaf] = coupled(fine[leaf], [fine_slots[j, leaf] for j in range(ENTRIES)])
         return 0
 
     lax.fori_loop(0, LEAVES // 4, couple, 0)
@@ -405,14 +441,14 @@
         send.wait()
 
 
-def result(perm, slots, skeletons, fine, coarse, transfer, basis, near):
+def result(perm, fine_slots, coarse_slots, skeletons, fine, coarse, transfer, basis, near):
     return pl.pallas_call(
         result_kernel,
         out_shape=jax.ShapeDtypeStruct((COLS, ROWS), F32),
         in_specs=[
             pl.BlockSpec(memory_space=pl.ANY),
-            pl.BlockSpec(memory_space=SMEM),
-            *[pl.BlockSpec(memory_space=VMEM)] * 14,
+            *[pl.BlockSpec(memory_space=SMEM)] * 2,
+            *[pl.BlockSpec(memory_space=VMEM)] * 12,
         ],
         out_specs=pl.BlockSpec(memory_space=pl.ANY),
         scratch_shapes=[
@@ -430,7 +466,7 @@
         ],
         compiler_params=params(36),
         name="result",
-    )(perm, slots, *skeletons, fine, coarse, transfer, basis, near)
+    )(perm, fine_slots, coarse_slots, *skeletons, fine, coarse, transfer, basis, near)
 
 
 def swaps(count, odd):
@@ -440,17 +476,6 @@
 
 def swap(x, axis, odd):
     return lax.ppermute(x, axis, swaps(lax.axis_size(axis), odd))
-
-
-def places(lists, clusters, first):
-    outer, inner = lax.axis_size("gx"), lax.axis_size("gy")
-    gx, gy = lax.axis_index("gx"), lax.axis_index("gy")
-    owner = lists // clusters
-    step_x = (owner // inner - gx + outer) % outer
-    step_y = (owner % inner - gy + inner) % inner
-    array_x = jnp.where(step_x == 0, 0, jnp.where((step_x == 1) == (gx % 2 == 0), 1, 2))
-    array_y = jnp.where(step_y == 0, 0, jnp.where((step_y == 1) == (gy % 2 == 0), 1, 2))
-    return (array_x * 3 + array_y) * (2 * PAIRS) + first + lists % clusters
 
 
 def on_device(
@@ -468,28 +493,26 @@
     task_count,
 ):
     basis_rows = basis.transpose(0, 2, 1)
-    slots = jnp.concatenate(
-        [
-            places(list_fine, LEAVES, 0).reshape(-1),
-            places(list_coarse, PARENTS, LEAVES).reshape(-1),
-        ]
+    ordered, own, even_sent, odd_edge, fine_slots, coarse_slots = order_points(
+        points_in.T, tree_perm, basis_rows, transfer, list_fine.T, list_coarse
     )
-    ordered, own, edges = order_points(points_in.T, tree_perm, basis_rows, transfer)
     x_even = swap(own, "gx", 0)
     x_odd = swap(own, "gx", 1)
-    y_even = swap(own, "gy", 0)
+    y_even = swap(even_sent, "gy", 0)
     y_odd = swap(own, "gy", 1)
     both = ("gx", "gy")
-    last = lax.axis_size(both) - 1
-    before = lax.ppermute(edges[1], both, [(i, i + 1) for i in range(last)])
-    after = lax.ppermute(edges[0], both, [(i + 1, i) for i in range(last)])
+    line = [(i, i + 1) for i in range(1, lax.axis_size(both) - 1, 2)]
+    odd_edge = lax.ppermute(odd_edge, both, line + [(b, a) for a, b in line])
     fine = turn_blocks(couple_fine.transpose(1, 2, 0))
     coarse = turn_blocks(couple_coarse.transpose(1, 2, 0))
-    near = near_field(near_target, near_source, task_count, before, after, ordered, near_blocks)
-    skeletons = [own, y_even, y_odd]
-    for x in (x_even, x_odd):
-        skeletons += [x, swap(x, "gy", 0), swap(x, "gy", 1)]
-    out = result(tree_perm, slots, skeletons, fine, coarse, transfer, basis_rows, near)
+    near = near_field(near_target, near_source, task_count, y_even, odd_edge, ordered, near_blocks)
+    x_both = jnp.concatenate([x_even, x_odd], axis=0)
+    xy_even = swap(x_both, "gy", 0)
+    xy_odd = swap(x_both, "gy", 1)
+    skeletons = (own, y_even, y_odd, x_even, x_odd, xy_even, xy_odd)
+    out = result(
+        tree_perm, fine_slots, coarse_slots, skeletons, fine, coarse, transfer, basis_rows, near
+    )
     return out.T
 
 

time: 62.4 us -> 64.3 us (1.030)
  waiting for transfers between devices: 0.03 us -> 14.7 us
  starting transfers between devices: 19.4 us -> 14.3 us
  local copies, waits for them, and re-layouts: 4.24 us -> 0.14 us
  Pallas kernels: 35.8 us -> 33.9 us
  other arithmetic: 1.48 us -> 0 us
    ppermute x8 -> x6, waiting for transfers between devices: 0.02 us -> 8.91 us  [swap(): return lax.ppermute(x, axis, swaps(lax.axis_size(axis), odd))]
    ppermute x2 -> x1, waiting for transfers between devices: 0.01 us -> 5.81 us  [on_device(): odd_edge = lax.ppermute(odd_edge, both, line + [(b, a) for a, b in line])]
    ppermute x2 -> x1, starting transfers between devices: 5.56 us -> 2.37 us  [on_device(): odd_edge = lax.ppermute(odd_edge, both, line + [(b, a) for a, b in line])]
    unnamed x20 -> x23, local copies, waits for them, and re-layouts: 3.12 us -> 0.09 us
    pallas_call x1, Pallas kernels: 10.1 us -> 8.07 us  [near_field(): pl.pallas_call(near_kernel, out_shape=jax.ShapeDtypeStruct((LEAVES + 1, P...]
    ppermute x8 -> x6, starting transfers between devices: 13.8 us -> 11.9 us  [swap(): return lax.ppermute(x, axis, swaps(lax.axis_size(axis), odd))]
    add x2 -> x0, other arithmetic: 1.47 us -> none  [places(): return (array_x * 3 + array_y) * (2 * PAIRS) + first + lists % clusters]
    squeeze x1 -> x0, local copies, waits for them, and re-layouts: 0.88 us -> none  [on_device(): after = lax.ppermute(edges[0], both, [(i + 1, i) for i in range(last)])]
  transfers between devices with their start and end apart: 10 -> 7, of which waited for: 0 -> 3; matrix products, arithmetic and copies ran while one was open for 4% -> 0% of each run, Pallas kernels for 23% -> 19%
where the time goes in v3:
time: 64.3 us; the launch traced here: 63.9 us
  Pallas kernels  33.9 us (53%)
  waiting for transfers between devices  14.7 us (23%)
  starting transfers between devices  14.3 us (22%)
  between operations  0.88 us (1%)
    pallas_call x1, Pallas kernels, result(): pl.pallas_call(result_kernel, out_shape=jax.ShapeDtypeStruct((COLS, ROWS)...  11.9 us
    ppermute x6, starting transfers between devices, swap(): return lax.ppermute(x, axis, swaps(lax.axis_size(axis), odd))  11.9 us
    pallas_call x1, Pallas kernels, order_points(): pl.pallas_call(order_kernel, out_shape=(jax.ShapeDtypeStruct((LEAVES, POI...  9.97 us
    ppermute x6, waiting for transfers between devices, swap(): return lax.ppermute(x, axis, swaps(lax.axis_size(axis), odd))  8.91 us
    pallas_call x1, Pallas kernels, near_field(): pl.pallas_call(near_kernel, out_shape=jax.ShapeDtypeStruct((LEAVES + 1, P...  8.07 us
    ppermute x1, waiting for transfers between devices, on_device(): odd_edge = lax.ppermute(odd_edge, both, line + [(b, a) for a, b in line])  5.81 us
    pallas_call x2, Pallas kernels, turn_blocks(): pl.pallas_call(turn_kernel, out_shape=jax.ShapeDtypeStruct((blocks.shape[...  3.94 us
    ppermute x1, starting transfers between devices, on_device(): odd_edge = lax.ppermute(odd_edge, both, line + [(b, a) for a, b in line])  2.37 us
  transfers between devices with their start and end apart: 7, of which 3 were waited for; matrix products, arithmetic and copies ran while one was open for 0% of the time, Pallas kernels for 19%

profile of v3, /device:TPU:1, one launch (start us, length us, event | category | flops | bytes accessed | tf_op | source)
XLA Modules:
  0.0 63.9 jit_solution(15604616613382287244)
XLA Ops:
  0.0 10.0 %order_points.1 = (bf16[32,256,128]{2,1,0:T(8,128)(2,1)}, bf16[24,64,128]{2,1,0:T(8,128)(2,1)}, bf16[28,64,128]{2,1,0:T(8,128)(2,1)}, bf16[256,128]{1,0:T(8,128)...) custom-call(s32[8192]{0:T(1024)} %refs_0_.1, bf16[64,8192]{1,0:T(8,128)(2,1)} %bitcast.10, bf16[32,64,256]{2,1,0:T(8,128)(2,1)} %bitcast.7, ...), custom_call_target="tpu_custom_call" | custom-call | tf_op jit(solution)/shard_map/order_points/pallas_call | solution.py:190
  10.0 0.0 copy-start
  10.0 2.1 %collective-permute-start.2 = (bf16[24,64,128]{2,1,0:T(8,128)(2,1)}, bf16[24,64,128]{2,1,0:T(8,128)(2,1)S(1)}, u32[]{:S(2)}, u32[]{:S(2)}) collective-permute-start(bf16[24,64,128]{2,1,0:T(8,128)(2,1)} %get-tuple-element.13.refs_3_), channel_id=1, source_target_pairs={{0,8},{16,24},{32,40},{48,56},{64,72},{80,88},{96,104},{112,120},{... | collective-permute-start | bytes 1179656 | tf_op jit(solution)/shard_map/ppermute | solution.py:478
  12.1 4.3 %collective-permute-start.3 = (bf16[24,64,128]{2,1,0:T(8,128)(2,1)}, bf16[24,64,128]{2,1,0:T(8,128)(2,1)S(1)}, u32[]{:S(2)}, u32[]{:S(2)}) collective-permute-start(bf16[24,64,128]{2,1,0:T(8,128)(2,1)} %get-tuple-element.13.refs_3_), channel_id=1, source_target_pairs={{8,16},{24,32},{40,48},{56,64},{72,80},{88,96},{104,112},{120,0},{... | collective-permute-start | bytes 1179656 | tf_op jit(solution)/shard_map/ppermute | solution.py:478
  16.4 4.3 %collective-permute-done.2.refs_6_ = bf16[24,64,128]{2,1,0:T(8,128)(2,1)S(1)} collective-permute-done((bf16[24,64,128]{2,1,0:T(8,128)(2,1)}, bf16[24,64,128]{2,1,0:T(8,128)(2,1)S(1)}, u32[]{:S(2)}, u32[]{:S(2)}) %collective-permute-start.2) | collective-permute-done | bytes 393248 | tf_op jit(solution)/shard_map/ppermute | solution.py:478
  20.7 4.6 %collective-permute-done.3.refs_7_ = bf16[24,64,128]{2,1,0:T(8,128)(2,1)S(1)} collective-permute-done((bf16[24,64,128]{2,1,0:T(8,128)(2,1)}, bf16[24,64,128]{2,1,0:T(8,128)(2,1)S(1)}, u32[]{:S(2)}, u32[]{:S(2)}) %collective-permute-start.3) | collective-permute-done | bytes 393248 | tf_op jit(solution)/shard_map/ppermute | solution.py:478
  25.3 0.1 constant_dynamic-update-slice_fusion
  25.4 3.5 %collective-permute-start.5 = (bf16[48,64,128]{2,1,0:T(8,128)(2,1)S(1)}, bf16[48,64,128]{2,1,0:T(8,128)(2,1)S(1)}, u32[]{:S(2)}, u32[]{:S(2)}) collective-permute-start(bf16[48,64,128]{2,1,0:T(8,128)(2,1)S(1)} %constant_dynamic-update-slice_fusion), channel_id=1, source_target_pairs={{1,2},{3,4},{5,6},{7,0},{2,1},{4,3},{6,5},{0,7},{9,10},{11,12},{13... | collective-permute-start | bytes 2359304 | tf_op jit(solution)/shard_map/ppermute | solution.py:478
  28.8 0.8 %collective-permute-start.4 = (bf16[48,64,128]{2,1,0:T(8,128)(2,1)S(1)}, bf16[48,64,128]{2,1,0:T(8,128)(2,1)S(1)}, u32[]{:S(2)}, u32[]{:S(2)}) collective-permute-start(bf16[48,64,128]{2,1,0:T(8,128)(2,1)S(1)} %constant_dynamic-update-slice_fusion), channel_id=1, source_target_pairs={{0,1},{2,3},{4,5},{6,7},{1,0},{3,2},{5,4},{7,6},{8,9},{10,11},{12,... | collective-permute-start | bytes 2359304 | tf_op jit(solution)/shard_map/ppermute | solution.py:478
  29.6 0.0 collective-permute-start
  29.6 1.3 %collective-permute-start.1 = (bf16[24,64,128]{2,1,0:T(8,128)(2,1)}, bf16[24,64,128]{2,1,0:T(8,128)(2,1)S(1)}, u32[]{:S(2)}, u32[]{:S(2)}) collective-permute-start(bf16[24,64,128]{2,1,0:T(8,128)(2,1)} %get-tuple-element.13.refs_3_), channel_id=1, source_target_pairs={{1,2},{3,4},{5,6},{7,0},{2,1},{4,3},{6,5},{0,7},{9,10},{11,12},{13... | collective-permute-start | bytes 1179656 | tf_op jit(solution)/shard_map/ppermute | solution.py:478
  30.9 2.4 %collective-permute-start.6 = (bf16[256,128]{1,0:T(8,128)(2,1)}, bf16[256,128]{1,0:T(8,128)(2,1)S(1)}, u32[]{:S(2)}, u32[]{:S(2)}) collective-permute-start(bf16[256,128]{1,0:T(8,128)(2,1)} %get-tuple-element.15), channel_id=1, source_target_pairs={{1,2},{3,4},{5,6},{7,8},{9,10},{11,12},{13,14},{15,16},{17,18},{19... | collective-permute-start | bytes 196616 | tf_op jit(solution)/shard_map/ppermute | solution.py:505
  33.9 0.0 copy-done.2
  33.9 1.3 %turn_blocks.3.refs_11_ = bf16[16,64,1024]{2,1,0:T(8,128)(2,1)S(1)} custom-call(bf16[64,64,256]{2,1,0:T(8,128)(2,1)S(1)} %bitcast.9), custom_call_target="tpu_custom_call" | custom-call | bytes 6291456 | tf_op jit(solution)/shard_map/turn_blocks/pallas_call | solution.py:248
  35.2 0.0 copy-done
  35.2 0.0 copy-start.4
  35.2 0.0 copy-start.9
  35.3 0.0 copy-start.10
  35.3 2.6 %turn_blocks.2.refs_10_ = bf16[32,64,1024]{2,1,0:T(8,128)(2,1)S(1)} custom-call(bf16[64,64,512]{2,1,0:T(8,128)(2,1)S(1)} %bitcast.6), custom_call_target="tpu_custom_call" | custom-call | bytes 12582912 | tf_op jit(solution)/shard_map/turn_blocks/pallas_call | solution.py:248
  37.9 5.8 %collective-permute-done.6.odd = bf16[256,128]{1,0:T(8,128)(2,1)S(1)} collective-permute-done((bf16[256,128]{1,0:T(8,128)(2,1)}, bf16[256,128]{1,0:T(8,128)(2,1)S(1)}, u32[]{:S(2)}, u32[]{:S(2)}) %collective-permute-start.6) | collective-permute-done | bytes 65568 | tf_op jit(solution)/shard_map/ppermute | solution.py:505
  43.7 0.0 collective-permute-done.even.refs_4_
  43.7 0.0 copy-done.9
  43.7 0.0 copy-start.1
  43.8 0.0 copy-start.3
  43.8 0.0 copy-start.6
  43.8 0.0 copy-start.7
  43.8 0.0 copy-start.8
  43.8 8.1 %near_field.1.refs_14_ = f32[33,256,128]{2,1,0:T(8,128)S(1)} custom-call(s32[128]{0:T(128)S(1)} %copy-done.9, s32[128]{0:T(128)S(1)} %copy-done.10, s32[1]{0:T(128)S(6)} %copy.14.count, bf16[28,64,128]{2,1,0:T(8,128)(2,1)S(1)} %collective-permute-done.even.refs_4_, bf16[256,128]{1,0:T(8,128)(2,1)S(1)} %collective-permute-done.6.odd, ...), custom_call_target="tpu_custom_call" | custom-call | flops 2147483648 | bytes 16777216 | tf_op jit(solution)/shard_map/near_field/pallas_call | solution.py:307
  51.9 0.0 collective-permute-done.1.refs_5_
  51.9 0.0 collective-permute-done.5.refs_9_
  51.9 0.0 collective-permute-done.4.refs_8_
  52.0 11.9 %result.1 = f32[64,8192]{1,0:T(8,128)} custom-call(s32[8192]{0:T(1024)S(1)} %copy-done.6, s32[16,32]{1,0:T(8,128)S(1)} %copy-done.7, s32[16,16]{1,0:T(8,128)S(1)} %copy-done.8, bf16[24,64,128]{2,1,0:T(8,128)(2,1)S(1)} %copy-done.5, bf16[28,64,128]{2,1,0:T(8,128)(2,1)S(1)} %collective-permute-done.even.refs_4_, ...), custom_call_target="tpu_custom_call" | custom-call | tf_op jit(solution)/shard_map/result/pallas_call | solution.py:445
  (11 shorter events, 0.0 us)
Async XLA Ops:
  0.0 33.9 %copy-start.2 = (bf16[256,64,64]{0,2,1:T(8,128)(2,1)S(1)}, bf16[256,64,64]{0,2,1:T(8,128)(2,1)}, u32[]{:S(2)}) copy-start(bf16[256,64,64]{0,2,1:T(8,128)(2,1)} %param.17) | copy-start | bytes 6291460
  10.0 25.2 %copy-start = (bf16[512,64,64]{0,2,1:T(8,128)(2,1)S(1)}, bf16[512,64,64]{0,2,1:T(8,128)(2,1)}, u32[]{:S(2)}) copy-start(bf16[512,64,64]{0,2,1:T(8,128)(2,1)} %param.16) | copy-start | bytes 12582916
  10.0 10.7 %collective-permute-start.2 = (bf16[24,64,128]{2,1,0:T(8,128)(2,1)}, bf16[24,64,128]{2,1,0:T(8,128)(2,1)S(1)}, u32[]{:S(2)}, u32[]{:S(2)}) collective-permute-start(bf16[24,64,128]{2,1,0:T(8,128)(2,1)} %get-tuple-element.13.refs_3_), channel_id=1, source_target_pairs={{0,8},{16,24},{32,40},{48,56},{64,72},{80,88},{96,104},{112,120},{... | collective-permute-start | bytes 1179656 | tf_op jit(solution)/shard_map/ppermute | solution.py:478
  12.1 13.2 %collective-permute-start.3 = (bf16[24,64,128]{2,1,0:T(8,128)(2,1)}, bf16[24,64,128]{2,1,0:T(8,128)(2,1)S(1)}, u32[]{:S(2)}, u32[]{:S(2)}) collective-permute-start(bf16[24,64,128]{2,1,0:T(8,128)(2,1)} %get-tuple-element.13.refs_3_), channel_id=1, source_target_pairs={{8,16},{24,32},{40,48},{56,64},{72,80},{88,96},{104,112},{120,0},{... | collective-permute-start | bytes 1179656 | tf_op jit(solution)/shard_map/ppermute | solution.py:478
  25.4 26.5 %collective-permute-start.5 = (bf16[48,64,128]{2,1,0:T(8,128)(2,1)S(1)}, bf16[48,64,128]{2,1,0:T(8,128)(2,1)S(1)}, u32[]{:S(2)}, u32[]{:S(2)}) collective-permute-start(bf16[48,64,128]{2,1,0:T(8,128)(2,1)S(1)} %constant_dynamic-update-slice_fusion), channel_id=1, source_target_pairs={{1,2},{3,4},{5,6},{7,0},{2,1},{4,3},{6,5},{0,7},{9,10},{11,12},{13... | collective-permute-start | bytes 2359304 | tf_op jit(solution)/shard_map/ppermute | solution.py:478
  28.8 23.1 %collective-permute-start.4 = (bf16[48,64,128]{2,1,0:T(8,128)(2,1)S(1)}, bf16[48,64,128]{2,1,0:T(8,128)(2,1)S(1)}, u32[]{:S(2)}, u32[]{:S(2)}) collective-permute-start(bf16[48,64,128]{2,1,0:T(8,128)(2,1)S(1)} %constant_dynamic-update-slice_fusion), channel_id=1, source_target_pairs={{0,1},{2,3},{4,5},{6,7},{1,0},{3,2},{5,4},{7,6},{8,9},{10,11},{12,... | collective-permute-start | bytes 2359304 | tf_op jit(solution)/shard_map/ppermute | solution.py:478
  29.6 14.1 %collective-permute-start = (bf16[28,64,128]{2,1,0:T(8,128)(2,1)}, bf16[28,64,128]{2,1,0:T(8,128)(2,1)S(1)}, u32[]{:S(2)}, u32[]{:S(2)}) collective-permute-start(bf16[28,64,128]{2,1,0:T(8,128)(2,1)} %get-tuple-element.14), channel_id=1, source_target_pairs={{0,1},{2,3},{4,5},{6,7},{1,0},{3,2},{5,4},{7,6},{8,9},{10,11},{12,... | collective-permute-start | bytes 1376264 | tf_op jit(solution)/shard_map/ppermute | solution.py:478
  29.6 22.3 %collective-permute-start.1 = (bf16[24,64,128]{2,1,0:T(8,128)(2,1)}, bf16[24,64,128]{2,1,0:T(8,128)(2,1)S(1)}, u32[]{:S(2)}, u32[]{:S(2)}) collective-permute-start(bf16[24,64,128]{2,1,0:T(8,128)(2,1)} %get-tuple-element.13.refs_3_), channel_id=1, source_target_pairs={{1,2},{3,4},{5,6},{7,0},{2,1},{4,3},{6,5},{0,7},{9,10},{11,12},{13... | collective-permute-start | bytes 1179656 | tf_op jit(solution)/shard_map/ppermute | solution.py:478
  30.9 12.9 %collective-permute-start.6 = (bf16[256,128]{1,0:T(8,128)(2,1)}, bf16[256,128]{1,0:T(8,128)(2,1)S(1)}, u32[]{:S(2)}, u32[]{:S(2)}) collective-permute-start(bf16[256,128]{1,0:T(8,128)(2,1)} %get-tuple-element.15), channel_id=1, source_target_pairs={{1,2},{3,4},{5,6},{7,8},{9,10},{11,12},{13,14},{15,16},{17,18},{19... | collective-permute-start | bytes 196616 | tf_op jit(solution)/shard_map/ppermute | solution.py:505
  35.2 8.5 %copy-start.4 = (bf16[32,256,128]{2,1,0:T(8,128)(2,1)S(1)}, bf16[32,256,128]{2,1,0:T(8,128)(2,1)}, u32[]{:S(2)}) copy-start(bf16[32,256,128]{2,1,0:T(8,128)(2,1)} %get-tuple-element.16.ordered) | copy-start | bytes 6291460
  35.2 8.5 %copy-start.9 = (s32[128]{0:T(128)S(1)}, s32[128]{0:T(128)}, u32[]{:S(2)}) copy-start(s32[128]{0:T(128)} %targets.1) | copy-start | bytes 1540
  35.3 8.5 %copy-start.10 = (s32[128]{0:T(128)S(1)}, s32[128]{0:T(128)}, u32[]{:S(2)}) copy-start(s32[128]{0:T(128)} %sources.1) | copy-start | bytes 1540
  43.7 8.2 %copy-start.1 = (bf16[32,256,64]{1,2,0:T(8,128)(2,1)S(1)}, bf16[32,256,64]{1,2,0:T(8,128)(2,1)}, u32[]{:S(2)}) copy-start(bf16[32,256,64]{1,2,0:T(8,128)(2,1)} %param.14) | copy-start | bytes 3145732
  43.8 8.2 %copy-start.3 = (bf16[32,64,64]{2,1,0:T(8,128)(2,1)S(1)}, bf16[32,64,64]{2,1,0:T(8,128)(2,1)}, u32[]{:S(2)}) copy-start(bf16[32,64,64]{2,1,0:T(8,128)(2,1)} %refs_12_.1) | copy-start | bytes 786436
  43.8 8.2 %copy-start.5 = (bf16[24,64,128]{2,1,0:T(8,128)(2,1)S(1)}, bf16[24,64,128]{2,1,0:T(8,128)(2,1)}, u32[]{:S(2)}) copy-start(bf16[24,64,128]{2,1,0:T(8,128)(2,1)} %get-tuple-element.13.refs_3_) | copy-start | bytes 1179652
  43.8 8.2 %copy-start.6 = (s32[8192]{0:T(1024)S(1)}, s32[8192]{0:T(1024)}, u32[]{:S(2)}) copy-start(s32[8192]{0:T(1024)} %refs_0_.1) | copy-start | bytes 98308
  43.8 8.2 %copy-start.7 = (s32[16,32]{1,0:T(8,128)S(1)}, s32[16,32]{1,0:T(8,128)}, u32[]{:S(2)}) copy-start(s32[16,32]{1,0:T(8,128)} %get-tuple-element.11.refs_1_) | copy-start | bytes 6148
  43.8 8.2 %copy-start.8 = (s32[16,16]{1,0:T(8,128)S(1)}, s32[16,16]{1,0:T(8,128)}, u32[]{:S(2)}) copy-start(s32[16,16]{1,0:T(8,128)} %get-tuple-element.12.refs_2_) | copy-start | bytes 3076

commit v4 on v3

--- a/solution.py
+++ b/solution.py
@@ -47,13 +47,13 @@
 def places(lists, clusters, first):
     outer, inner = lax.axis_size("gx"), lax.axis_size("gy")
     gx, gy = lax.axis_index("gx"), lax.axis_index("gy")
-    owner = lax.div(lists, clusters)
-    step_x = lax.rem(lax.div(owner, inner) - gx + outer, outer)
-    step_y = lax.rem(lax.rem(owner, inner) - gy + inner, inner)
-    swap_x = jnp.where(step_x == 1, 1 + lax.rem(gx, 2), 2 - lax.rem(gx, 2))
-    swap_y = jnp.where(step_y == 1, 1 + lax.rem(gy, 2), 2 - lax.rem(gy, 2))
+    owner = lists >> (clusters.bit_length() - 1)
+    step_x = ((owner >> (inner.bit_length() - 1)) - gx) & (outer - 1)
+    step_y = (owner - gy) & (inner - 1)
+    swap_x = jnp.where(step_x == 1, 1 + (gx & 1), 2 - (gx & 1))
+    swap_y = jnp.where(step_y == 1, 1 + (gy & 1), 2 - (gy & 1))
     array = jnp.where(step_x == 0, 0, swap_x) * 3 + jnp.where(step_y == 0, 0, swap_y)
-    return array * (2 * PAIRS) + first + lax.rem(lists, clusters)
+    return array * (2 * PAIRS) + first + (lists & (clusters - 1))
 
 
 def order_kernel(
@@ -469,6 +469,31 @@
     )(perm, fine_slots, coarse_slots, *skeletons, fine, coarse, transfer, basis, near)
 
 
+def join_kernel(first, second, *refs):
+    joined, sems = refs[-2:]
+    copies = [
+        pltpu.make_async_copy(x, joined.at[pl.ds(n * PAIRS, PAIRS)], sems.at[n])
+        for n, x in enumerate((first, second))
+    ]
+    for copy in copies:
+        copy.start()
+    for copy in copies:
+        copy.wait()
+
+
+def join(first, second, *earlier):
+    anywhere = pl.BlockSpec(memory_space=pl.ANY)
+    return pl.pallas_call(
+        join_kernel,
+        out_shape=jax.ShapeDtypeStruct((2 * PAIRS, RANK, 128), BF16),
+        in_specs=[anywhere] * (2 + len(earlier)),
+        out_specs=anywhere,
+        scratch_shapes=[pltpu.SemaphoreType.DMA((2,))],
+        compiler_params=params(1),
+        name="join",
+    )(first, second, *earlier)
+
+
 def swaps(count, odd):
     pairs = [((i + odd) % count, (i + odd + 1) % count) for i in range(0, count, 2)]
     return [(a, b) for a, b in pairs] + [(b, a) for a, b in pairs]
@@ -506,7 +531,7 @@
     fine = turn_blocks(couple_fine.transpose(1, 2, 0))
     coarse = turn_blocks(couple_coarse.transpose(1, 2, 0))
     near = near_field(near_target, near_source, task_count, y_even, odd_edge, ordered, near_blocks)
-    x_both = jnp.concatenate([x_even, x_odd], axis=0)
+    x_both = join(x_even, x_odd, y_even, y_odd, odd_edge, fine, coarse)
     xy_even = swap(x_both, "gy", 0)
     xy_odd = swap(x_both, "gy", 1)
     skeletons = (own, y_even, y_odd, x_even, x_odd, xy_even, xy_odd)

time: 64.3 us -> 55 us (0.86)
  the two profiles are of different devices: /device:TPU:1 before, /device:TPU:2 now
where the time goes in v4:
time: 55 us; the launch traced here: 54.6 us
  Pallas kernels  34 us (62%)
  starting transfers between devices  11.5 us (21%)
  waiting for transfers between devices  6.54 us (12%)
  local copies, waits for them, and re-layouts  1.64 us (3%)
  between operations  0.89 us (2%)
    pallas_call x1, Pallas kernels, result(): pl.pallas_call(result_kernel, out_shape=jax.ShapeDtypeStruct((COLS, ROWS)...  11.8 us
    pallas_call x1, Pallas kernels, order_points(): pl.pallas_call(order_kernel, out_shape=(jax.ShapeDtypeStruct((LEAVES, POI...  9.82 us
    ppermute x6, starting transfers between devices, swap(): return lax.ppermute(x, axis, swaps(lax.axis_size(axis), odd))  9.59 us
    pallas_call x1, Pallas kernels, near_field(): pl.pallas_call(near_kernel, out_shape=jax.ShapeDtypeStruct((LEAVES + 1, P...  8.06 us
    pallas_call x2, Pallas kernels, turn_blocks(): pl.pallas_call(turn_kernel, out_shape=jax.ShapeDtypeStruct((blocks.shape[...  3.94 us
    ppermute x6, waiting for transfers between devices, swap(): return lax.ppermute(x, axis, swaps(lax.axis_size(axis), odd))  3.72 us
    ppermute x1, waiting for transfers between devices, on_device(): odd_edge = lax.ppermute(odd_edge, both, line + [(b, a) for a, b in line])  2.82 us
    ppermute x1, starting transfers between devices, on_device(): odd_edge = lax.ppermute(odd_edge, both, line + [(b, a) for a, b in line])  1.91 us
  transfers between devices with their start and end apart: 7, of which 2 were waited for; matrix products, arithmetic and copies ran while one was open for 0% of the time, Pallas kernels for 22%

profile of v4, /device:TPU:2, one launch (start us, length us, event | category | flops | bytes accessed | tf_op | source)
XLA Modules:
  0.0 54.6 jit_solution(15675551103534035107)
XLA Ops:
  0.0 9.8 %order_points.1 = (bf16[32,256,128]{2,1,0:T(8,128)(2,1)}, bf16[24,64,128]{2,1,0:T(8,128)(2,1)}, bf16[28,64,128]{2,1,0:T(8,128)(2,1)}, bf16[256,128]{1,0:T(8,128)...) custom-call(s32[8192]{0:T(1024)} %refs_0_.1, bf16[64,8192]{1,0:T(8,128)(2,1)} %bitcast.10, bf16[32,64,256]{2,1,0:T(8,128)(2,1)} %bitcast.7, ...), custom_call_target="tpu_custom_call" | custom-call | tf_op jit(solution)/shard_map/order_points/pallas_call | solution.py:190
  9.8 0.0 copy-start
  9.8 0.1 collective-permute-start
  9.9 1.6 %collective-permute-start.3 = (bf16[24,64,128]{2,1,0:T(8,128)(2,1)}, bf16[24,64,128]{2,1,0:T(8,128)(2,1)S(1)}, u32[]{:S(2)}, u32[]{:S(2)}) collective-permute-start(bf16[24,64,128]{2,1,0:T(8,128)(2,1)} %get-tuple-element.13.refs_3_), channel_id=1, source_target_pairs={{8,16},{24,32},{40,48},{56,64},{72,80},{88,96},{104,112},{120,0},{... | collective-permute-start | bytes 1179656 | tf_op jit(solution)/shard_map/ppermute | solution.py:503
  11.5 4.2 %collective-permute-start.2 = (bf16[24,64,128]{2,1,0:T(8,128)(2,1)}, bf16[24,64,128]{2,1,0:T(8,128)(2,1)S(1)}, u32[]{:S(2)}, u32[]{:S(2)}) collective-permute-start(bf16[24,64,128]{2,1,0:T(8,128)(2,1)} %get-tuple-element.13.refs_3_), channel_id=1, source_target_pairs={{0,8},{16,24},{32,40},{48,56},{64,72},{80,88},{96,104},{112,120},{... | collective-permute-start | bytes 1179656 | tf_op jit(solution)/shard_map/ppermute | solution.py:503
  15.8 3.5 %collective-permute-start.1 = (bf16[24,64,128]{2,1,0:T(8,128)(2,1)}, bf16[24,64,128]{2,1,0:T(8,128)(2,1)S(1)}, u32[]{:S(2)}, u32[]{:S(2)}) collective-permute-start(bf16[24,64,128]{2,1,0:T(8,128)(2,1)} %get-tuple-element.13.refs_3_), channel_id=1, source_target_pairs={{1,2},{3,4},{5,6},{7,0},{2,1},{4,3},{6,5},{0,7},{9,10},{11,12},{13... | collective-permute-start | bytes 1179656 | tf_op jit(solution)/shard_map/ppermute | solution.py:503
  19.3 1.9 %collective-permute-start.4 = (bf16[256,128]{1,0:T(8,128)(2,1)}, bf16[256,128]{1,0:T(8,128)(2,1)S(1)}, u32[]{:S(2)}, u32[]{:S(2)}) collective-permute-start(bf16[256,128]{1,0:T(8,128)(2,1)} %get-tuple-element.15), channel_id=1, source_target_pairs={{1,2},{3,4},{5,6},{7,8},{9,10},{11,12},{13,14},{15,16},{17,18},{19... | collective-permute-start | bytes 196616 | tf_op jit(solution)/shard_map/ppermute | solution.py:530
  21.2 0.0 copy-start.2
  21.2 1.6 %copy-done.2 = bf16[256,64,64]{0,2,1:T(8,128)(2,1)S(1)} copy-done((bf16[256,64,64]{0,2,1:T(8,128)(2,1)S(1)}, bf16[256,64,64]{0,2,1:T(8,128)(2,1)}, u32[]{:S(2)}) %copy-start.2) | copy-done | bytes 2097176
  22.8 1.3 %turn_blocks.3.refs_4_.refs_11_ = bf16[16,64,1024]{2,1,0:T(8,128)(2,1)S(1)} custom-call(bf16[64,64,256]{2,1,0:T(8,128)(2,1)S(1)} %bitcast.9), custom_call_target="tpu_custom_call" | custom-call | bytes 6291456 | tf_op jit(solution)/shard_map/turn_blocks/pallas_call | solution.py:248
  24.1 0.0 copy-done
  24.1 2.6 %turn_blocks.2.refs_3_.refs_10_ = bf16[32,64,1024]{2,1,0:T(8,128)(2,1)S(1)} custom-call(bf16[64,64,512]{2,1,0:T(8,128)(2,1)S(1)} %bitcast.6), custom_call_target="tpu_custom_call" | custom-call | bytes 12582912 | tf_op jit(solution)/shard_map/turn_blocks/pallas_call | solution.py:248
  26.7 0.0 copy-start.4
  26.8 0.0 copy-start.9
  26.8 0.0 copy-start.10
  26.8 2.8 %collective-permute-done.4.refs_2_.odd = bf16[256,128]{1,0:T(8,128)(2,1)S(1)} collective-permute-done((bf16[256,128]{1,0:T(8,128)(2,1)}, bf16[256,128]{1,0:T(8,128)(2,1)S(1)}, u32[]{:S(2)}, u32[]{:S(2)}) %collective-permute-start.4) | collective-permute-done | bytes 65568 | tf_op jit(solution)/shard_map/ppermute | solution.py:530
  29.6 0.0 collective-permute-done.3.second.refs_7_
  29.6 0.0 collective-permute-done.2.first.refs_6_
  29.6 0.0 collective-permute-done.1.refs_1_.refs_5_
  29.6 0.0 collective-permute-done.refs_0_.even.refs_4_
  29.6 0.4 join.1
  30.0 0.1 collective-permute-start.6
  30.1 0.1 collective-permute-start.5
  30.9 0.0 copy-start.1
  30.9 0.0 copy-start.3
  30.9 0.0 copy-start.6
  30.9 0.0 copy-start.7
  31.0 0.0 copy-start.8
  31.0 8.1 %near_field.1.refs_14_ = f32[33,256,128]{2,1,0:T(8,128)S(1)} custom-call(s32[128]{0:T(128)S(1)} %copy-done.9, s32[128]{0:T(128)S(1)} %copy-done.10, s32[1]{0:T(128)S(6)} %copy.13.count, bf16[28,64,128]{2,1,0:T(8,128)(2,1)S(1)} %collective-permute-done.refs_0_.even.refs_4_, bf16[256,128]{1,0:T(8,128)(2,1)S(1)} %collective-permute-done.4.refs_2_.odd, ...), custom_call_target="tpu_custom_call" | custom-call | flops 2147483648 | bytes 16777216 | tf_op jit(solution)/shard_map/near_field/pallas_call | solution.py:307
  39.0 3.7 %collective-permute-done.6.refs_9_ = bf16[48,64,128]{2,1,0:T(8,128)(2,1)S(1)} collective-permute-done((bf16[48,64,128]{2,1,0:T(8,128)(2,1)S(1)}, bf16[48,64,128]{2,1,0:T(8,128)(2,1)S(1)}, u32[]{:S(2)}, u32[]{:S(2)}) %collective-permute-start.6) | collective-permute-done | bytes 786464 | tf_op jit(solution)/shard_map/ppermute | solution.py:503
  42.7 0.0 collective-permute-done.5.refs_8_
  42.8 11.8 %result.1 = f32[64,8192]{1,0:T(8,128)} custom-call(s32[8192]{0:T(1024)S(1)} %copy-done.6, s32[16,32]{1,0:T(8,128)S(1)} %copy-done.7, s32[16,16]{1,0:T(8,128)S(1)} %copy-done.8, bf16[24,64,128]{2,1,0:T(8,128)(2,1)S(1)} %copy-done.5, bf16[28,64,128]{2,1,0:T(8,128)(2,1)S(1)} %collective-permute-done.refs_0_.even.refs_4_, ...), custom_call_target="tpu_custom_call" | custom-call | tf_op jit(solution)/shard_map/result/pallas_call | solution.py:445
  (10 shorter events, 0.0 us)
Async XLA Ops:
  9.8 14.3 %copy-start = (bf16[512,64,64]{0,2,1:T(8,128)(2,1)S(1)}, bf16[512,64,64]{0,2,1:T(8,128)(2,1)}, u32[]{:S(2)}) copy-start(bf16[512,64,64]{0,2,1:T(8,128)(2,1)} %param.16) | copy-start | bytes 12582916
  9.8 19.8 %collective-permute-start = (bf16[28,64,128]{2,1,0:T(8,128)(2,1)}, bf16[28,64,128]{2,1,0:T(8,128)(2,1)S(1)}, u32[]{:S(2)}, u32[]{:S(2)}) collective-permute-start(bf16[28,64,128]{2,1,0:T(8,128)(2,1)} %get-tuple-element.14), channel_id=1, source_target_pairs={{0,1},{2,3},{4,5},{6,7},{1,0},{3,2},{5,4},{7,6},{8,9},{10,11},{12,... | collective-permute-start | bytes 1376264 | tf_op jit(solution)/shard_map/ppermute | solution.py:503
  9.9 19.7 %collective-permute-start.3 = (bf16[24,64,128]{2,1,0:T(8,128)(2,1)}, bf16[24,64,128]{2,1,0:T(8,128)(2,1)S(1)}, u32[]{:S(2)}, u32[]{:S(2)}) collective-permute-start(bf16[24,64,128]{2,1,0:T(8,128)(2,1)} %get-tuple-element.13.refs_3_), channel_id=1, source_target_pairs={{8,16},{24,32},{40,48},{56,64},{72,80},{88,96},{104,112},{120,0},{... | collective-permute-start | bytes 1179656 | tf_op jit(solution)/shard_map/ppermute | solution.py:503
  11.5 18.1 %collective-permute-start.2 = (bf16[24,64,128]{2,1,0:T(8,128)(2,1)}, bf16[24,64,128]{2,1,0:T(8,128)(2,1)S(1)}, u32[]{:S(2)}, u32[]{:S(2)}) collective-permute-start(bf16[24,64,128]{2,1,0:T(8,128)(2,1)} %get-tuple-element.13.refs_3_), channel_id=1, source_target_pairs={{0,8},{16,24},{32,40},{48,56},{64,72},{80,88},{96,104},{112,120},{... | collective-permute-start | bytes 1179656 | tf_op jit(solution)/shard_map/ppermute | solution.py:503
  15.8 13.9 %collective-permute-start.1 = (bf16[24,64,128]{2,1,0:T(8,128)(2,1)}, bf16[24,64,128]{2,1,0:T(8,128)(2,1)S(1)}, u32[]{:S(2)}, u32[]{:S(2)}) collective-permute-start(bf16[24,64,128]{2,1,0:T(8,128)(2,1)} %get-tuple-element.13.refs_3_), channel_id=1, source_target_pairs={{1,2},{3,4},{5,6},{7,0},{2,1},{4,3},{6,5},{0,7},{9,10},{11,12},{13... | collective-permute-start | bytes 1179656 | tf_op jit(solution)/shard_map/ppermute | solution.py:503
  19.3 10.3 %collective-permute-start.4 = (bf16[256,128]{1,0:T(8,128)(2,1)}, bf16[256,128]{1,0:T(8,128)(2,1)S(1)}, u32[]{:S(2)}, u32[]{:S(2)}) collective-permute-start(bf16[256,128]{1,0:T(8,128)(2,1)} %get-tuple-element.15), channel_id=1, source_target_pairs={{1,2},{3,4},{5,6},{7,8},{9,10},{11,12},{13,14},{15,16},{17,18},{19... | collective-permute-start | bytes 196616 | tf_op jit(solution)/shard_map/ppermute | solution.py:530
  21.2 1.6 %copy-start.2 = (bf16[256,64,64]{0,2,1:T(8,128)(2,1)S(1)}, bf16[256,64,64]{0,2,1:T(8,128)(2,1)}, u32[]{:S(2)}) copy-start(bf16[256,64,64]{0,2,1:T(8,128)(2,1)} %param.17) | copy-start | bytes 6291460
  26.7 4.1 %copy-start.4 = (bf16[32,256,128]{2,1,0:T(8,128)(2,1)S(1)}, bf16[32,256,128]{2,1,0:T(8,128)(2,1)}, u32[]{:S(2)}) copy-start(bf16[32,256,128]{2,1,0:T(8,128)(2,1)} %get-tuple-element.16.ordered) | copy-start | bytes 6291460
  26.8 4.1 %copy-start.9 = (s32[128]{0:T(128)S(1)}, s32[128]{0:T(128)}, u32[]{:S(2)}) copy-start(s32[128]{0:T(128)} %targets.1) | copy-start | bytes 1540
  26.8 4.1 %copy-start.10 = (s32[128]{0:T(128)S(1)}, s32[128]{0:T(128)}, u32[]{:S(2)}) copy-start(s32[128]{0:T(128)} %sources.1) | copy-start | bytes 1540
  30.0 12.7 %collective-permute-start.6 = (bf16[48,64,128]{2,1,0:T(8,128)(2,1)S(1)}, bf16[48,64,128]{2,1,0:T(8,128)(2,1)S(1)}, u32[]{:S(2)}, u32[]{:S(2)}) collective-permute-start(bf16[48,64,128]{2,1,0:T(8,128)(2,1)S(1)} %join.1), channel_id=1, source_target_pairs={{1,2},{3,4},{5,6},{7,0},{2,1},{4,3},{6,5},{0,7},{9,10},{11,12},{13... | collective-permute-start | bytes 2359304 | tf_op jit(solution)/shard_map/ppermute | solution.py:503
  30.1 12.6 %collective-permute-start.5 = (bf16[48,64,128]{2,1,0:T(8,128)(2,1)S(1)}, bf16[48,64,128]{2,1,0:T(8,128)(2,1)S(1)}, u32[]{:S(2)}, u32[]{:S(2)}) collective-permute-start(bf16[48,64,128]{2,1,0:T(8,128)(2,1)S(1)} %join.1), channel_id=1, source_target_pairs={{0,1},{2,3},{4,5},{6,7},{1,0},{3,2},{5,4},{7,6},{8,9},{10,11},{12,... | collective-permute-start | bytes 2359304 | tf_op jit(solution)/shard_map/ppermute | solution.py:503
  30.9 11.8 %copy-start.1 = (bf16[32,256,64]{1,2,0:T(8,128)(2,1)S(1)}, bf16[32,256,64]{1,2,0:T(8,128)(2,1)}, u32[]{:S(2)}) copy-start(bf16[32,256,64]{1,2,0:T(8,128)(2,1)} %param.14) | copy-start | bytes 3145732
  30.9 11.8 %copy-start.3 = (bf16[32,64,64]{2,1,0:T(8,128)(2,1)S(1)}, bf16[32,64,64]{2,1,0:T(8,128)(2,1)}, u32[]{:S(2)}) copy-start(bf16[32,64,64]{2,1,0:T(8,128)(2,1)} %refs_12_.1) | copy-start | bytes 786436
  30.9 11.8 %copy-start.5 = (bf16[24,64,128]{2,1,0:T(8,128)(2,1)S(1)}, bf16[24,64,128]{2,1,0:T(8,128)(2,1)}, u32[]{:S(2)}) copy-start(bf16[24,64,128]{2,1,0:T(8,128)(2,1)} %get-tuple-element.13.refs_3_) | copy-start | bytes 1179652
  30.9 11.8 %copy-start.6 = (s32[8192]{0:T(1024)S(1)}, s32[8192]{0:T(1024)}, u32[]{:S(2)}) copy-start(s32[8192]{0:T(1024)} %refs_0_.1) | copy-start | bytes 98308
  30.9 11.8 %copy-start.7 = (s32[16,32]{1,0:T(8,128)S(1)}, s32[16,32]{1,0:T(8,128)}, u32[]{:S(2)}) copy-start(s32[16,32]{1,0:T(8,128)} %get-tuple-element.11.refs_1_) | copy-start | bytes 6148
  31.0 11.8 %copy-start.8 = (s32[16,16]{1,0:T(8,128)S(1)}, s32[16,16]{1,0:T(8,128)}, u32[]{:S(2)}) copy-start(s32[16,16]{1,0:T(8,128)} %get-tuple-element.12.refs_2_) | copy-start | bytes 3076

commit v5 on v4

--- a/solution.py
+++ b/solution.py
@@ -15,7 +15,6 @@
 TASKS = 128
 ROWS = LEAVES * POINTS
 PAIRS = LEAVES // 2 + PARENTS // 2
-EDGE = POINTS // RANK
 TASK_STEP = 16
 LEAF_STEP = 4
 CHUNK = 1024
@@ -65,7 +64,7 @@
     coarse_lists,
     ordered,
     skeleton,
-    even_sent,
+    even_edge,
     odd_edge,
     fine_slots,
     coarse_slots,
@@ -157,12 +156,8 @@
     low = low_half(RANK)
     low_points = low_half(POINTS)
 
-    def put(n, block):
-        skeleton[n] = block
-        even_sent[n] = block
-
     for p in range(PARENTS):
-        put(p, jnp.where(low, fine[2 * p], fine[2 * p + 1]))
+        skeleton[p] = jnp.where(low, fine[2 * p], fine[2 * p + 1])
     for q in range(PARENTS // 2):
         coarse = []
         for p in (2 * q, 2 * q + 1):
@@ -173,11 +168,10 @@
                     pair, stacked, (((0,), (0,)), ((), ())), preferred_element_type=F32
                 ).astype(BF16)
             )
-        put(PARENTS + q, jnp.where(low, coarse[0], coarse[1]))
+        skeleton[PARENTS + q] = jnp.where(low, coarse[0], coarse[1])
     odd_here = lax.rem(lax.axis_index("gy"), 2)
     last = (1 - odd_here) * (LEAVES - 2)
-    edge = jnp.where(low_points, ordered_here[last], ordered_here[last + 1])
-    even_sent[PAIRS:] = edge.reshape(EDGE, RANK, 128)
+    even_edge[...] = jnp.where(low_points, ordered_here[last], ordered_here[last + 1])
     last = odd_here * (LEAVES - 2)
     odd_edge[...] = jnp.where(low_points, ordered_here[last], ordered_here[last + 1])
     for chunk in range(ROWS // CHUNK):
@@ -192,7 +186,7 @@
         out_shape=(
             jax.ShapeDtypeStruct((LEAVES, POINTS, 128), BF16),
             jax.ShapeDtypeStruct((PAIRS, RANK, 128), BF16),
-            jax.ShapeDtypeStruct((PAIRS + EDGE, RANK, 128), BF16),
+            jax.ShapeDtypeStruct((POINTS, 128), BF16),
             jax.ShapeDtypeStruct((POINTS, 128), BF16),
             jax.ShapeDtypeStruct(fine_lists.shape, jnp.int32),
             jax.ShapeDtypeStruct(coarse_lists.shape, jnp.int32),
@@ -275,9 +269,8 @@
         fetch(step).start()
     low = low_half(POINTS)
     odd_here = lax.rem(lax.axis_index("gy"), 2)
-    from_even = even[PAIRS:].reshape(POINTS, 128)
     after = LEAVES + HALO
-    for pair, place in ((from_even, (1 - odd_here) * after), (odd[...], odd_here * after)):
+    for pair, place in ((even[...], (1 - odd_here) * after), (odd[...], odd_here * after)):
         swapped = swap_halves(pair)
         window[place] = jnp.where(low, pair, swapped)
         window[place + 1] = jnp.where(low, swapped, pair)
@@ -364,17 +357,17 @@
         return jnp.dot(matrix, jnp.concatenate(picked, axis=0), preferred_element_type=F32)
 
     def couple(step, _):
-        for p in range(2):
-            parent = step * 2 + p
+        for p in range(4):
+            parent = step * 4 + p
             above[parent] = coupled(
                 coarse[parent], [coarse_slots[parent, j] for j in range(ENTRIES)]
             )
-        for c in range(4):
-            leaf = step * 4 + c
+        for c in range(8):
+            leaf = step * 8 + c
             below[leaf] = coupled(fine[leaf], [fine_slots[j, leaf] for j in range(ENTRIES)])
         return 0
 
-    lax.fori_loop(0, LEAVES // 4, couple, 0)
+    lax.fori_loop(0, LEAVES // 8, couple, 0)
 
     def fold(halves):
         return halves + pltpu.roll(halves, 64, 1)
@@ -518,20 +511,21 @@
     task_count,
 ):
     basis_rows = basis.transpose(0, 2, 1)
-    ordered, own, even_sent, odd_edge, fine_slots, coarse_slots = order_points(
+    ordered, own, even_edge, odd_edge, fine_slots, coarse_slots = order_points(
         points_in.T, tree_perm, basis_rows, transfer, list_fine.T, list_coarse
     )
     x_even = swap(own, "gx", 0)
     x_odd = swap(own, "gx", 1)
-    y_even = swap(even_sent, "gy", 0)
+    y_even = swap(own, "gy", 0)
+    even_edge = swap(even_edge, "gy", 0)
     y_odd = swap(own, "gy", 1)
     both = ("gx", "gy")
     line = [(i, i + 1) for i in range(1, lax.axis_size(both) - 1, 2)]
     odd_edge = lax.ppermute(odd_edge, both, line + [(b, a) for a, b in line])
     fine = turn_blocks(couple_fine.transpose(1, 2, 0))
     coarse = turn_blocks(couple_coarse.transpose(1, 2, 0))
-    near = near_field(near_target, near_source, task_count, y_even, odd_edge, ordered, near_blocks)
-    x_both = join(x_even, x_odd, y_even, y_odd, odd_edge, fine, coarse)
+    near = near_field(near_target, near_source, task_count, even_edge, odd_edge, ordered, near_blocks)
+    x_both = join(x_even, x_odd, y_even, y_odd, even_edge, odd_edge, fine, coarse)
     xy_even = swap(x_both, "gy", 0)
     xy_odd = swap(x_both, "gy", 1)
     skeletons = (own, y_even, y_odd, x_even, x_odd, xy_even, xy_odd)

time: 55 us -> 54.5 us (level)
  the two profiles are of different devices: /device:TPU:2 before, /device:TPU:1 now
where the time goes in v5:
time: 54.5 us; the launch traced here: 54 us
  Pallas kernels  33.3 us (61%)
  starting transfers between devices  16.5 us (30%)
  waiting for transfers between devices  1.67 us (3%)
  local copies, waits for them, and re-layouts  1.64 us (3%)
  between operations  0.93 us (2%)
    ppermute x7, starting transfers between devices, swap(): return lax.ppermute(x, axis, swaps(lax.axis_size(axis), odd))  14.2 us
    pallas_call x1, Pallas kernels, result(): pl.pallas_call(result_kernel, out_shape=jax.ShapeDtypeStruct((COLS, ROWS)...  11.2 us
    pallas_call x1, Pallas kernels, order_points(): pl.pallas_call(order_kernel, out_shape=(jax.ShapeDtypeStruct((LEAVES, POI...  9.69 us
    pallas_call x1, Pallas kernels, near_field(): pl.pallas_call(near_kernel, out_shape=jax.ShapeDtypeStruct((LEAVES + 1, P...  8.06 us
    pallas_call x2, Pallas kernels, turn_blocks(): pl.pallas_call(turn_kernel, out_shape=jax.ShapeDtypeStruct((blocks.shape[...  3.94 us
    ppermute x1, starting transfers between devices, on_device(): odd_edge = lax.ppermute(odd_edge, both, line + [(b, a) for a, b in line])  2.25 us
    ppermute x7, waiting for transfers between devices, swap(): return lax.ppermute(x, axis, swaps(lax.axis_size(axis), odd))  1.67 us
    unnamed x22, local copies, waits for them, and re-layouts  1.64 us
  transfers between devices with their start and end apart: 8, of which 1 were waited for; matrix products, arithmetic and copies ran while one was open for 0% of the time, Pallas kernels for 22%

profile of v5, /device:TPU:1, one launch (start us, length us, event | category | flops | bytes accessed | tf_op | source)
XLA Modules:
  0.0 54.0 jit_solution(8685503394150303444)
XLA Ops:
  0.0 9.7 %order_points.1 = (bf16[32,256,128]{2,1,0:T(8,128)(2,1)}, bf16[24,64,128]{2,1,0:T(8,128)(2,1)}, bf16[256,128]{1,0:T(8,128)(2,1)}, bf16[256,128]{1,0:T(8,128)(2,1)}, s32[16,32]{1,0:T(8,128)}, /*index=5*/s32[16,16]{1,0:T(8,128)}) custom-call(s32[8192]{0:T(1024)} %refs_0_.1, bf16[64,8192]{1,0:T(8,128)(2,1)} %bitcast.10, bf16[32,64,256]{2,1,0:T(8,128)(2,1)} %bitcast.7, ...), custom_call_target="tpu_custom_call" | custom-call | tf_op jit(solution)/shard_map/order_points/pallas_call | solution.py:184
  9.7 0.0 copy-start
  9.7 5.8 %collective-permute-start.3 = (bf16[24,64,128]{2,1,0:T(8,128)(2,1)}, bf16[24,64,128]{2,1,0:T(8,128)(2,1)S(1)}, u32[]{:S(2)}, u32[]{:S(2)}) collective-permute-start(bf16[24,64,128]{2,1,0:T(8,128)(2,1)} %get-tuple-element.13.refs_3_), channel_id=1, source_target_pairs={{8,16},{24,32},{40,48},{56,64},{72,80},{88,96},{104,112},{120,0},{... | collective-permute-start | bytes 1179656 | tf_op jit(solution)/shard_map/ppermute | solution.py:496
  15.5 0.0 collective-permute-start.2
  15.5 2.5 %collective-permute-start.1 = (bf16[24,64,128]{2,1,0:T(8,128)(2,1)}, bf16[24,64,128]{2,1,0:T(8,128)(2,1)S(1)}, u32[]{:S(2)}, u32[]{:S(2)}) collective-permute-start(bf16[24,64,128]{2,1,0:T(8,128)(2,1)} %get-tuple-element.13.refs_3_), channel_id=1, source_target_pairs={{1,2},{3,4},{5,6},{7,0},{2,1},{4,3},{6,5},{0,7},{9,10},{11,12},{13... | collective-permute-start | bytes 1179656 | tf_op jit(solution)/shard_map/ppermute | solution.py:496
  18.0 1.7 %collective-permute-start = (bf16[24,64,128]{2,1,0:T(8,128)(2,1)}, bf16[24,64,128]{2,1,0:T(8,128)(2,1)S(1)}, u32[]{:S(2)}, u32[]{:S(2)}) collective-permute-start(bf16[24,64,128]{2,1,0:T(8,128)(2,1)} %get-tuple-element.13.refs_3_), channel_id=1, source_target_pairs={{0,1},{2,3},{4,5},{6,7},{1,0},{3,2},{5,4},{7,6},{8,9},{10,11},{12,... | collective-permute-start | bytes 1179656 | tf_op jit(solution)/shard_map/ppermute | solution.py:496
  19.7 0.0 collective-permute-start.4
  19.7 1.7 %collective-permute-done.4.refs_2_.even = bf16[256,128]{1,0:T(8,128)(2,1)S(1)} collective-permute-done((bf16[256,128]{1,0:T(8,128)(2,1)}, bf16[256,128]{1,0:T(8,128)(2,1)S(1)}, u32[]{:S(2)}, u32[]{:S(2)}) %collective-permute-start.4) | collective-permute-done | bytes 65568 | tf_op jit(solution)/shard_map/ppermute | solution.py:496
  21.4 2.3 %collective-permute-start.5 = (bf16[256,128]{1,0:T(8,128)(2,1)}, bf16[256,128]{1,0:T(8,128)(2,1)S(1)}, u32[]{:S(2)}, u32[]{:S(2)}) collective-permute-start(bf16[256,128]{1,0:T(8,128)(2,1)} %get-tuple-element.15), channel_id=1, source_target_pairs={{1,2},{3,4},{5,6},{7,8},{9,10},{11,12},{13,14},{15,16},{17,18},{19... | collective-permute-start | bytes 196616 | tf_op jit(solution)/shard_map/ppermute | solution.py:524
  23.6 0.0 copy-start.3
  23.6 1.6 %copy-done.3 = bf16[256,64,64]{0,2,1:T(8,128)(2,1)S(1)} copy-done((bf16[256,64,64]{0,2,1:T(8,128)(2,1)S(1)}, bf16[256,64,64]{0,2,1:T(8,128)(2,1)}, u32[]{:S(2)}) %copy-start.3) | copy-done | bytes 2097176
  25.2 1.3 %turn_blocks.3.refs_5_.refs_11_ = bf16[16,64,1024]{2,1,0:T(8,128)(2,1)S(1)} custom-call(bf16[64,64,256]{2,1,0:T(8,128)(2,1)S(1)} %bitcast.9), custom_call_target="tpu_custom_call" | custom-call | bytes 6291456 | tf_op jit(solution)/shard_map/turn_blocks/pallas_call | solution.py:242
  26.5 2.6 %turn_blocks.2.refs_4_.refs_10_ = bf16[32,64,1024]{2,1,0:T(8,128)(2,1)S(1)} custom-call(bf16[64,64,512]{2,1,0:T(8,128)(2,1)S(1)} %bitcast.6), custom_call_target="tpu_custom_call" | custom-call | bytes 12582912 | tf_op jit(solution)/shard_map/turn_blocks/pallas_call | solution.py:242
  29.2 0.0 copy-start.2
  29.2 0.0 copy-start.9
  29.2 0.0 copy-start.10
  29.2 0.0 collective-permute-done.5.refs_3_.odd
  29.2 0.0 collective-permute-done.3.second.refs_7_
  29.2 0.0 collective-permute-done.2.first.refs_6_
  29.2 0.0 collective-permute-done.1.refs_1_.refs_5_
  29.3 0.0 collective-permute-done.refs_0_.refs_4_
  29.3 0.4 join.1
  29.7 1.5 %collective-permute-start.7 = (bf16[48,64,128]{2,1,0:T(8,128)(2,1)S(1)}, bf16[48,64,128]{2,1,0:T(8,128)(2,1)S(1)}, u32[]{:S(2)}, u32[]{:S(2)}) collective-permute-start(bf16[48,64,128]{2,1,0:T(8,128)(2,1)S(1)} %join.1), channel_id=1, source_target_pairs={{1,2},{3,4},{5,6},{7,0},{2,1},{4,3},{6,5},{0,7},{9,10},{11,12},{13... | collective-permute-start | bytes 2359304 | tf_op jit(solution)/shard_map/ppermute | solution.py:496
  31.1 2.8 %collective-permute-start.6 = (bf16[48,64,128]{2,1,0:T(8,128)(2,1)S(1)}, bf16[48,64,128]{2,1,0:T(8,128)(2,1)S(1)}, u32[]{:S(2)}, u32[]{:S(2)}) collective-permute-start(bf16[48,64,128]{2,1,0:T(8,128)(2,1)S(1)} %join.1), channel_id=1, source_target_pairs={{0,1},{2,3},{4,5},{6,7},{1,0},{3,2},{5,4},{7,6},{8,9},{10,11},{12,... | collective-permute-start | bytes 2359304 | tf_op jit(solution)/shard_map/ppermute | solution.py:496
  34.5 0.0 copy-done.2
  34.6 0.0 copy-start.1
  34.6 0.0 copy-start.4
  34.6 0.0 copy-start.6
  34.6 8.1 %near_field.1.refs_14_ = f32[33,256,128]{2,1,0:T(8,128)S(1)} custom-call(s32[128]{0:T(128)S(1)} %copy-done.9, s32[128]{0:T(128)S(1)} %copy-done.10, s32[1]{0:T(128)S(6)} %copy.13.count, bf16[256,128]{1,0:T(8,128)(2,1)S(1)} %collective-permute-done.4.refs_2_.even, bf16[256,128]{1,0:T(8,128)(2,1)S(1)} %collective-permute-done.5.refs_3_.odd, ...), custom_call_target="tpu_custom_call" | custom-call | flops 2147483648 | bytes 16777216 | tf_op jit(solution)/shard_map/near_field/pallas_call | solution.py:300
  42.7 0.0 collective-permute-done.7.refs_9_
  42.7 0.0 collective-permute-done.6.refs_8_
  42.8 11.2 %result.1 = f32[64,8192]{1,0:T(8,128)} custom-call(s32[8192]{0:T(1024)S(1)} %copy-done.6, s32[16,32]{1,0:T(8,128)S(1)} %copy-done.7, s32[16,16]{1,0:T(8,128)S(1)} %copy-done.8, bf16[24,64,128]{2,1,0:T(8,128)(2,1)S(1)} %copy-done.5, bf16[24,64,128]{2,1,0:T(8,128)(2,1)S(1)} %collective-permute-done.refs_0_.refs_4_, ...), custom_call_target="tpu_custom_call" | custom-call | tf_op jit(solution)/shard_map/result/pallas_call | solution.py:438
  (12 shorter events, 0.0 us)
Async XLA Ops:
  9.7 16.8 %copy-start = (bf16[512,64,64]{0,2,1:T(8,128)(2,1)S(1)}, bf16[512,64,64]{0,2,1:T(8,128)(2,1)}, u32[]{:S(2)}) copy-start(bf16[512,64,64]{0,2,1:T(8,128)(2,1)} %param.16) | copy-start | bytes 12582916
  9.7 19.5 %collective-permute-start.3 = (bf16[24,64,128]{2,1,0:T(8,128)(2,1)}, bf16[24,64,128]{2,1,0:T(8,128)(2,1)S(1)}, u32[]{:S(2)}, u32[]{:S(2)}) collective-permute-start(bf16[24,64,128]{2,1,0:T(8,128)(2,1)} %get-tuple-element.13.refs_3_), channel_id=1, source_target_pairs={{8,16},{24,32},{40,48},{56,64},{72,80},{88,96},{104,112},{120,0},{... | collective-permute-start | bytes 1179656 | tf_op jit(solution)/shard_map/ppermute | solution.py:496
  15.5 13.7 %collective-permute-start.2 = (bf16[24,64,128]{2,1,0:T(8,128)(2,1)}, bf16[24,64,128]{2,1,0:T(8,128)(2,1)S(1)}, u32[]{:S(2)}, u32[]{:S(2)}) collective-permute-start(bf16[24,64,128]{2,1,0:T(8,128)(2,1)} %get-tuple-element.13.refs_3_), channel_id=1, source_target_pairs={{0,8},{16,24},{32,40},{48,56},{64,72},{80,88},{96,104},{112,120},{... | collective-permute-start | bytes 1179656 | tf_op jit(solution)/shard_map/ppermute | solution.py:496
  15.5 13.7 %collective-permute-start.1 = (bf16[24,64,128]{2,1,0:T(8,128)(2,1)}, bf16[24,64,128]{2,1,0:T(8,128)(2,1)S(1)}, u32[]{:S(2)}, u32[]{:S(2)}) collective-permute-start(bf16[24,64,128]{2,1,0:T(8,128)(2,1)} %get-tuple-element.13.refs_3_), channel_id=1, source_target_pairs={{1,2},{3,4},{5,6},{7,0},{2,1},{4,3},{6,5},{0,7},{9,10},{11,12},{13... | collective-permute-start | bytes 1179656 | tf_op jit(solution)/shard_map/ppermute | solution.py:496
  18.0 11.2 %collective-permute-start = (bf16[24,64,128]{2,1,0:T(8,128)(2,1)}, bf16[24,64,128]{2,1,0:T(8,128)(2,1)S(1)}, u32[]{:S(2)}, u32[]{:S(2)}) collective-permute-start(bf16[24,64,128]{2,1,0:T(8,128)(2,1)} %get-tuple-element.13.refs_3_), channel_id=1, source_target_pairs={{0,1},{2,3},{4,5},{6,7},{1,0},{3,2},{5,4},{7,6},{8,9},{10,11},{12,... | collective-permute-start | bytes 1179656 | tf_op jit(solution)/shard_map/ppermute | solution.py:496
  19.7 1.7 %collective-permute-start.4 = (bf16[256,128]{1,0:T(8,128)(2,1)}, bf16[256,128]{1,0:T(8,128)(2,1)S(1)}, u32[]{:S(2)}, u32[]{:S(2)}) collective-permute-start(bf16[256,128]{1,0:T(8,128)(2,1)} %get-tuple-element.14), channel_id=1, source_target_pairs={{0,1},{2,3},{4,5},{6,7},{1,0},{3,2},{5,4},{7,6},{8,9},{10,11},{12,... | collective-permute-start | bytes 196616 | tf_op jit(solution)/shard_map/ppermute | solution.py:496
  21.4 7.9 %collective-permute-start.5 = (bf16[256,128]{1,0:T(8,128)(2,1)}, bf16[256,128]{1,0:T(8,128)(2,1)S(1)}, u32[]{:S(2)}, u32[]{:S(2)}) collective-permute-start(bf16[256,128]{1,0:T(8,128)(2,1)} %get-tuple-element.15), channel_id=1, source_target_pairs={{1,2},{3,4},{5,6},{7,8},{9,10},{11,12},{13,14},{15,16},{17,18},{19... | collective-permute-start | bytes 196616 | tf_op jit(solution)/shard_map/ppermute | solution.py:524
  23.6 1.6 %copy-start.3 = (bf16[256,64,64]{0,2,1:T(8,128)(2,1)S(1)}, bf16[256,64,64]{0,2,1:T(8,128)(2,1)}, u32[]{:S(2)}) copy-start(bf16[256,64,64]{0,2,1:T(8,128)(2,1)} %param.17) | copy-start | bytes 6291460
  29.2 5.4 %copy-start.2 = (bf16[32,256,128]{2,1,0:T(8,128)(2,1)S(1)}, bf16[32,256,128]{2,1,0:T(8,128)(2,1)}, u32[]{:S(2)}) copy-start(bf16[32,256,128]{2,1,0:T(8,128)(2,1)} %get-tuple-element.16.ordered) | copy-start | bytes 6291460
  29.2 5.4 %copy-start.9 = (s32[128]{0:T(128)S(1)}, s32[128]{0:T(128)}, u32[]{:S(2)}) copy-start(s32[128]{0:T(128)} %targets.1) | copy-start | bytes 1540
  29.2 5.4 %copy-start.10 = (s32[128]{0:T(128)S(1)}, s32[128]{0:T(128)}, u32[]{:S(2)}) copy-start(s32[128]{0:T(128)} %sources.1) | copy-start | bytes 1540
  29.7 13.0 %collective-permute-start.7 = (bf16[48,64,128]{2,1,0:T(8,128)(2,1)S(1)}, bf16[48,64,128]{2,1,0:T(8,128)(2,1)S(1)}, u32[]{:S(2)}, u32[]{:S(2)}) collective-permute-start(bf16[48,64,128]{2,1,0:T(8,128)(2,1)S(1)} %join.1), channel_id=1, source_target_pairs={{1,2},{3,4},{5,6},{7,0},{2,1},{4,3},{6,5},{0,7},{9,10},{11,12},{13... | collective-permute-start | bytes 2359304 | tf_op jit(solution)/shard_map/ppermute | solution.py:496
  31.1 11.6 %collective-permute-start.6 = (bf16[48,64,128]{2,1,0:T(8,128)(2,1)S(1)}, bf16[48,64,128]{2,1,0:T(8,128)(2,1)S(1)}, u32[]{:S(2)}, u32[]{:S(2)}) collective-permute-start(bf16[48,64,128]{2,1,0:T(8,128)(2,1)S(1)} %join.1), channel_id=1, source_target_pairs={{0,1},{2,3},{4,5},{6,7},{1,0},{3,2},{5,4},{7,6},{8,9},{10,11},{12,... | collective-permute-start | bytes 2359304 | tf_op jit(solution)/shard_map/ppermute | solution.py:496
  34.6 8.2 %copy-start.1 = (bf16[32,256,64]{1,2,0:T(8,128)(2,1)S(1)}, bf16[32,256,64]{1,2,0:T(8,128)(2,1)}, u32[]{:S(2)}) copy-start(bf16[32,256,64]{1,2,0:T(8,128)(2,1)} %param.14) | copy-start | bytes 3145732
  34.6 8.2 %copy-start.4 = (bf16[32,64,64]{2,1,0:T(8,128)(2,1)S(1)}, bf16[32,64,64]{2,1,0:T(8,128)(2,1)}, u32[]{:S(2)}) copy-start(bf16[32,64,64]{2,1,0:T(8,128)(2,1)} %refs_12_.1) | copy-start | bytes 786436
  34.6 8.2 %copy-start.5 = (bf16[24,64,128]{2,1,0:T(8,128)(2,1)S(1)}, bf16[24,64,128]{2,1,0:T(8,128)(2,1)}, u32[]{:S(2)}) copy-start(bf16[24,64,128]{2,1,0:T(8,128)(2,1)} %get-tuple-element.13.refs_3_) | copy-start | bytes 1179652
  34.6 8.2 %copy-start.6 = (s32[8192]{0:T(1024)S(1)}, s32[8192]{0:T(1024)}, u32[]{:S(2)}) copy-start(s32[8192]{0:T(1024)} %refs_0_.1) | copy-start | bytes 98308
  34.6 8.2 %copy-start.7 = (s32[16,32]{1,0:T(8,128)S(1)}, s32[16,32]{1,0:T(8,128)}, u32[]{:S(2)}) copy-start(s32[16,32]{1,0:T(8,128)} %get-tuple-element.11.refs_1_) | copy-start | bytes 6148
  34.6 8.2 %copy-start.8 = (s32[16,16]{1,0:T(8,128)S(1)}, s32[16,16]{1,0:T(8,128)}, u32[]{:S(2)}) copy-start(s32[16,16]{1,0:T(8,128)} %get-tuple-element.12.refs_2_) | copy-start | bytes 3076

commit v6 on v4

--- a/solution.py
+++ b/solution.py
@@ -73,8 +73,10 @@
     even,
     odd,
     fine,
-    first_rows,
-    second_rows,
+    places_0,
+    places_1,
+    places_2,
+    places_3,
     points_here,
     basis_here,
     transfer_here,
@@ -95,12 +97,14 @@
 
     for n in range(POINT_PARTS):
         part(n).start()
-    load_rows(0, first_rows, 0).start()
-    load_rows(1, second_rows, 1).start()
-    bases = pltpu.make_async_copy(basis, basis_here, sems.at[POINT_PARTS + 2])
-    transfers = pltpu.make_async_copy(transfer, transfer_here, sems.at[POINT_PARTS + 3])
+    held = (places_0, places_1, places_2, places_3)
+    for n, into in enumerate(held):
+        load_rows(n, into, n).start()
+    bases = pltpu.make_async_copy(basis, basis_here, sems.at[POINT_PARTS + 4])
+    transfers = pltpu.make_async_copy(transfer, transfer_here, sems.at[POINT_PARTS + 5])
     bases.start()
     transfers.start()
+    odd[...] = jnp.zeros_like(odd)
     for n in range(POINT_PARTS):
         part(n).wait()
         for c in range(n * width // 128, (n + 1) * width // 128):
@@ -126,28 +130,26 @@
         return pltpu.make_async_copy(ordered_here.at[span], ordered.at[span], out_sems.at[chunk])
 
     chunks = ROWS // CHUNK
-    load_rows(0, first_rows, 0).wait()
-    gather(first_rows, even)
-
-    def two_chunks(step, _):
-        load_rows(2 * step + 1, second_rows, 1).wait()
-        load_rows(2 * step + 2, first_rows, 0).start()
-        finish(2 * step, even)
-        gather(second_rows, odd)
-        send(2 * step).start()
-
-        load_rows(2 * step + 3, second_rows, 1).start()
-        load_rows(2 * step + 2, first_rows, 0).wait()
-        finish(2 * step + 1, odd)
-        gather(first_rows, even)
-        send(2 * step + 1).start()
+    rounds = chunks // len(held)
+
+    def one_round(step, _):
+        for n, rows in enumerate(held):
+            chunk = step * len(held) + n
+            load_rows(chunk, rows, n).wait()
+            finish(jnp.maximum(chunk - 1, 0), (odd, even)[n % 2])
+            gather(rows, (even, odd)[n % 2])
+
+            @pl.when(step < rounds - 1)
+            def _():
+                load_rows(chunk + len(held), rows, n).start()
+
+            @pl.when(chunk > 0)
+            def _():
+                send(chunk - 1).start()
+
         return 0
 
-    lax.fori_loop(0, chunks // 2 - 1, two_chunks, 0)
-    load_rows(chunks - 1, second_rows, 1).wait()
-    finish(chunks - 2, even)
-    gather(second_rows, odd)
-    send(chunks - 2).start()
+    lax.fori_loop(0, rounds, one_round, 0)
     finish(chunks - 1, odd)
     send(chunks - 1).start()
 
@@ -204,13 +206,12 @@
             pltpu.VMEM((CHUNK, 128), F32),
             pltpu.VMEM((CHUNK, 128), F32),
             pltpu.VMEM((LEAVES, RANK, 128), BF16),
-            pltpu.SMEM((CHUNK,), jnp.int32),
-            pltpu.SMEM((CHUNK,), jnp.int32),
+            *[pltpu.SMEM((CHUNK,), jnp.int32)] * 4,
             pltpu.VMEM((COLS, ROWS), BF16),
             pltpu.VMEM((LEAVES, RANK, POINTS), BF16),
             pltpu.VMEM((LEAVES, RANK, RANK), BF16),
             pltpu.VMEM((LEAVES, POINTS, 128), BF16),
-            pltpu.SemaphoreType.DMA((POINT_PARTS + 4,)),
+            pltpu.SemaphoreType.DMA((POINT_PARTS + 6,)),
             pltpu.SemaphoreType.DMA((ROWS // CHUNK,)),
         ],
         compiler_params=params(ORDER_MIB),
@@ -364,17 +365,17 @@
         return jnp.dot(matrix, jnp.concatenate(picked, axis=0), preferred_element_type=F32)
 
     def couple(step, _):
-        for p in range(2):
-            parent = step * 2 + p
+        for p in range(4):
+            parent = step * 4 + p
             above[parent] = coupled(
                 coarse[parent], [coarse_slots[parent, j] for j in range(ENTRIES)]
             )
-        for c in range(4):
-            leaf = step * 4 + c
+        for c in range(8):
+            leaf = step * 8 + c
             below[leaf] = coupled(fine[leaf], [fine_slots[j, leaf] for j in range(ENTRIES)])
         return 0
 
-    lax.fori_loop(0, LEAVES // 4, couple, 0)
+    lax.fori_loop(0, LEAVES // 8, couple, 0)
 
     def fold(halves):
         return halves + pltpu.roll(halves, 64, 1)

time: 55 us -> 54 us (0.982)
  Pallas kernels: 34 us -> 33.2 us
    pallas_call x1, Pallas kernels: 11.8 us -> 11.2 us  [result(): pl.pallas_call(result_kernel, out_shape=jax.ShapeDtypeStruct((COLS, ROWS)...]
where the time goes in v6:
time: 54 us; the launch traced here: 53.8 us
  Pallas kernels  33.2 us (61%)
  starting transfers between devices  11.5 us (21%)
  waiting for transfers between devices  6.54 us (12%)
  local copies, waits for them, and re-layouts  1.64 us (3%)
  between operations  0.89 us (2%)
    pallas_call x1, Pallas kernels, result(): pl.pallas_call(result_kernel, out_shape=jax.ShapeDtypeStruct((COLS, ROWS)...  11.2 us
    pallas_call x1, Pallas kernels, order_points(): pl.pallas_call(order_kernel, out_shape=(jax.ShapeDtypeStruct((LEAVES, POI...  9.62 us
    ppermute x6, starting transfers between devices, swap(): return lax.ppermute(x, axis, swaps(lax.axis_size(axis), odd))  9.59 us
    pallas_call x1, Pallas kernels, near_field(): pl.pallas_call(near_kernel, out_shape=jax.ShapeDtypeStruct((LEAVES + 1, P...  8.06 us
    pallas_call x2, Pallas kernels, turn_blocks(): pl.pallas_call(turn_kernel, out_shape=jax.ShapeDtypeStruct((blocks.shape[...  3.94 us
    ppermute x6, waiting for transfers between devices, swap(): return lax.ppermute(x, axis, swaps(lax.axis_size(axis), odd))  3.72 us
    ppermute x1, waiting for transfers between devices, on_device(): odd_edge = lax.ppermute(odd_edge, both, line + [(b, a) for a, b in line])  2.82 us
    ppermute x1, starting transfers between devices, on_device(): odd_edge = lax.ppermute(odd_edge, both, line + [(b, a) for a, b in line])  1.91 us
  transfers between devices with their start and end apart: 7, of which 2 were waited for; matrix products, arithmetic and copies ran while one was open for 0% of the time, Pallas kernels for 22%

profile of v6, /device:TPU:2, one launch (start us, length us, event | category | flops | bytes accessed | tf_op | source)
XLA Modules:
  0.0 53.8 jit_solution(1725506089856505133)
XLA Ops:
  0.0 9.6 %order_points.1 = (bf16[32,256,128]{2,1,0:T(8,128)(2,1)}, bf16[24,64,128]{2,1,0:T(8,128)(2,1)}, bf16[28,64,128]{2,1,0:T(8,128)(2,1)}, bf16[256,128]{1,0:T(8,128)...) custom-call(s32[8192]{0:T(1024)} %refs_0_.1, bf16[64,8192]{1,0:T(8,128)(2,1)} %bitcast.10, bf16[32,64,256]{2,1,0:T(8,128)(2,1)} %bitcast.7, ...), custom_call_target="tpu_custom_call" | custom-call | tf_op jit(solution)/shard_map/order_points/pallas_call | solution.py:192
  9.6 0.0 copy-start
  9.6 0.1 collective-permute-start
  9.7 1.6 %collective-permute-start.3 = (bf16[24,64,128]{2,1,0:T(8,128)(2,1)}, bf16[24,64,128]{2,1,0:T(8,128)(2,1)S(1)}, u32[]{:S(2)}, u32[]{:S(2)}) collective-permute-start(bf16[24,64,128]{2,1,0:T(8,128)(2,1)} %get-tuple-element.13.refs_3_), channel_id=1, source_target_pairs={{8,16},{24,32},{40,48},{56,64},{72,80},{88,96},{104,112},{120,0},{... | collective-permute-start | bytes 1179656 | tf_op jit(solution)/shard_map/ppermute | solution.py:504
  11.3 4.3 %collective-permute-start.2 = (bf16[24,64,128]{2,1,0:T(8,128)(2,1)}, bf16[24,64,128]{2,1,0:T(8,128)(2,1)S(1)}, u32[]{:S(2)}, u32[]{:S(2)}) collective-permute-start(bf16[24,64,128]{2,1,0:T(8,128)(2,1)} %get-tuple-element.13.refs_3_), channel_id=1, source_target_pairs={{0,8},{16,24},{32,40},{48,56},{64,72},{80,88},{96,104},{112,120},{... | collective-permute-start | bytes 1179656 | tf_op jit(solution)/shard_map/ppermute | solution.py:504
  15.6 3.5 %collective-permute-start.1 = (bf16[24,64,128]{2,1,0:T(8,128)(2,1)}, bf16[24,64,128]{2,1,0:T(8,128)(2,1)S(1)}, u32[]{:S(2)}, u32[]{:S(2)}) collective-permute-start(bf16[24,64,128]{2,1,0:T(8,128)(2,1)} %get-tuple-element.13.refs_3_), channel_id=1, source_target_pairs={{1,2},{3,4},{5,6},{7,0},{2,1},{4,3},{6,5},{0,7},{9,10},{11,12},{13... | collective-permute-start | bytes 1179656 | tf_op jit(solution)/shard_map/ppermute | solution.py:504
  19.1 1.9 %collective-permute-start.4 = (bf16[256,128]{1,0:T(8,128)(2,1)}, bf16[256,128]{1,0:T(8,128)(2,1)S(1)}, u32[]{:S(2)}, u32[]{:S(2)}) collective-permute-start(bf16[256,128]{1,0:T(8,128)(2,1)} %get-tuple-element.15), channel_id=1, source_target_pairs={{1,2},{3,4},{5,6},{7,8},{9,10},{11,12},{13,14},{15,16},{17,18},{19... | collective-permute-start | bytes 196616 | tf_op jit(solution)/shard_map/ppermute | solution.py:531
  21.0 0.0 copy-start.2
  21.0 1.6 %copy-done.2 = bf16[256,64,64]{0,2,1:T(8,128)(2,1)S(1)} copy-done((bf16[256,64,64]{0,2,1:T(8,128)(2,1)S(1)}, bf16[256,64,64]{0,2,1:T(8,128)(2,1)}, u32[]{:S(2)}) %copy-start.2) | copy-done | bytes 2097176
  22.6 1.3 %turn_blocks.3.refs_4_.refs_11_ = bf16[16,64,1024]{2,1,0:T(8,128)(2,1)S(1)} custom-call(bf16[64,64,256]{2,1,0:T(8,128)(2,1)S(1)} %bitcast.9), custom_call_target="tpu_custom_call" | custom-call | bytes 6291456 | tf_op jit(solution)/shard_map/turn_blocks/pallas_call | solution.py:249
  23.9 0.0 copy-done
  23.9 2.6 %turn_blocks.2.refs_3_.refs_10_ = bf16[32,64,1024]{2,1,0:T(8,128)(2,1)S(1)} custom-call(bf16[64,64,512]{2,1,0:T(8,128)(2,1)S(1)} %bitcast.6), custom_call_target="tpu_custom_call" | custom-call | bytes 12582912 | tf_op jit(solution)/shard_map/turn_blocks/pallas_call | solution.py:249
  26.5 0.0 copy-start.4
  26.6 0.0 copy-start.9
  26.6 0.0 copy-start.10
  26.6 2.8 %collective-permute-done.4.refs_2_.odd = bf16[256,128]{1,0:T(8,128)(2,1)S(1)} collective-permute-done((bf16[256,128]{1,0:T(8,128)(2,1)}, bf16[256,128]{1,0:T(8,128)(2,1)S(1)}, u32[]{:S(2)}, u32[]{:S(2)}) %collective-permute-start.4) | collective-permute-done | bytes 65568 | tf_op jit(solution)/shard_map/ppermute | solution.py:531
  29.4 0.0 collective-permute-done.3.second.refs_7_
  29.4 0.0 collective-permute-done.2.first.refs_6_
  29.4 0.0 collective-permute-done.1.refs_1_.refs_5_
  29.4 0.0 collective-permute-done.refs_0_.even.refs_4_
  29.4 0.4 join.1
  29.8 0.1 collective-permute-start.6
  29.9 0.1 collective-permute-start.5
  30.7 0.0 copy-done.4
  30.7 0.0 copy-start.1
  30.7 0.0 copy-start.3
  30.7 0.0 copy-start.6
  30.8 8.1 %near_field.1.refs_14_ = f32[33,256,128]{2,1,0:T(8,128)S(1)} custom-call(s32[128]{0:T(128)S(1)} %copy-done.9, s32[128]{0:T(128)S(1)} %copy-done.10, s32[1]{0:T(128)S(6)} %copy.13.count, bf16[28,64,128]{2,1,0:T(8,128)(2,1)S(1)} %collective-permute-done.refs_0_.even.refs_4_, bf16[256,128]{1,0:T(8,128)(2,1)S(1)} %collective-permute-done.4.refs_2_.odd, ...), custom_call_target="tpu_custom_call" | custom-call | flops 2147483648 | bytes 16777216 | tf_op jit(solution)/shard_map/near_field/pallas_call | solution.py:308
  38.8 3.7 %collective-permute-done.6.refs_9_ = bf16[48,64,128]{2,1,0:T(8,128)(2,1)S(1)} collective-permute-done((bf16[48,64,128]{2,1,0:T(8,128)(2,1)S(1)}, bf16[48,64,128]{2,1,0:T(8,128)(2,1)S(1)}, u32[]{:S(2)}, u32[]{:S(2)}) %collective-permute-start.6) | collective-permute-done | bytes 786464 | tf_op jit(solution)/shard_map/ppermute | solution.py:504
  42.5 0.0 collective-permute-done.5.refs_8_
  42.5 0.0 copy-done.1
  42.6 11.2 %result.1 = f32[64,8192]{1,0:T(8,128)} custom-call(s32[8192]{0:T(1024)S(1)} %copy-done.6, s32[16,32]{1,0:T(8,128)S(1)} %copy-done.7, s32[16,16]{1,0:T(8,128)S(1)} %copy-done.8, bf16[24,64,128]{2,1,0:T(8,128)(2,1)S(1)} %copy-done.5, bf16[28,64,128]{2,1,0:T(8,128)(2,1)S(1)} %collective-permute-done.refs_0_.even.refs_4_, ...), custom_call_target="tpu_custom_call" | custom-call | tf_op jit(solution)/shard_map/result/pallas_call | solution.py:446
  (10 shorter events, 0.0 us)
Async XLA Ops:
  9.6 14.3 %copy-start = (bf16[512,64,64]{0,2,1:T(8,128)(2,1)S(1)}, bf16[512,64,64]{0,2,1:T(8,128)(2,1)}, u32[]{:S(2)}) copy-start(bf16[512,64,64]{0,2,1:T(8,128)(2,1)} %param.16) | copy-start | bytes 12582916
  9.6 19.8 %collective-permute-start = (bf16[28,64,128]{2,1,0:T(8,128)(2,1)}, bf16[28,64,128]{2,1,0:T(8,128)(2,1)S(1)}, u32[]{:S(2)}, u32[]{:S(2)}) collective-permute-start(bf16[28,64,128]{2,1,0:T(8,128)(2,1)} %get-tuple-element.14), channel_id=1, source_target_pairs={{0,1},{2,3},{4,5},{6,7},{1,0},{3,2},{5,4},{7,6},{8,9},{10,11},{12,... | collective-permute-start | bytes 1376264 | tf_op jit(solution)/shard_map/ppermute | solution.py:504
  9.7 19.7 %collective-permute-start.3 = (bf16[24,64,128]{2,1,0:T(8,128)(2,1)}, bf16[24,64,128]{2,1,0:T(8,128)(2,1)S(1)}, u32[]{:S(2)}, u32[]{:S(2)}) collective-permute-start(bf16[24,64,128]{2,1,0:T(8,128)(2,1)} %get-tuple-element.13.refs_3_), channel_id=1, source_target_pairs={{8,16},{24,32},{40,48},{56,64},{72,80},{88,96},{104,112},{120,0},{... | collective-permute-start | bytes 1179656 | tf_op jit(solution)/shard_map/ppermute | solution.py:504
  11.3 18.1 %collective-permute-start.2 = (bf16[24,64,128]{2,1,0:T(8,128)(2,1)}, bf16[24,64,128]{2,1,0:T(8,128)(2,1)S(1)}, u32[]{:S(2)}, u32[]{:S(2)}) collective-permute-start(bf16[24,64,128]{2,1,0:T(8,128)(2,1)} %get-tuple-element.13.refs_3_), channel_id=1, source_target_pairs={{0,8},{16,24},{32,40},{48,56},{64,72},{80,88},{96,104},{112,120},{... | collective-permute-start | bytes 1179656 | tf_op jit(solution)/shard_map/ppermute | solution.py:504
  15.6 13.9 %collective-permute-start.1 = (bf16[24,64,128]{2,1,0:T(8,128)(2,1)}, bf16[24,64,128]{2,1,0:T(8,128)(2,1)S(1)}, u32[]{:S(2)}, u32[]{:S(2)}) collective-permute-start(bf16[24,64,128]{2,1,0:T(8,128)(2,1)} %get-tuple-element.13.refs_3_), channel_id=1, source_target_pairs={{1,2},{3,4},{5,6},{7,0},{2,1},{4,3},{6,5},{0,7},{9,10},{11,12},{13... | collective-permute-start | bytes 1179656 | tf_op jit(solution)/shard_map/ppermute | solution.py:504
  19.1 10.3 %collective-permute-start.4 = (bf16[256,128]{1,0:T(8,128)(2,1)}, bf16[256,128]{1,0:T(8,128)(2,1)S(1)}, u32[]{:S(2)}, u32[]{:S(2)}) collective-permute-start(bf16[256,128]{1,0:T(8,128)(2,1)} %get-tuple-element.15), channel_id=1, source_target_pairs={{1,2},{3,4},{5,6},{7,8},{9,10},{11,12},{13,14},{15,16},{17,18},{19... | collective-permute-start | bytes 196616 | tf_op jit(solution)/shard_map/ppermute | solution.py:531
  21.0 1.6 %copy-start.2 = (bf16[256,64,64]{0,2,1:T(8,128)(2,1)S(1)}, bf16[256,64,64]{0,2,1:T(8,128)(2,1)}, u32[]{:S(2)}) copy-start(bf16[256,64,64]{0,2,1:T(8,128)(2,1)} %param.17) | copy-start | bytes 6291460
  26.5 4.1 %copy-start.4 = (bf16[32,256,128]{2,1,0:T(8,128)(2,1)S(1)}, bf16[32,256,128]{2,1,0:T(8,128)(2,1)}, u32[]{:S(2)}) copy-start(bf16[32,256,128]{2,1,0:T(8,128)(2,1)} %get-tuple-element.16.ordered) | copy-start | bytes 6291460
  26.6 4.1 %copy-start.9 = (s32[128]{0:T(128)S(1)}, s32[128]{0:T(128)}, u32[]{:S(2)}) copy-start(s32[128]{0:T(128)} %targets.1) | copy-start | bytes 1540
  26.6 4.1 %copy-start.10 = (s32[128]{0:T(128)S(1)}, s32[128]{0:T(128)}, u32[]{:S(2)}) copy-start(s32[128]{0:T(128)} %sources.1) | copy-start | bytes 1540
  29.8 12.7 %collective-permute-start.6 = (bf16[48,64,128]{2,1,0:T(8,128)(2,1)S(1)}, bf16[48,64,128]{2,1,0:T(8,128)(2,1)S(1)}, u32[]{:S(2)}, u32[]{:S(2)}) collective-permute-start(bf16[48,64,128]{2,1,0:T(8,128)(2,1)S(1)} %join.1), channel_id=1, source_target_pairs={{1,2},{3,4},{5,6},{7,0},{2,1},{4,3},{6,5},{0,7},{9,10},{11,12},{13... | collective-permute-start | bytes 2359304 | tf_op jit(solution)/shard_map/ppermute | solution.py:504
  29.9 12.6 %collective-permute-start.5 = (bf16[48,64,128]{2,1,0:T(8,128)(2,1)S(1)}, bf16[48,64,128]{2,1,0:T(8,128)(2,1)S(1)}, u32[]{:S(2)}, u32[]{:S(2)}) collective-permute-start(bf16[48,64,128]{2,1,0:T(8,128)(2,1)S(1)} %join.1), channel_id=1, source_target_pairs={{0,1},{2,3},{4,5},{6,7},{1,0},{3,2},{5,4},{7,6},{8,9},{10,11},{12,... | collective-permute-start | bytes 2359304 | tf_op jit(solution)/shard_map/ppermute | solution.py:504
  30.7 11.8 %copy-start.1 = (bf16[32,256,64]{1,2,0:T(8,128)(2,1)S(1)}, bf16[32,256,64]{1,2,0:T(8,128)(2,1)}, u32[]{:S(2)}) copy-start(bf16[32,256,64]{1,2,0:T(8,128)(2,1)} %param.14) | copy-start | bytes 3145732
  30.7 11.8 %copy-start.3 = (bf16[32,64,64]{2,1,0:T(8,128)(2,1)S(1)}, bf16[32,64,64]{2,1,0:T(8,128)(2,1)}, u32[]{:S(2)}) copy-start(bf16[32,64,64]{2,1,0:T(8,128)(2,1)} %refs_12_.1) | copy-start | bytes 786436
  30.7 11.8 %copy-start.5 = (bf16[24,64,128]{2,1,0:T(8,128)(2,1)S(1)}, bf16[24,64,128]{2,1,0:T(8,128)(2,1)}, u32[]{:S(2)}) copy-start(bf16[24,64,128]{2,1,0:T(8,128)(2,1)} %get-tuple-element.13.refs_3_) | copy-start | bytes 1179652
  30.7 11.8 %copy-start.6 = (s32[8192]{0:T(1024)S(1)}, s32[8192]{0:T(1024)}, u32[]{:S(2)}) copy-start(s32[8192]{0:T(1024)} %refs_0_.1) | copy-start | bytes 98308
  30.7 11.8 %copy-start.7 = (s32[16,32]{1,0:T(8,128)S(1)}, s32[16,32]{1,0:T(8,128)}, u32[]{:S(2)}) copy-start(s32[16,32]{1,0:T(8,128)} %get-tuple-element.11.refs_1_) | copy-start | bytes 6148
  30.8 11.8 %copy-start.8 = (s32[16,16]{1,0:T(8,128)S(1)}, s32[16,16]{1,0:T(8,128)}, u32[]{:S(2)}) copy-start(s32[16,16]{1,0:T(8,128)} %get-tuple-element.12.refs_2_) | copy-start | bytes 3076
